TPU v7x, 32 devices: a whole 2x2x4 slice. The times are simulated.
32 devices in a mesh: seq: 8 (over z, x), batch: 4 (over y, core).
Axes of the slice: x: 2, y: 2, z: 4, core: 2. Of those that a mesh axis runs over, the one named last changes fastest.
Arguments:
- tokens: bfloat16 [4, 1024, 768], P('batch', 'seq'), may hold values from -6 to 6
- doc_lengths: int32 [4, 4], P('batch'), may hold values from 1 to 960, 1024 in all within a row
- mixer_norm_gain: float32 [768], replicated, may hold values from 0.5 to 1.5
- mixer_in: bfloat16 [768, 2304], replicated, may hold values from -0.21875 to 0.21875
- shift_taps: float32 [64, 768], replicated, may hold values from -0.75 to 0.75
- mode_coef: float32 [64, 768], replicated, may hold values from -0.0625 to 0.0625
- mode_rate: float32 [64, 768], replicated, may hold values from 0.00024414062 to 0.1
- skip_gain: float32 [768], replicated, may hold values from 0.5 to 1.5
- mixer_out: bfloat16 [768, 768], replicated, may hold values from -0.21875 to 0.21875
- gain_second: float32 [768], replicated, may hold values from 0.5 to 1.5
- up_first: bfloat16 [768, 3072], replicated, may hold values from -0.21875 to 0.21875
- down_first: bfloat16 [3072, 768], replicated, may hold values from -0.109375 to 0.109375
- attention_norm_gain: float32 [768], replicated, may hold values from 0.5 to 1.5
- project_in: bfloat16 [768, 2304], replicated, may hold values from -0.21875 to 0.21875
- project_out: bfloat16 [768, 768], replicated, may hold values from -1.25 to 1.25
- gain_fourth: float32 [768], replicated, may hold values from 0.5 to 1.5
- up_second: bfloat16 [768, 3072], replicated, may hold values from -0.21875 to 0.21875
- down_second: bfloat16 [3072, 768], replicated, may hold values from -0.109375 to 0.109375
- cotangent: bfloat16 [4, 1024, 768], P('batch', 'seq'), may hold values from -6 to 6
Outputs:
- block_out: bfloat16 [4, 1024, 768], P('batch', 'seq')
- token_grad: float32 [4, 1024, 768], P('batch', 'seq')
- gain_first_grad: float32 [768], P('seq')
- mixer_in_grad: float32 [768, 2304], P('seq', 'batch')
- shift_taps_grad: float32 [64, 768], P('batch', 'seq')
- mode_coef_grad: float32 [64, 768], P(None, 'seq')
- mode_rate_grad: float32 [64, 768], P(None, 'seq')
- skip_gain_grad: float32 [768], P('seq')
- mixer_out_grad: float32 [768, 768], P('seq', 'batch')
- gain_second_grad: float32 [768], P('seq')
- up_first_grad: float32 [768, 3072], P('seq', 'batch')
- down_first_grad: float32 [3072, 768], P('seq', 'batch')
- gain_third_grad: float32 [768], P('seq')
- project_in_grad: float32 [768, 2304], P('seq', 'batch')
- project_out_grad: float32 [768, 768], P('seq', 'batch')
- gain_fourth_grad: float32 [768], P('seq')
- up_second_grad: float32 [768, 3072], P('seq', 'batch')
- down_second_grad: float32 [3072, 768], P('seq', 'batch')
Inputs may be any that keep to these rules, and one draw needn't show every extreme that they name: `doc_lengths`: each row holds the lengths of the 4 documents packed in order into one stream; they sum to 1024, and the longest has exactly 960 tokens.
All inputs are finite; a program needn't handle non-finite values.
Results may differ from a plain program's by a relative error of at most 0.024.
Values may be sent and summed in bfloat16 or wider, within the bound.
A program may use at most 256 MiB of HBM per device.

v0:
```python
import math

import jax
import jax.numpy as jnp
from jax import lax
from jax.sharding import PartitionSpec as P

HEADS = 12


HIGH = lax.Precision.HIGHEST
NEGATIVE = -1e30


def shifted_2(value, axis, steps):
    count = lax.axis_size(axis)
    leading, last = (max(0, -steps), min(count, count - steps))
    return lax.ppermute(value, axis, [(source, source + steps) for source in range(leading, last)])


def shortened(x):

    def short(part):
        return part.astype(jnp.bfloat16) if part.dtype == jnp.float32 else part

    return jax.tree.map(short, x)


def mult(form, left, right):
    return jnp.einsum(form, left, right, precision=HIGH, preferred_element_type=jnp.float32)


def norm_pieces(value):
    row_mean = jnp.mean(value, axis=-1, keepdims=True)
    cent = value - row_mean
    inverse_deviation = lax.rsqrt(jnp.mean(cent * cent, axis=-1, keepdims=True) + 1e-05)
    return (cent * inverse_deviation, inverse_deviation)


def norm_backward(incoming_gradient, centered_normalized, inverse_deviation, gain_vector):
    gain_share = jnp.sum(incoming_gradient * centered_normalized, axis=0)
    scaled_rows = incoming_gradient * gain_vector
    inner_product = jnp.mean(scaled_rows, axis=-1, keepdims=True)
    cross_term = jnp.mean(scaled_rows * centered_normalized, axis=-1, keepdims=True)
    return (
        inverse_deviation * (scaled_rows - inner_product - centered_normalized * cross_term),
        gain_share,
    )


def segment_of(where, ends):
    return jnp.sum((where[:, None] >= ends[None, :]).astype(jnp.int32), axis=1)


def allowed(query_pos, key_pos, ends):
    same = segment_of(query_pos, ends)[:, None] == segment_of(key_pos, ends)[None, :]
    return (key_pos[None, :] <= query_pos[:, None]) & same


def kernel_rows(coef, rate, times):

    def step(total, pair):
        scale, decay = pair
        return (total + scale[:, None] * jnp.exp(-decay[:, None] * times[None, :]), None)

    start = jnp.zeros((coef.shape[1], times.shape[0]), jnp.float32)
    return lax.scan(step, start, (coef, rate))[0]


def kernel_grads(coef, rate, times, incoming_gradient):

    def step(carry, pair):
        scale, decay = pair
        fall = incoming_gradient * jnp.exp(-decay[:, None] * times[None, :])
        return (carry, (jnp.sum(fall, axis=1), -scale * jnp.sum(fall * times[None, :], axis=1)))

    return lax.scan(step, jnp.zeros((), jnp.float32), (coef, rate))[1]


def angle_pair(left, right, period):
    turns = left[:, None] * right[None, :] % period
    angle = turns.astype(jnp.float32) * (2.0 * math.pi / period)
    return (jnp.cos(angle), jnp.sin(angle))


def dft_tables(blocks, rows):
    wide = 2 * blocks
    block_ids = jnp.arange(blocks, dtype=jnp.int32)
    wide_ids = jnp.arange(wide, dtype=jnp.int32)
    row_ids = jnp.arange(rows, dtype=jnp.int32)
    return (
        angle_pair(block_ids, wide_ids, wide),
        angle_pair(wide_ids, row_ids, wide * rows),
        angle_pair(row_ids, row_ids, rows),
    )


def forward_spectrum(signal, tables, blocks, rows):
    (cos_one, sin_one), (cos_two, sin_two), (cos_three, sin_three) = tables
    folded = signal.reshape(signal.shape[0], blocks, rows)
    first_re = mult("cpr,pf->cfr", folded, cos_one)
    first_im = -mult("cpr,pf->cfr", folded, sin_one)
    turned_re = first_re * cos_two + first_im * sin_two
    turned_im = first_im * cos_two - first_re * sin_two
    spec_re = mult("cfr,rk->cfk", turned_re, cos_three) + mult("cfr,rk->cfk", turned_im, sin_three)
    spec_im = mult("cfr,rk->cfk", turned_im, cos_three) - mult("cfr,rk->cfk", turned_re, sin_three)
    return (spec_re, spec_im)


def inverse_signal(spec_re, spec_im, tables, blocks, rows):
    (cos_one, sin_one), (cos_two, sin_two), (cos_three, sin_three) = tables
    inner_re = mult("cfk,rk->cfr", spec_re, cos_three) - mult("cfk,rk->cfr", spec_im, sin_three)
    inner_im = mult("cfk,rk->cfr", spec_im, cos_three) + mult("cfk,rk->cfr", spec_re, sin_three)
    turned_re = inner_re * cos_two - inner_im * sin_two
    turned_im = inner_im * cos_two + inner_re * sin_two
    result_value = mult("cfr,pf->cpr", turned_re, cos_one) - mult("cfr,pf->cpr", turned_im, sin_one)
    return result_value.reshape(spec_re.shape[0], blocks * rows) / (2.0 * blocks * rows)


def attend_block(state, query, query_pos, key_block, value_block, key_pos, ends, scale):
    top, mass, accum = state
    scores = (
        jnp.einsum("qhd,khd->hqk", query, key_block, preferred_element_type=jnp.float32) * scale
    )
    mask = allowed(query_pos, key_pos, ends)[None]
    newtop = jnp.maximum(top, jnp.max(jnp.where(mask, scores, NEGATIVE), axis=-1))
    weights = jnp.where(mask, jnp.exp(scores - newtop[:, :, None]), 0.0)
    factor = jnp.exp(top - newtop)
    mass = mass * factor + jnp.sum(weights, axis=-1)
    accum = accum * factor[:, :, None] + jnp.einsum(
        "hqk,khd->hqd", weights, value_block.astype(jnp.float32), preferred_element_type=jnp.float32
    )
    return (newtop, mass, accum)


def score_grads(
    query, grads, lse_rows, delta_rows, query_pos, key_block, value_block, key_pos, ends, scale
):
    scores = (
        jnp.einsum("qhd,khd->hqk", query, key_block, preferred_element_type=jnp.float32) * scale
    )
    mask = allowed(query_pos, key_pos, ends)[None]
    probs = jnp.where(mask, jnp.exp(scores - lse_rows[:, :, None]), 0.0)
    dots = jnp.einsum("qhd,khd->hqk", grads, value_block, preferred_element_type=jnp.float32)
    return (probs, (probs * (dots - delta_rows[:, :, None])).astype(jnp.bfloat16))


def query_back(
    query, grads, lse_rows, delta_rows, query_pos, key_block, value_block, key_pos, ends, scale
):
    score_grad = score_grads(
        query, grads, lse_rows, delta_rows, query_pos, key_block, value_block, key_pos, ends, scale
    )[1]
    return (
        jnp.einsum("hqk,khd->qhd", score_grad, key_block, preferred_element_type=jnp.float32)
        * scale
    )


def key_back(
    query, grads, lse_rows, delta_rows, query_pos, key_block, value_block, key_pos, ends, scale
):
    probs, score_grad = score_grads(
        query, grads, lse_rows, delta_rows, query_pos, key_block, value_block, key_pos, ends, scale
    )
    key_part = (
        jnp.einsum("hqk,qhd->khd", score_grad, query, preferred_element_type=jnp.float32) * scale
    )
    value_part = jnp.einsum(
        "hqk,qhd->khd", probs, grads.astype(jnp.float32), preferred_element_type=jnp.float32
    )
    return (key_part, value_part)


def scan_keys(carry, keys, values, update):
    count = keys.shape[0]
    width = keys.shape[1]
    head_size = width // HEADS
    step = math.gcd(count, 1024)
    firsts = step * jnp.arange(count // step, dtype=jnp.int32)

    def inner_product(state, item):
        key_block, value_block, first = item
        key_pos = first + jnp.arange(step, dtype=jnp.int32)
        return (update(state, key_block, value_block, key_pos), None)

    items = (
        keys.reshape(count // step, step, HEADS, head_size),
        values.reshape(count // step, step, HEADS, head_size),
        firsts,
    )
    return lax.scan(inner_product, carry, items)[0]


def feed_forward(residual_stream, gain_vector, w_up, w_down):
    centered_normalized, inverse_deviation = norm_pieces(residual_stream)
    normed_rows = (centered_normalized * gain_vector).astype(jnp.bfloat16)
    raised_rows = jnp.dot(normed_rows, w_up, preferred_element_type=jnp.float32)
    active_tokens = jax.nn.gelu(raised_rows).astype(jnp.bfloat16)
    result_value = residual_stream + jnp.dot(
        active_tokens, w_down, preferred_element_type=jnp.float32
    )
    return (
        result_value,
        (centered_normalized, inverse_deviation, normed_rows, raised_rows, active_tokens),
    )


def feed_back(incoming_gradient, saved_residuals, gain_vector, w_up, w_down):
    centered_normalized, inverse_deviation, normed_rows, raised_rows, active_tokens = (
        saved_residuals
    )
    grad_low = incoming_gradient.astype(jnp.bfloat16)
    down_part = jnp.einsum("tf,td->fd", active_tokens, grad_low, preferred_element_type=jnp.float32)
    active_grad = jnp.einsum("td,fd->tf", grad_low, w_down, preferred_element_type=jnp.float32)
    slope = jax.vjp(jax.nn.gelu, raised_rows)[1](active_grad)[0].astype(jnp.bfloat16)
    up_part = jnp.einsum("td,tf->df", normed_rows, slope, preferred_element_type=jnp.float32)
    normed_gradient = jnp.einsum("tf,df->td", slope, w_up, preferred_element_type=jnp.float32)
    input_gradient, gain_share = norm_backward(
        normed_gradient, centered_normalized, inverse_deviation, gain_vector
    )
    return (incoming_gradient + input_gradient, gain_share, up_part, down_part)


def shards(
    tokens,
    doc_lengths,
    mixer_norm_gain,
    mixer_in,
    shift_taps,
    mode_coef,
    mode_rate,
    skip_gain,
    mixer_out,
    gain_second,
    up_first,
    down_first,
    attention_norm_gain,
    project_in,
    project_out,
    gain_fourth,
    up_second,
    down_second,
    cotangent,
):
    rows = tokens.shape[1]
    width = tokens.shape[2]
    blocks = lax.axis_size("seq")
    rank = lax.axis_index("seq")
    total = rows * blocks
    head_size = width // HEADS
    scale = head_size ** (-0.5)
    lags = shift_taps.shape[0]
    channels = width // blocks
    ends = jnp.cumsum(doc_lengths[0])
    here = rank * rows + jnp.arange(rows, dtype=jnp.int32)
    residual_stream = tokens[0].astype(jnp.float32)
    mixer_centered_normalized, mixer_inverse_deviation = norm_pieces(residual_stream)
    mixer_normed_rows = (mixer_centered_normalized * mixer_norm_gain).astype(jnp.bfloat16)
    mixed_a = jnp.dot(mixer_normed_rows, mixer_in, preferred_element_type=jnp.float32)
    query_a = mixed_a[:, :width]
    key_a = mixed_a[:, width : 2 * width]
    value_a = mixed_a[:, 2 * width :]
    rim = shifted_2(key_a[rows - (lags - 1) :].astype(jnp.bfloat16), "seq", 1).astype(jnp.float32)
    key_ext = jnp.concatenate([rim, key_a], axis=0)
    shifted = jnp.zeros_like(key_a)
    for lag in range(lags):
        shifted = shifted + shift_taps[lag] * key_ext[lags - 1 - lag : lags - 1 - lag + rows]
    product_kv = shifted * value_a
    channel_in = lax.all_to_all(
        product_kv.T.reshape(blocks, channels, rows).astype(jnp.bfloat16),
        "seq",
        split_axis=0,
        concat_axis=2,
        tiled=True,
    ).astype(jnp.float32)[0]
    times = jnp.arange(total, dtype=jnp.int32).astype(jnp.float32)
    coef_here = lax.dynamic_slice_in_dim(mode_coef, rank * channels, channels, 1)
    rate_here = lax.dynamic_slice_in_dim(mode_rate, rank * channels, channels, 1)
    kernel_here = kernel_rows(coef_here, rate_here, times)
    tables = dft_tables(blocks, rows)
    sig_re, sig_im = forward_spectrum(channel_in, tables, blocks, rows)
    ker_re, ker_im = forward_spectrum(kernel_here, tables, blocks, rows)
    conv_chan = inverse_signal(
        sig_re * ker_re - sig_im * ker_im, sig_re * ker_im + sig_im * ker_re, tables, blocks, rows
    )
    conv_home = lax.all_to_all(
        conv_chan.reshape(1, channels, total).astype(jnp.bfloat16),
        "seq",
        split_axis=2,
        concat_axis=0,
        tiled=True,
    ).astype(jnp.float32)
    response = conv_home.reshape(width, rows).T + skip_gain * product_kv
    gated = (query_a * response).astype(jnp.bfloat16)
    stream_b = residual_stream + jnp.dot(gated, mixer_out, preferred_element_type=jnp.float32)
    attention_residual_stream, saved_b = feed_forward(stream_b, gain_second, up_first, down_first)
    attention_centered_normalized, attention_inverse_deviation = norm_pieces(
        attention_residual_stream
    )
    attention_normed_rows = (attention_centered_normalized * attention_norm_gain).astype(
        jnp.bfloat16
    )
    mixed_c = jnp.dot(attention_normed_rows, project_in, preferred_element_type=jnp.float32).astype(
        jnp.bfloat16
    )
    query_flat = mixed_c[:, :width]
    key_flat = mixed_c[:, width : 2 * width]
    value_flat = mixed_c[:, 2 * width :]
    query_c = query_flat.reshape(rows, HEADS, head_size)
    key_heads = key_flat.reshape(rows, HEADS, head_size)
    value_heads = value_flat.reshape(rows, HEADS, head_size)

    def forward_update(state, key_block, value_block, key_pos):
        return attend_block(state, query_c, here, key_block, value_block, key_pos, ends, scale)

    begin = (
        jnp.full((HEADS, rows), NEGATIVE, jnp.float32),
        jnp.zeros((HEADS, rows), jnp.float32),
        jnp.zeros((HEADS, rows, head_size), jnp.float32),
    )
    piece = (
        lax.all_gather(key_flat, "seq", axis=0, tiled=True),
        lax.all_gather(value_flat, "seq", axis=0, tiled=True),
    )
    top, mass, accum = scan_keys(begin, piece[0], piece[1], forward_update)
    lse = top + jnp.log(mass)
    att_full = accum / mass[:, :, None]
    attended = att_full.transpose(1, 0, 2).reshape(rows, width).astype(jnp.bfloat16)
    stream_d = attention_residual_stream + jnp.dot(
        attended, project_out, preferred_element_type=jnp.float32
    )
    result_value, saved_d = feed_forward(stream_d, gain_fourth, up_second, down_second)
    block_out = result_value.astype(jnp.bfloat16)[None]
    incoming_gradient = cotangent[0].astype(jnp.float32)
    incoming_gradient, gain_four_part, up_two_part, down_two_part = feed_back(
        incoming_gradient, saved_d, gain_fourth, up_second, down_second
    )
    grad_low = incoming_gradient.astype(jnp.bfloat16)
    out_part_c = jnp.einsum("td,te->de", attended, grad_low, preferred_element_type=jnp.float32)
    att_grad = jnp.einsum(
        "te,de->td", grad_low, project_out, preferred_element_type=jnp.float32
    ).astype(jnp.bfloat16)
    grad_heads = att_grad.reshape(rows, HEADS, head_size)
    delta = jnp.sum(grad_heads.astype(jnp.float32).transpose(1, 0, 2) * att_full, axis=-1)
    zero_heads = jnp.zeros((rows, HEADS, head_size), jnp.float32)

    def query_update(summed, key_block, value_block, key_pos):
        return summed + query_back(
            query_c, grad_heads, lse, delta, here, key_block, value_block, key_pos, ends, scale
        )

    piece = (
        lax.all_gather(key_flat, "seq", axis=0, tiled=True),
        lax.all_gather(value_flat, "seq", axis=0, tiled=True),
    )
    query_grad = scan_keys(zero_heads, piece[0], piece[1], query_update)
    lse_all, delta_all = (
        lax.all_gather(lse, "seq", axis=1, tiled=True),
        lax.all_gather(delta, "seq", axis=1, tiled=True),
    )
    queries = lax.all_gather(query_flat, "seq", axis=0, tiled=True)
    grads = lax.all_gather(att_grad, "seq", axis=0, tiled=True)
    count = queries.shape[0]
    step = math.gcd(count, 1024)
    firsts = step * jnp.arange(count // step, dtype=jnp.int32)

    def inner_product(summed, item):
        query_block, grad_block, first = item
        query_pos = first + jnp.arange(step, dtype=jnp.int32)
        lse_rows = lax.dynamic_slice_in_dim(lse_all, first, step, 1)
        delta_rows = lax.dynamic_slice_in_dim(delta_all, first, step, 1)
        parts = key_back(
            query_block,
            grad_block,
            lse_rows,
            delta_rows,
            query_pos,
            key_heads,
            value_heads,
            here,
            ends,
            scale,
        )
        return ((summed[0] + parts[0], summed[1] + parts[1]), None)

    items = (
        queries.reshape(count // step, step, HEADS, head_size),
        grads.reshape(count // step, step, HEADS, head_size),
        firsts,
    )
    key_grad, value_grad = lax.scan(inner_product, (zero_heads, zero_heads), items)[0]
    key_grad = key_grad.reshape(rows, width)
    value_grad = value_grad.reshape(rows, width)
    mixed_grad_c = jnp.concatenate(
        [query_grad.reshape(rows, width), key_grad, value_grad], axis=1
    ).astype(jnp.bfloat16)
    in_part_c = jnp.einsum(
        "td,te->de", attention_normed_rows, mixed_grad_c, preferred_element_type=jnp.float32
    )
    attention_normed_gradient = jnp.einsum(
        "te,de->td", mixed_grad_c, project_in, preferred_element_type=jnp.float32
    )
    attention_norm_gradient, attention_gain_share = norm_backward(
        attention_normed_gradient,
        attention_centered_normalized,
        attention_inverse_deviation,
        attention_norm_gain,
    )
    incoming_gradient = incoming_gradient + attention_norm_gradient
    incoming_gradient, gain_two_part, up_one_part, down_one_part = feed_back(
        incoming_gradient, saved_b, gain_second, up_first, down_first
    )
    grad_low = incoming_gradient.astype(jnp.bfloat16)
    out_part_a = jnp.einsum("td,te->de", gated, grad_low, preferred_element_type=jnp.float32)
    gated_grad = jnp.einsum("te,de->td", grad_low, mixer_out, preferred_element_type=jnp.float32)
    query_grad_a = gated_grad * response
    response_grad = gated_grad * query_a
    skip_part = jnp.sum(response_grad * product_kv, axis=0)
    chan_grad = lax.all_to_all(
        response_grad.T.reshape(blocks, channels, rows).astype(jnp.bfloat16),
        "seq",
        split_axis=0,
        concat_axis=2,
        tiled=True,
    ).astype(jnp.float32)[0]
    grad_re, grad_im = forward_spectrum(chan_grad, tables, blocks, rows)
    signal_grad = inverse_signal(
        ker_re * grad_re + ker_im * grad_im,
        ker_re * grad_im - ker_im * grad_re,
        tables,
        blocks,
        rows,
    )
    kernel_grad = inverse_signal(
        sig_re * grad_re + sig_im * grad_im,
        sig_re * grad_im - sig_im * grad_re,
        tables,
        blocks,
        rows,
    )
    coef_part, rate_part = kernel_grads(coef_here, rate_here, times, kernel_grad)
    returned = lax.all_to_all(
        signal_grad.reshape(1, channels, total).astype(jnp.bfloat16),
        "seq",
        split_axis=2,
        concat_axis=0,
        tiled=True,
    ).astype(jnp.float32)
    kv_grad = returned.reshape(width, rows).T + skip_gain * response_grad
    shifted_grad = kv_grad * value_a
    value_grad_a = kv_grad * shifted
    later = shifted_2(shortened(shifted_grad[: lags - 1]), "seq", -1)
    grad_ext = jnp.concatenate([shifted_grad, later], axis=0)
    key_grad_a = jnp.zeros_like(key_a)
    tap_rows = []
    for lag in range(lags):
        key_grad_a = key_grad_a + shift_taps[lag] * grad_ext[lag : lag + rows]
        tap_rows.append(
            jnp.sum(shifted_grad * key_ext[lags - 1 - lag : lags - 1 - lag + rows], axis=0)
        )
    taps_part = jnp.stack(tap_rows)
    mixed_grad_a = jnp.concatenate([query_grad_a, key_grad_a, value_grad_a], axis=1).astype(
        jnp.bfloat16
    )
    in_part_a = jnp.einsum(
        "td,te->de", mixer_normed_rows, mixed_grad_a, preferred_element_type=jnp.float32
    )
    mixer_normed_gradient = jnp.einsum(
        "te,de->td", mixed_grad_a, mixer_in, preferred_element_type=jnp.float32
    )
    mixer_norm_gradient, mixer_gain_share = norm_backward(
        mixer_normed_gradient, mixer_centered_normalized, mixer_inverse_deviation, mixer_norm_gain
    )
    token_grad = (incoming_gradient + mixer_norm_gradient)[None]
    parts = (
        lax.psum_scatter(mixer_gain_share, "seq", scatter_dimension=0, tiled=True),
        lax.psum_scatter(in_part_a, "seq", scatter_dimension=0, tiled=True),
        lax.psum_scatter(taps_part, "seq", scatter_dimension=1, tiled=True),
        lax.psum_scatter(skip_part, "seq", scatter_dimension=0, tiled=True),
        lax.psum_scatter(out_part_a, "seq", scatter_dimension=0, tiled=True),
        lax.psum_scatter(gain_two_part, "seq", scatter_dimension=0, tiled=True),
        lax.psum_scatter(up_one_part, "seq", scatter_dimension=0, tiled=True),
        lax.psum_scatter(down_one_part, "seq", scatter_dimension=0, tiled=True),
        lax.psum_scatter(attention_gain_share, "seq", scatter_dimension=0, tiled=True),
        lax.psum_scatter(in_part_c, "seq", scatter_dimension=0, tiled=True),
        lax.psum_scatter(out_part_c, "seq", scatter_dimension=0, tiled=True),
        lax.psum_scatter(gain_four_part, "seq", scatter_dimension=0, tiled=True),
        lax.psum_scatter(up_two_part, "seq", scatter_dimension=0, tiled=True),
        lax.psum_scatter(down_two_part, "seq", scatter_dimension=0, tiled=True),
    )
    matrices = (
        lax.psum_scatter(
            parts[1].astype(jnp.bfloat16), "batch", scatter_dimension=1, tiled=True
        ).astype(jnp.float32),
        lax.psum_scatter(
            parts[2].astype(jnp.bfloat16), "batch", scatter_dimension=0, tiled=True
        ).astype(jnp.float32),
        lax.psum_scatter(
            parts[4].astype(jnp.bfloat16), "batch", scatter_dimension=1, tiled=True
        ).astype(jnp.float32),
        lax.psum_scatter(
            parts[6].astype(jnp.bfloat16), "batch", scatter_dimension=1, tiled=True
        ).astype(jnp.float32),
        lax.psum_scatter(
            parts[7].astype(jnp.bfloat16), "batch", scatter_dimension=1, tiled=True
        ).astype(jnp.float32),
        lax.psum_scatter(
            parts[9].astype(jnp.bfloat16), "batch", scatter_dimension=1, tiled=True
        ).astype(jnp.float32),
        lax.psum_scatter(
            parts[10].astype(jnp.bfloat16), "batch", scatter_dimension=1, tiled=True
        ).astype(jnp.float32),
        lax.psum_scatter(
            parts[12].astype(jnp.bfloat16), "batch", scatter_dimension=1, tiled=True
        ).astype(jnp.float32),
        lax.psum_scatter(
            parts[13].astype(jnp.bfloat16), "batch", scatter_dimension=1, tiled=True
        ).astype(jnp.float32),
    )
    smalls = lax.psum(
        (parts[0], coef_part, rate_part, parts[3], parts[5], parts[8], parts[11]), "batch"
    )
    return (
        block_out,
        token_grad,
        smalls[0],
        matrices[0],
        matrices[1],
        smalls[1],
        smalls[2],
        smalls[3],
        matrices[2],
        smalls[4],
        matrices[3],
        matrices[4],
        smalls[5],
        matrices[5],
        matrices[6],
        smalls[6],
        matrices[7],
        matrices[8],
    )


def solution(mesh):
    in_specs = (
        P("batch", "seq", None),
        P("batch", None),
        P(),
        P(),
        P(),
        P(),
        P(),
        P(),
        P(),
        P(),
        P(),
        P(),
        P(),
        P(),
        P(),
        P(),
        P(),
        P(),
        P("batch", "seq", None),
    )
    out_specs = (
        P("batch", "seq", None),
        P("batch", "seq", None),
        P("seq"),
        P("seq", "batch"),
        P("batch", "seq"),
        P(None, "seq"),
        P(None, "seq"),
        P("seq"),
        P("seq", "batch"),
        P("seq"),
        P("seq", "batch"),
        P("seq", "batch"),
        P("seq"),
        P("seq", "batch"),
        P("seq", "batch"),
        P("seq"),
        P("seq", "batch"),
        P("seq", "batch"),
    )
    return jax.shard_map(shards, mesh=mesh, in_specs=in_specs, out_specs=out_specs, check_vma=False)
```

profile of v0, /device:TPU:0, one launch (start us, length us, event | category | flops | bytes accessed | tf_op | source)
XLA Modules:
  0.0 1926.0 jit_solution(5463685312886791195)
XLA Ops:
  9.6 2.8 fusion.669
  13.2 5.5 collective-permute-start
  23.2 164.5 %while.8 = (s32[]{:T(128)}, f32[96,1024]{1,0:T(8,128)}, f32[64,96]{1,0:T(8,128)}, f32[64,96]{1,0:T(8,128)}, s32[]{:T(128)}, /*index=5*/s32[]{:T(128)}) while((s32[]{:T(128)}, f32[96,1024]{1,0:T(8,128)}, f32[64,96]{1,0:T(8,128)}, f32[64,96]{1,0:T(8,128)}, s32[]{:T(128)}, /*index=5*/s32[]{:T(128)}) %tuple.215), condition=%wide.region_3.4_spmd.clone, body=%wide.region_2.3_spmd.clone.sunk | while | flops 394339 | bytes 797019 | solution.py:67
  196.4 6.1 convert_bitcast_fusion.4
  204.3 4.3 all-to-all-start
  208.9 2.5 fusion.62
  213.3 3.2 all-to-all-done
  223.0 2.1 multiply_subtract_fusion.3
  235.6 3.8 reduce.129
  239.4 2.1 reshape.537
  241.4 11.8 all_to_all.48
  265.0 3.2 fusion.672
  268.2 4.1 fusion.677
  280.6 35.9 %all-gather.5.cloned.1.call-done = bf16[1024,768]{1,0:T(8,128)(2,1)} async-done(((bf16[128,768]{1,0:T(8,128)(2,1)}), bf16[1024,768]{1,0:T(8,128)(2,1)}) %all-gather.5.cloned.1.call-update) | async-done | bytes 1572880 | tf_op jit(solution)/shard_map/all_gather | solution.py:323
  316.5 2.6 copy.143
  319.1 2.7 select_reduce_fusion
  325.8 36.5 %all-gather.7.cloned.1.call-done = bf16[1024,768]{1,0:T(8,128)(2,1)} async-done(((bf16[128,768]{1,0:T(8,128)(2,1)}), bf16[1024,768]{1,0:T(8,128)(2,1)}) %all-gather.7.cloned.1.call-update) | async-done | bytes 1572880 | tf_op jit(solution)/shard_map/all_gather | solution.py:324
  362.3 2.6 copy.144
  364.9 5.7 fusion.361
  372.3 4.8 fusion.37
  377.1 2.3 multiply_reduce_fusion.1
  388.5 19.4 %all-gather.9.cloned.1.call-done = bf16[1024,768]{1,0:T(8,128)(2,1)} async-done(((bf16[128,768]{1,0:T(8,128)(2,1)}), bf16[1024,768]{1,0:T(8,128)(2,1)}) %all-gather.9.cloned.1.call-update) | async-done | bytes 1572880 | tf_op jit(solution)/shard_map/all_gather | solution.py:362
  407.9 2.6 copy.146
  410.5 32.7 %all_gather.23 = f32[12,1024]{1,0:T(8,128)} all-gather(f32[12,128]{1,0:T(8,128)} %get-tuple-element.533), channel_id=1, replica_groups=mesh['seq'=8,'batch'=4] {'seq'}, dimensions={1}, use_global_device_ids=true | all-gather | bytes 55296 | tf_op jit(solution)/shard_map/all_gather | solution.py:359
  444.9 32.6 %all_gather.25 = f32[12,1024]{1,0:T(8,128)} all-gather(f32[12,128]{1,0:T(8,128)S(1)} %fusion.359), channel_id=1, replica_groups=mesh['seq'=8,'batch'=4] {'seq'}, dimensions={1}, use_global_device_ids=true | all-gather | bytes 55296 | tf_op jit(solution)/shard_map/all_gather | solution.py:360
  477.5 5.2 fusion.679
  482.6 7.4 fusion.43
  490.0 2.8 copy.148
  492.8 5.1 fusion.48
  497.9 8.8 fusion.44
  506.8 3.4 multiply_reduce_fusion.2
  511.6 4.4 fusion.30
  516.9 2.3 multiply_reduce_fusion.3
  523.1 10.9 all_to_all.49
  539.2 2.6 multiply_add_fusion
  549.3 2.3 reduce.130
  552.1 10.2 all_to_all.50
  576.8 4.1 fusion.376
  582.9 5.2 collective-permute-done.1
  588.5 5.9 fusion.112
  594.5 4.8 fusion.374
  600.6 5.3 fusion.381
  607.2 5.1 fusion.673
  613.3 6.6 fusion.398
  621.1 5.1 fusion.671
  626.3 4.2 reduce-scatter.57.cloned.1.call-done
  632.0 69.8 %reduce-scatter.47.cloned.1.call-done = f32[96,768]{1,0:T(8,128)} async-done(((f32[768,768]{1,0:T(8,128)}), f32[96,768]{1,0:T(8,128)}) %reduce-scatter.47.cloned.1.call-update) | async-done | bytes 294928 | tf_op jit(solution)/shard_map/reduce_scatter | solution.py:487
  703.7 69.7 %reduce-scatter.37.cloned.1.call-done = f32[96,768]{1,0:T(8,128)} async-done(((f32[768,768]{1,0:T(8,128)}), f32[96,768]{1,0:T(8,128)}) %reduce-scatter.37.cloned.1.call-update) | async-done | bytes 294928 | tf_op jit(solution)/shard_map/reduce_scatter | solution.py:481
  775.2 129.9 %reduce-scatter.45.cloned.1.call-done = f32[96,2304]{1,0:T(8,128)} async-done(((f32[768,2304]{1,0:T(8,128)}), f32[96,2304]{1,0:T(8,128)}) %reduce-scatter.45.cloned.1.call-update) | async-done | bytes 884752 | tf_op jit(solution)/shard_map/reduce_scatter | solution.py:486
  907.5 129.9 %reduce-scatter.33.cloned.1.call-done = f32[96,2304]{1,0:T(8,128)} async-done(((f32[768,2304]{1,0:T(8,128)}), f32[96,2304]{1,0:T(8,128)}) %reduce-scatter.33.cloned.1.call-update) | async-done | bytes 884752 | tf_op jit(solution)/shard_map/reduce_scatter | solution.py:478
  1039.8 163.6 %reduce-scatter.53.cloned.1.call-done = f32[384,768]{1,0:T(8,128)} async-done(((f32[3072,768]{1,0:T(8,128)}), f32[384,768]{1,0:T(8,128)}) %reduce-scatter.53.cloned.1.call-update) | async-done | bytes 1179664 | tf_op jit(solution)/shard_map/reduce_scatter | solution.py:490
  1205.8 163.7 %reduce-scatter.49.cloned.1.call-done = f32[96,3072]{1,0:T(8,128)} async-done(((f32[768,3072]{1,0:T(8,128)}), f32[96,3072]{1,0:T(8,128)}) %reduce-scatter.49.cloned.1.call-update) | async-done | bytes 1179664 | tf_op jit(solution)/shard_map/reduce_scatter | solution.py:489
  1369.6 2.2 convert_element_type.429
  1373.3 4.1 fusion.51
  1379.4 156.2 %reduce-scatter.43.cloned.1.call-done = f32[384,768]{1,0:T(8,128)} async-done(((f32[3072,768]{1,0:T(8,128)}), f32[384,768]{1,0:T(8,128)}) %reduce-scatter.43.cloned.1.call-update) | async-done | bytes 1179664 | tf_op jit(solution)/shard_map/reduce_scatter | solution.py:484
  1539.1 2.2 convolution_add_fusion
  1543.6 158.2 %reduce-scatter.39.cloned.1.call-done = f32[96,3072]{1,0:T(8,128)} async-done(((f32[768,3072]{1,0:T(8,128)}), f32[96,3072]{1,0:T(8,128)}) %reduce-scatter.39.cloned.1.call-update) | async-done | bytes 1179664 | tf_op jit(solution)/shard_map/reduce_scatter | solution.py:483
  1701.8 2.2 convert_element_type.421
  1704.0 110.9 %while.7 = (s32[]{:T(128)}, f32[64,96]{1,0:T(8,128)S(1)}, f32[64,96]{1,0:T(8,128)S(1)}, f32[64,96]{1,0:T(8,128)}, f32[96,1024]{1,0:T(8,128)S(1)}, /*index=5*/f32[64,96]{1,0:T(8,128)}, s32[]{:T(128)}, s32[]{:T(128)}) while((s32[]{:T(128)}, f32[64,96]{1,0:T(8,128)S(1)}, f32[64,96]{1,0:T(8,128)S(1)}, ...), condition=%wide.region_98.99_spmd.clone.clone, body=%wide.region_95.98_spmd.clone.clone.sunk | while | flops 492642 | bytes 406125 | solution.py:77
  1815.0 3.5 fusion.106
  1818.5 35.1 %all-reduce.5 = (f32[768]{0:T(1024)S(1)}, f32[768]{0:T(1024)S(1)}, f32[768]{0:T(1024)S(1)}, f32[768]{0:T(1024)S(1)}, f32[768]{0:T(1024)S(1)}) all-reduce(f32[768]{0:T(1024)S(1)} %get-tuple-element.407, f32[768]{0:T(1024)S(1)} %copy-done.174, f32[768]{0:T(1024)S(1)} %copy-done.176, ...), channel_id=2, replica_groups=mesh['seq'=8,'batch'=4] {'seq'}, use_global_device_ids=true, to_apply=%region_25.26.clone | all-reduce | flops 3840 | bytes 30720
  1854.0 12.4 all-reduce.6
  1882.1 10.2 reduce-scatter.61.cloned.1.call-done
  1895.8 21.3 %reduce-scatter.41.cloned.1.call-done = bf16[96,768]{1,0:T(8,128)(2,1)} async-done(((bf16[96,3072]{1,0:T(8,128)(2,1)}), bf16[96,768]{1,0:T(8,128)(2,1)}) %reduce-scatter.41.cloned.1.call-update) | async-done | bytes 147472 | tf_op jit(solution)/shard_map/reduce_scatter | solution.py:502
  (1260 shorter events, 428.6 us)
Async XLA Ops:
  7.2 265.4 %copy-start = (bf16[768,2304]{1,0:T(8,128)(2,1)S(1)}, bf16[768,2304]{1,0:T(8,128)(2,1)}, u32[]{:S(2)}) copy-start(bf16[768,2304]{1,0:T(8,128)(2,1)} %param.36) | copy-start | bytes 10616836
  9.6 9.8 copy-start.74
  13.2 181.9 %collective-permute-start = (bf16[63,768]{1,0:T(8,128)(2,1)}, bf16[63,768]{1,0:T(8,128)(2,1)}, u32[]{:S(2)}, u32[]{:S(2)}) collective-permute-start(bf16[63,768]{1,0:T(8,128)(2,1)} %slice.2990), channel_id=1, source_target_pairs={{0,4},{4,8},{8,12},{12,16},{16,20},{20,24},{24,28},{1,5},{5,9},{9,... | collective-permute-start | bytes 290312 | tf_op jit(solution)/shard_map/ppermute | solution.py:18
  195.0 7.5 copy-start.157
  195.0 7.5 copy-start.158
  195.0 7.5 copy-start.159
  195.0 7.5 copy-start.160
  195.0 7.5 copy-start.161
  195.0 7.5 copy-start.162
  195.1 7.5 copy-start.163
  204.3 12.2 all-to-all-start
  208.6 107.9 %all-gather.5.cloned.1.call-start = ((), (), s32[]{:S(2)}) async-start(), calls=%async_computation.22 | async-start | bytes 1769472 | tf_op jit(solution)/shard_map/all_gather | solution.py:323
  274.1 88.2 %all-gather.7.cloned.1.call-start = ((), (), s32[]{:S(2)}) async-start(), calls=%async_computation.23 | async-start | bytes 1769472 | tf_op jit(solution)/shard_map/all_gather | solution.py:324
  274.9 133.0 %all-gather.9.cloned.1.call-start = ((), (), s32[]{:S(2)}) async-start(), calls=%async_computation.24 | async-start | bytes 1769472 | tf_op jit(solution)/shard_map/all_gather | solution.py:362
  280.4 209.6 %all-gather.11.cloned.1.call-start = ((), (), s32[]{:S(2)}) async-start(), calls=%async_computation.25 | async-start | bytes 1769472 | tf_op jit(solution)/shard_map/all_gather | solution.py:363
  371.1 8.4 copy-start.11
  371.1 8.3 copy-start.172
  371.3 8.1 copy-start.182
  381.7 248.8 %reduce-scatter.57.cloned.1.call-start = ((), (), s32[]{:S(2)}) async-start(), calls=%async_computation.38 | async-start | bytes 442368
  506.8 10.1 slice-start.2
  511.6 7.7 copy-start.48
  520.6 52.3 %copy-start.34 = (f32[128,768]{1,0:T(8,128)}, f32[128,768]{1,0:T(8,128)S(1)}, u32[]{:S(2)}) copy-start(f32[128,768]{1,0:T(8,128)S(1)} %multiply_add_fusion.6) | copy-start | bytes 1179652
  570.9 130.9 %reduce-scatter.47.cloned.1.call-start = ((), (), s32[]{:S(2)}) async-start(), calls=%async_computation.33 | async-start | bytes 2654208 | tf_op jit(solution)/shard_map/reduce_scatter | solution.py:487
  572.8 200.6 %reduce-scatter.37.cloned.1.call-start = ((), (), s32[]{:S(2)}) async-start(), calls=%async_computation.28 | async-start | bytes 2654208 | tf_op jit(solution)/shard_map/reduce_scatter | solution.py:481
  575.7 329.5 %reduce-scatter.45.cloned.1.call-start = ((), (), s32[]{:S(2)}) async-start(), calls=%async_computation.32 | async-start | bytes 7962624 | tf_op jit(solution)/shard_map/reduce_scatter | solution.py:486
  580.9 7.2 copy-start.87
  580.9 7.2 copy-start.89
  580.9 7.2 copy-start.91
  581.0 7.2 copy-start.93
  581.0 7.2 copy-start.95
  581.0 7.2 copy-start.97
  581.0 7.2 copy-start.99
  581.0 7.2 copy-start.101
  581.3 13.2 copy-start.25
  581.3 13.2 copy-start.63
  581.3 13.2 copy-start.78
  581.3 456.1 %reduce-scatter.33.cloned.1.call-start = ((), (), s32[]{:S(2)}) async-start(), calls=%async_computation.26 | async-start | bytes 7962624 | tf_op jit(solution)/shard_map/reduce_scatter | solution.py:478
  581.4 6.8 collective-permute-start.1
  582.9 16.3 copy-start.67
  599.3 604.1 %reduce-scatter.53.cloned.1.call-start = ((), (), s32[]{:S(2)}) async-start(), calls=%async_computation.36 | async-start | bytes 10616832 | tf_op jit(solution)/shard_map/reduce_scatter | solution.py:490
  606.0 763.6 %reduce-scatter.49.cloned.1.call-start = ((), (), s32[]{:S(2)}) async-start(), calls=%async_computation.34 | async-start | bytes 10616832 | tf_op jit(solution)/shard_map/reduce_scatter | solution.py:489
  612.3 923.2 %reduce-scatter.43.cloned.1.call-start = ((), (), s32[]{:S(2)}) async-start(), calls=%async_computation.31 | async-start | bytes 10616832 | tf_op jit(solution)/shard_map/reduce_scatter | solution.py:484
  620.0 1081.8 %reduce-scatter.39.cloned.1.call-start = ((), (), s32[]{:S(2)}) async-start(), calls=%async_computation.29 | async-start | bytes 10616832 | tf_op jit(solution)/shard_map/reduce_scatter | solution.py:483
  626.2 1241.1 %reduce-scatter.35.cloned.1.call-start = ((), (), s32[]{:S(2)}) async-start(), calls=%async_computation.27 | async-start | bytes 20480 | tf_op jit(solution)/shard_map/reduce_scatter | solution.py:496
  631.9 1236.7 %reduce-scatter.65.cloned.1.call-start = ((), (), s32[]{:S(2)}) async-start(), calls=%async_computation.42 | async-start | bytes 245760
  703.6 1166.6 %reduce-scatter.59.cloned.1.call-start = ((), (), s32[]{:S(2)}) async-start(), calls=%async_computation.39 | async-start | bytes 245760
  775.2 1096.6 %reduce-scatter.63.cloned.1.call-start = ((), (), s32[]{:S(2)}) async-start(), calls=%async_computation.41 | async-start | bytes 737280
  907.5 966.1 %reduce-scatter.55.cloned.1.call-start = ((), (), s32[]{:S(2)}) async-start(), calls=%async_computation.37 | async-start | bytes 737280
  1039.7 837.3 %reduce-scatter.67.cloned.1.call-start = ((), (), s32[]{:S(2)}) async-start(), calls=%async_computation.43 | async-start | bytes 737280
  1205.7 166.3 %copy-start.195 = (u32[32]{0:T(128)S(1)}, u32[32]{0:T(128)}, u32[]{:S(2)}) copy-start(u32[32]{0:T(128)} %constant.186) | copy-start | bytes 388
  1205.8 674.7 %reduce-scatter.51.cloned.1.call-start = ((), (), s32[]{:S(2)}) async-start(), calls=%async_computation.35 | async-start | bytes 737280 | tf_op jit(solution)/shard_map/reduce_scatter | solution.py:514
  1371.8 520.5 %reduce-scatter.61.cloned.1.call-start = ((), (), s32[]{:S(2)}) async-start(), calls=%async_computation.40 | async-start | bytes 737280
  1379.4 158.7 %copy-start.27 = (f32[96,16,128]{2,1,0:T(8,128)S(1)}, f32[96,16,128]{2,1,0:T(8,128)}, u32[]{:S(2)}) copy-start(f32[96,16,128]{2,1,0:T(8,128)} %get-tuple-element.517) | copy-start | bytes 2359300
  1538.0 379.1 %reduce-scatter.41.cloned.1.call-start = ((), (), s32[]{:S(2)}) async-start(), calls=%async_computation.30 | async-start | bytes 737280 | tf_op jit(solution)/shard_map/reduce_scatter | solution.py:502
  1543.5 160.5 %copy-start.167 = (f32[64,96]{1,0:T(8,128)S(1)}, f32[64,96]{1,0:T(8,128)}, u32[]{:S(2)}) copy-start(f32[64,96]{1,0:T(8,128)} %custom-call.1) | copy-start | bytes 73732
  1543.5 160.5 %copy-start.168 = (f32[64,96]{1,0:T(8,128)S(1)}, f32[64,96]{1,0:T(8,128)}, u32[]{:S(2)}) copy-start(f32[64,96]{1,0:T(8,128)} %custom-call.2) | copy-start | bytes 73732
  1703.9 111.0 %copy-start.64 = (bf16[128,768]{1,0:T(8,128)(2,1)S(1)}, bf16[128,768]{1,0:T(8,128)(2,1)}, u32[]{:S(2)}) copy-start(bf16[128,768]{1,0:T(8,128)(2,1)} %get-tuple-element.525) | copy-start | bytes 589828
  1703.9 111.0 %copy-start.66 = (bf16[128,768]{1,0:T(8,128)(2,1)S(1)}, bf16[128,768]{1,0:T(8,128)(2,1)}, u32[]{:S(2)}) copy-start(bf16[128,768]{1,0:T(8,128)(2,1)} %copy-done.65) | copy-start | bytes 589828
  1703.9 111.0 %copy-start.68 = (bf16[128,768]{1,0:T(8,128)(2,1)S(1)}, bf16[128,768]{1,0:T(8,128)(2,1)}, u32[]{:S(2)}) copy-start(bf16[128,768]{1,0:T(8,128)(2,1)} %copy-done.67) | copy-start | bytes 589828
  1703.9 111.0 %copy-start.79 = (f32[768]{0:T(1024)S(1)}, f32[768]{0:T(1024)}, u32[]{:S(2)}) copy-start(f32[768]{0:T(1024)} %param.25) | copy-start | bytes 9220
  1703.9 111.0 %copy-start.178 = (f32[128]{0:T(128)S(1)}, f32[128]{0:T(128)}, u32[]{:S(2)}) copy-start(f32[128]{0:T(128)} %copy-done.177) | copy-start | bytes 1540
  1704.0 111.0 %copy-start.188 = (f32[128]{0:T(128)S(1)}, f32[128]{0:T(128)}, u32[]{:S(2)}) copy-start(f32[128]{0:T(128)} %copy-done.187) | copy-start | bytes 1540
  1815.0 51.5 %copy-start.35 = (f32[128,768]{1,0:T(8,128)S(1)}, f32[128,768]{1,0:T(8,128)}, u32[]{:S(2)}) copy-start(f32[128,768]{1,0:T(8,128)} %copy-done.34) | copy-start | bytes 1179652
  1873.5 45.2 %copy-start.1 = (bf16[768,2304]{1,0:T(8,128)(2,1)S(1)}, bf16[768,2304]{1,0:T(8,128)(2,1)}, u32[]{:S(2)}) copy-start(bf16[768,2304]{1,0:T(8,128)(2,1)} %param.36) | copy-start | bytes 10616836
  (161 other events, 582.0 us)
Sparse Core Ops, SparseCore 0:
  274.3 42.2 all-gather.4
  319.3 42.9 all-gather.6
  365.1 42.7 all-gather.8
  410.5 43.6 all-gather.10
  571.0 59.4 reduce-scatter.56
  633.8 67.9 reduce-scatter.46
  705.3 68.0 reduce-scatter.36
  777.0 128.0 reduce-scatter.44
  909.3 128.0 reduce-scatter.32
  1040.8 162.4 reduce-scatter.52
  1207.0 162.5 reduce-scatter.48
  1373.0 162.5 reduce-scatter.42
  1539.2 162.5 reduce-scatter.38
  1704.6 18.5 reduce-scatter.34
  1726.2 19.7 reduce-scatter.64
  1749.0 19.7 reduce-scatter.58
  1771.3 22.1 reduce-scatter.62
  1796.0 22.0 reduce-scatter.54
  1820.8 22.0 reduce-scatter.66
  1845.4 22.4 reduce-scatter.50
  1870.6 21.6 reduce-scatter.60
  1894.9 22.0 reduce-scatter.40
where the time goes:
time: 1940 us; the launch traced here: 1930 us
  waiting for transfers between devices  1180 us (61%)
  other arithmetic  330 us (17%)
  matrix products  155 us (8%)
  blocking collectives  146 us (8%)
  local copies, waits for them, and re-layouts  85.3 us (4%)
    reduce_scatter x1, waiting for transfers between devices, shards(): lax.psum_scatter(up_two_part, 'seq', scatter_dimension=0, tiled=True)  164 us
    reduce_scatter x1, waiting for transfers between devices, shards(): lax.psum_scatter(down_two_part, 'seq', scatter_dimension=0, tiled=True)  164 us
    reduce_scatter x1, waiting for transfers between devices, shards(): lax.psum_scatter(up_one_part, 'seq', scatter_dimension=0, tiled=True)  158 us
    reduce_scatter x1, waiting for transfers between devices, shards(): lax.psum_scatter(down_one_part, 'seq', scatter_dimension=0, tiled=True)  156 us
    reduce_scatter x1, waiting for transfers between devices, shards(): lax.psum_scatter(in_part_c, 'seq', scatter_dimension=0, tiled=True)  130 us
    reduce_scatter x1, waiting for transfers between devices, shards(): lax.psum_scatter(in_part_a, 'seq', scatter_dimension=0, tiled=True)  130 us
    add x64, other arithmetic, step(): total + scale[:, None] * jnp.exp(-decay[:, None] * times[None, :])  119 us
    reduce_scatter x1, waiting for transfers between devices, shards(): lax.psum_scatter(out_part_c, 'seq', scatter_dimension=0, tiled=True)  69.8 us
  transfers between devices with their start and end apart: 25, of which 16 were waited for; matrix products, arithmetic and copies ran while one was open for 23% of the time, Pallas kernels for 0%

commit v1 on v0

--- a/solution.py
+++ b/solution.py
@@ -1,8 +1,11 @@
+import functools
 import math
 
 import jax
 import jax.numpy as jnp
 from jax import lax
+from jax.experimental import pallas as pl
+from jax.experimental.pallas import tpu as pltpu
 from jax.sharding import PartitionSpec as P
 
 HEADS = 12
@@ -543,6 +546,601 @@
     )
 
 
+MESH = pl.DeviceIdType.MESH
+BF = jnp.bfloat16
+F32 = jnp.float32
+LAYER, PAIR = (0, 1)
+GIVEN = (4, 3)
+OWN = (5, 3)
+
+
+def flip(value):
+    return 1 - value
+
+
+def weight_sum_kernel(kinds, *refs):
+    refs = list(refs)
+    given = [[refs.pop(0) for _ in range(GIVEN[kind])] for kind in kinds]
+    outs = [refs.pop(0) for _ in kinds]
+    own_of = [[refs.pop(0) for _ in range(OWN[kind])] for kind in kinds]
+    sums_of = [[refs.pop(0) for _ in range(7)] for kind in kinds]
+    send_sem, recv_sem = refs
+    s = lax.axis_index("seq")
+    b = lax.axis_index("batch")
+    z, x = s // 2, lax.rem(s, 2)
+    y, c = b // 2, lax.rem(b, 2)
+    zh, zl = z // 2, lax.rem(z, 2)
+    sibling = (s, 2 * y + flip(c))
+    by_x = (2 * z + flip(x), b)
+    by_y = (s, 2 * flip(y) + c)
+    by_l = (2 * (2 * zh + flip(zl)) + x, b)
+    by_h = (2 * (2 * flip(zh) + zl) + x, b)
+    barrier = pltpu.get_barrier_semaphore()
+    for other in (sibling, by_x, by_y, by_l, by_h):
+        pl.semaphore_signal(barrier, inc=1, device_id=other, device_id_type=MESH)
+    pl.semaphore_wait(barrier, 5)
+    started = []
+
+    def send(source, target, other):
+        at = len(started)
+        copy = pltpu.make_async_remote_copy(
+            src_ref=source,
+            dst_ref=target,
+            send_sem=send_sem.at[at],
+            recv_sem=recv_sem.at[at],
+            device_id=other,
+            device_id_type=MESH,
+        )
+        copy.start()
+        started.append(copy)
+        return copy
+
+    shared = []
+    for kind, inputs, own in zip(kinds, given, own_of):
+        mine = []
+        own[0][:, 0:128] = inputs[0][...].T
+        mine.append(send(own[0].at[:, 0:128], own[0].at[:, 128:256], sibling))
+        own[1][0:128, :] = inputs[1][c]
+        mine.append(send(inputs[1].at[flip(c)], own[1].at[128:256, :], sibling))
+        if kind == LAYER:
+            own[2][:, 0:128] = inputs[2][c].T
+            own[3][...] = inputs[2][flip(c)].T
+            mine.append(send(own[3], own[2].at[:, 128:256], sibling))
+            own[4][0:128, :] = inputs[3][...]
+            mine.append(send(inputs[3], own[4].at[128:256, :], sibling))
+        else:
+            own[2][:, 0:128] = inputs[2][...].T
+            mine.append(send(own[2].at[:, 0:128], own[2].at[:, 128:256], sibling))
+        shared.append(mine)
+
+    stages = []
+    for kind, own, sums, mine in zip(kinds, own_of, sums_of, shared):
+        for copy in mine:
+            copy.wait_recv()
+        grads, near_a, near_b, next_a, next_b, third, fourth = sums
+        half = grads.shape[4] // 2
+
+        def place(product, at, tile):
+            for block in range(8):
+                grads[block % 2, at, block // 4, (block // 2) % 2, pl.ds(pl.multiple_of(96 * tile, 16), 96), :] = product[
+                    96 * block : 96 * block + 96
+                ].astype(BF)
+
+        if kind == LAYER:
+
+            @pl.loop(0, 6)
+            def _(step):
+                at, chunk = step // 3, lax.rem(step, 3)
+                lanes = pl.ds(pl.multiple_of(256 * step, 256), 256)
+                product = jnp.dot(own[0][...], own[1][:, lanes], preferred_element_type=F32)
+                place(product[:, 0:128], at, 2 * chunk)
+                place(product[:, 128:256], at, 2 * chunk + 1)
+
+            @pl.loop(0, 8)
+            def _(block):
+                lanes = pl.ds(pl.multiple_of(384 * block, 384), 384)
+                product = jnp.dot(own[2][...], own[4][:, lanes], preferred_element_type=F32)
+                for at in range(2):
+                    for tile in range(3):
+                        grads[
+                            lax.rem(block, 2), at, block // 4, lax.rem(block // 2, 2), 576 + 192 * tile : 768 + 192 * tile, :
+                        ] = product[192 * at : 192 * at + 192, 128 * tile : 128 * tile + 128].astype(BF)
+
+        else:
+
+            @pl.loop(0, 2)
+            def _(at):
+                for chunk in range(3):
+                    lanes = pl.ds(pl.multiple_of(768 * at + 256 * chunk, 256), 256)
+                    right = own[1][:, lanes]
+                    if chunk < 2:
+                        product = jnp.dot(own[0][...], right, preferred_element_type=F32)
+                    else:
+                        first = lax.broadcasted_iota(jnp.int32, right.shape, 1) < 64
+                        zero = jnp.zeros_like(right)
+                        product = jnp.dot(own[0][...], jnp.where(first, right, zero), preferred_element_type=F32)
+                        product += jnp.dot(own[2][...], jnp.where(first, zero, right), preferred_element_type=F32)
+                    place(product[:, 0:128], at, 2 * chunk)
+                    place(product[:, 128:256], at, 2 * chunk + 1)
+
+        stages.append(
+            [
+                send(grads.at[flip(x), :, :, :, 0:half, :], near_a, by_x),
+                send(grads.at[:, flip(y), :, :, half:, :], near_b, by_y),
+            ]
+        )
+
+    for index, sums in enumerate(sums_of):
+        grads, near_a, near_b, next_a, next_b, third, fourth = sums
+        half = grads.shape[4] // 2
+        for copy in stages[index]:
+            copy.wait_recv()
+
+        @pl.loop(0, 8)
+        def _(step):
+            high, mid, low = step // 4, lax.rem(step // 2, 2), lax.rem(step, 2)
+            grads[x, high, mid, low, 0:half, :] += near_a[high, mid, low]
+            grads[high, y, mid, low, half:, :] += near_b[high, mid, low]
+
+        stages[index] = [
+            send(grads.at[x, flip(y), :, :, 0:half, :], next_a, by_y),
+            send(grads.at[flip(x), y, :, :, half:, :], next_b, by_x),
+        ]
+    for index, sums in enumerate(sums_of):
+        grads, near_a, near_b, next_a, next_b, third, fourth = sums
+        half = grads.shape[4] // 2
+        for copy in stages[index]:
+            copy.wait_recv()
+
+        @pl.loop(0, 4)
+        def _(step):
+            mid, low = step // 2, lax.rem(step, 2)
+            grads[x, y, mid, low, 0:half, :] += next_a[mid, low]
+            grads[x, y, mid, low, half:, :] += next_b[mid, low]
+
+        stages[index] = [send(grads.at[x, y, :, flip(zl), :, :], third, by_l)]
+    for index, sums in enumerate(sums_of):
+        grads, near_a, near_b, next_a, next_b, third, fourth = sums
+        for copy in stages[index]:
+            copy.wait_recv()
+
+        @pl.loop(0, 2)
+        def _(mid):
+            grads[x, y, mid, zl] += third[mid]
+
+        stages[index] = [send(grads.at[x, y, flip(zh), zl], fourth, by_h)]
+    for index, sums in enumerate(sums_of):
+        grads, near_a, near_b, next_a, next_b, third, fourth = sums
+        for copy in stages[index]:
+            copy.wait_recv()
+        outs[index][...] = grads[x, y, zh, zl].astype(F32) + fourth[...].astype(F32)
+    for copy in started:
+        copy.wait_send()
+
+
+def weight_sums(kinds, groups, identity):
+    lengths = [1152 if kind == LAYER else 576 for kind in kinds]
+    own, sums = [], []
+    for kind, length in zip(kinds, lengths):
+        own += [pltpu.VMEM((768, 256), BF), pltpu.VMEM((256, 1536), BF)]
+        if kind == LAYER:
+            own += [pltpu.VMEM((384, 256), BF), pltpu.VMEM((384, 128), BF), pltpu.VMEM((256, 3072), BF)]
+        else:
+            own += [pltpu.VMEM((768, 256), BF)]
+        half = length // 2
+        sums += [
+            pltpu.VMEM((2, 2, 2, 2, length, 128), BF),
+            pltpu.VMEM((2, 2, 2, half, 128), BF),
+            pltpu.VMEM((2, 2, 2, half, 128), BF),
+            pltpu.VMEM((2, 2, half, 128), BF),
+            pltpu.VMEM((2, 2, half, 128), BF),
+            pltpu.VMEM((2, length, 128), BF),
+            pltpu.VMEM((length, 128), BF),
+        ]
+    copies = sum(GIVEN[kind] + 6 for kind in kinds)
+    flat = [array for group in groups for array in group]
+    vmem = pl.BlockSpec(memory_space=pltpu.VMEM)
+    return pl.pallas_call(
+        functools.partial(weight_sum_kernel, kinds),
+        out_shape=[jax.ShapeDtypeStruct((length, 128), F32) for length in lengths],
+        in_specs=[vmem] * len(flat),
+        out_specs=[vmem] * len(kinds),
+        scratch_shapes=own + sums + [pltpu.SemaphoreType.DMA((copies,)), pltpu.SemaphoreType.DMA((copies,))],
+        compiler_params=pltpu.CompilerParams(
+            collective_id=identity, has_side_effects=True, vmem_limit_bytes=60 * 2**20
+        ),
+    )(*flat)
+
+
+def by_core(array, count):
+    width = array.shape[1] // 4
+    return array.reshape(128, 2, 2, width).transpose(2, 0, 1, 3).reshape(2, 128, 2 * width)
+
+
+def pair_columns(wide, narrow):
+    parts = jnp.concatenate([wide.reshape(128, 4, 576), narrow.reshape(128, 4, 192)], axis=2)
+    return parts.reshape(128, 2, 2, 768).transpose(2, 0, 1, 3).reshape(2, 128, 1536)
+
+
+def untile_layer(block):
+    up = block[:576].reshape(6, 96, 128).transpose(1, 0, 2).reshape(96, 768)
+    down = block[576:].reshape(3, 192, 128).transpose(0, 2, 1).reshape(384, 192)
+    return up, down
+
+
+def untile_pair(block):
+    both = block.reshape(6, 96, 128).transpose(1, 0, 2).reshape(96, 768)
+    return both[:, :576], both[:, 576:]
+
+
+def mode_kernel(coef_ref, rate_ref, out_ref):
+    blocks = out_ref.shape[0] // 8
+    width = out_ref.shape[1]
+    row = lax.broadcasted_iota(jnp.int32, (8, width), 0).astype(F32)
+    out_ref[...] = jnp.zeros_like(out_ref)
+
+    @pl.loop(0, 8)
+    def _(group):
+        rate = rate_ref[pl.ds(pl.multiple_of(8 * group, 8), 8), :]
+        coef = coef_ref[pl.ds(pl.multiple_of(8 * group, 8), 8), :]
+        falls = [coef[n : n + 1] * jnp.exp(-rate[n : n + 1] * row) for n in range(8)]
+        steps = [jnp.exp(-rate[n : n + 1] * jnp.maximum(row, 8.0)) for n in range(8)]
+
+        def step(at, falls):
+            rows = pl.ds(pl.multiple_of(8 * at, 8), 8)
+            out_ref[rows, :] += sum(falls[1:], falls[0])
+            return tuple(fall * factor for fall, factor in zip(falls, steps))
+
+        lax.fori_loop(0, blocks, step, tuple(falls), unroll=4)
+
+
+def mode_rows(coef, rate, total):
+    vmem = pl.BlockSpec(memory_space=pltpu.VMEM)
+    return pl.pallas_call(
+        mode_kernel,
+        out_shape=jax.ShapeDtypeStruct((total, coef.shape[1]), F32),
+        in_specs=[vmem] * 2,
+        out_specs=vmem,
+    )(coef, rate)
+
+
+def mode_grad_kernel(coef_ref, rate_ref, grad_ref, coef_out, rate_out):
+    blocks = grad_ref.shape[0] // 8
+    width = grad_ref.shape[1]
+    row = lax.broadcasted_iota(jnp.int32, (8, width), 0).astype(F32)
+
+    @pl.loop(0, 8)
+    def _(group):
+        at_group = pl.ds(pl.multiple_of(8 * group, 8), 8)
+        rate = rate_ref[at_group, :]
+        coef = coef_ref[at_group, :]
+        steps = [jnp.exp(-rate[n : n + 1] * jnp.maximum(row, 8.0)) for n in range(8)]
+        zero = jnp.minimum(row, 0.0)
+
+        def step(at, carry):
+            totals, slopes = carry
+            rows = pl.ds(pl.multiple_of(8 * (blocks - 1 - at), 8), 8)
+            here = grad_ref[rows, :]
+            slopes = tuple(slope * factor + total for slope, factor, total in zip(slopes, steps, totals))
+            totals = tuple(total * factor + here for total, factor in zip(totals, steps))
+            return totals, slopes
+
+        totals, slopes = lax.fori_loop(0, blocks, step, ((zero,) * 8, (zero,) * 8), unroll=2)
+        coef_rows, rate_rows = [], []
+        for n in range(8):
+            fall = jnp.exp(-rate[n : n + 1] * row)
+            coef_rows.append(jnp.sum(fall * totals[n], axis=0, keepdims=True))
+            rate_rows.append(
+                -coef[n : n + 1] * jnp.sum(fall * (8.0 * steps[n] * slopes[n] + row * totals[n]), axis=0, keepdims=True)
+            )
+        coef_out[at_group, :] = jnp.concatenate(coef_rows, axis=0)
+        rate_out[at_group, :] = jnp.concatenate(rate_rows, axis=0)
+
+
+def mode_grads(coef, rate, grad):
+    vmem = pl.BlockSpec(memory_space=pltpu.VMEM)
+    shape = jax.ShapeDtypeStruct(coef.shape, F32)
+    return pl.pallas_call(
+        mode_grad_kernel, out_shape=[shape, shape], in_specs=[vmem] * 3, out_specs=[vmem] * 2
+    )(coef, rate, grad)
+
+
+def feed_back_only(incoming_gradient, saved_residuals, gain_vector, w_up, w_down):
+    centered_normalized, inverse_deviation, normed_rows, raised_rows, active_tokens = (
+        saved_residuals
+    )
+    grad_low = incoming_gradient.astype(jnp.bfloat16)
+    active_grad = jnp.einsum("td,fd->tf", grad_low, w_down, preferred_element_type=jnp.float32)
+    slope = jax.vjp(jax.nn.gelu, raised_rows)[1](active_grad)[0].astype(jnp.bfloat16)
+    normed_gradient = jnp.einsum("tf,df->td", slope, w_up, preferred_element_type=jnp.float32)
+    input_gradient, gain_share = norm_backward(
+        normed_gradient, centered_normalized, inverse_deviation, gain_vector
+    )
+    return (incoming_gradient + input_gradient, gain_share, slope)
+
+
+def shards_fast(
+    tokens,
+    doc_lengths,
+    mixer_norm_gain,
+    mixer_in,
+    shift_taps,
+    mode_coef,
+    mode_rate,
+    skip_gain,
+    mixer_out,
+    gain_second,
+    up_first,
+    down_first,
+    attention_norm_gain,
+    project_in,
+    project_out,
+    gain_fourth,
+    up_second,
+    down_second,
+    cotangent,
+):
+    rows = tokens.shape[1]
+    width = tokens.shape[2]
+    blocks = lax.axis_size("seq")
+    rank = lax.axis_index("seq")
+    total = rows * blocks
+    head_size = width // HEADS
+    scale = head_size ** (-0.5)
+    lags = shift_taps.shape[0]
+    channels = width // blocks
+    ends = jnp.cumsum(doc_lengths[0])
+    here = rank * rows + jnp.arange(rows, dtype=jnp.int32)
+    residual_stream = tokens[0].astype(jnp.float32)
+    mixer_centered_normalized, mixer_inverse_deviation = norm_pieces(residual_stream)
+    mixer_normed_rows = (mixer_centered_normalized * mixer_norm_gain).astype(jnp.bfloat16)
+    mixed_a = jnp.dot(mixer_normed_rows, mixer_in, preferred_element_type=jnp.float32)
+    query_a = mixed_a[:, :width]
+    key_a = mixed_a[:, width : 2 * width]
+    value_a = mixed_a[:, 2 * width :]
+    rim = shifted_2(key_a[rows - (lags - 1) :].astype(jnp.bfloat16), "seq", 1).astype(jnp.float32)
+    key_ext = jnp.concatenate([rim, key_a], axis=0)
+    shifted = jnp.zeros_like(key_a)
+    for lag in range(lags):
+        shifted = shifted + shift_taps[lag] * key_ext[lags - 1 - lag : lags - 1 - lag + rows]
+    product_kv = shifted * value_a
+    channel_in = lax.all_to_all(
+        product_kv.T.reshape(blocks, channels, rows).astype(jnp.bfloat16),
+        "seq",
+        split_axis=0,
+        concat_axis=2,
+        tiled=True,
+    ).astype(jnp.float32)[0]
+    times = jnp.arange(total, dtype=jnp.int32).astype(jnp.float32)
+    coef_here = lax.dynamic_slice_in_dim(mode_coef, rank * channels, channels, 1)
+    rate_here = lax.dynamic_slice_in_dim(mode_rate, rank * channels, channels, 1)
+    kernel_here = mode_rows(coef_here, rate_here, total).T
+    tables = dft_tables(blocks, rows)
+    sig_re, sig_im = forward_spectrum(channel_in, tables, blocks, rows)
+    ker_re, ker_im = forward_spectrum(kernel_here, tables, blocks, rows)
+    conv_chan = inverse_signal(
+        sig_re * ker_re - sig_im * ker_im, sig_re * ker_im + sig_im * ker_re, tables, blocks, rows
+    )
+    conv_home = lax.all_to_all(
+        conv_chan.reshape(1, channels, total).astype(jnp.bfloat16),
+        "seq",
+        split_axis=2,
+        concat_axis=0,
+        tiled=True,
+    ).astype(jnp.float32)
+    response = conv_home.reshape(width, rows).T + skip_gain * product_kv
+    gated = (query_a * response).astype(jnp.bfloat16)
+    stream_b = residual_stream + jnp.dot(gated, mixer_out, preferred_element_type=jnp.float32)
+    attention_residual_stream, saved_b = feed_forward(stream_b, gain_second, up_first, down_first)
+    attention_centered_normalized, attention_inverse_deviation = norm_pieces(
+        attention_residual_stream
+    )
+    attention_normed_rows = (attention_centered_normalized * attention_norm_gain).astype(
+        jnp.bfloat16
+    )
+    mixed_c = jnp.dot(attention_normed_rows, project_in, preferred_element_type=jnp.float32).astype(
+        jnp.bfloat16
+    )
+    query_flat = mixed_c[:, :width]
+    key_flat = mixed_c[:, width : 2 * width]
+    value_flat = mixed_c[:, 2 * width :]
+    query_c = query_flat.reshape(rows, HEADS, head_size)
+    key_heads = key_flat.reshape(rows, HEADS, head_size)
+    value_heads = value_flat.reshape(rows, HEADS, head_size)
+
+    def forward_update(state, key_block, value_block, key_pos):
+        return attend_block(state, query_c, here, key_block, value_block, key_pos, ends, scale)
+
+    begin = (
+        jnp.full((HEADS, rows), NEGATIVE, jnp.float32),
+        jnp.zeros((HEADS, rows), jnp.float32),
+        jnp.zeros((HEADS, rows, head_size), jnp.float32),
+    )
+    piece = (
+        lax.all_gather(key_flat, "seq", axis=0, tiled=True),
+        lax.all_gather(value_flat, "seq", axis=0, tiled=True),
+    )
+    top, mass, accum = scan_keys(begin, piece[0], piece[1], forward_update)
+    lse = top + jnp.log(mass)
+    att_full = accum / mass[:, :, None]
+    attended = att_full.transpose(1, 0, 2).reshape(rows, width).astype(jnp.bfloat16)
+    stream_d = attention_residual_stream + jnp.dot(
+        attended, project_out, preferred_element_type=jnp.float32
+    )
+    result_value, saved_d = feed_forward(stream_d, gain_fourth, up_second, down_second)
+    block_out = result_value.astype(jnp.bfloat16)[None]
+    incoming_gradient = cotangent[0].astype(jnp.float32)
+    incoming_gradient, gain_four_part, slope_d = feed_back_only(
+        incoming_gradient, saved_d, gain_fourth, up_second, down_second
+    )
+    grad_low_c = incoming_gradient.astype(jnp.bfloat16)
+    att_grad = jnp.einsum(
+        "te,de->td", grad_low_c, project_out, preferred_element_type=jnp.float32
+    ).astype(jnp.bfloat16)
+    grad_heads = att_grad.reshape(rows, HEADS, head_size)
+    delta = jnp.sum(grad_heads.astype(jnp.float32).transpose(1, 0, 2) * att_full, axis=-1)
+    zero_heads = jnp.zeros((rows, HEADS, head_size), jnp.float32)
+
+    def query_update(summed, key_block, value_block, key_pos):
+        return summed + query_back(
+            query_c, grad_heads, lse, delta, here, key_block, value_block, key_pos, ends, scale
+        )
+
+    piece = (
+        lax.all_gather(key_flat, "seq", axis=0, tiled=True),
+        lax.all_gather(value_flat, "seq", axis=0, tiled=True),
+    )
+    query_grad = scan_keys(zero_heads, piece[0], piece[1], query_update)
+    lse_all, delta_all = (
+        lax.all_gather(lse, "seq", axis=1, tiled=True),
+        lax.all_gather(delta, "seq", axis=1, tiled=True),
+    )
+    queries = lax.all_gather(query_flat, "seq", axis=0, tiled=True)
+    grads = lax.all_gather(att_grad, "seq", axis=0, tiled=True)
+    count = queries.shape[0]
+    step = math.gcd(count, 1024)
+    firsts = step * jnp.arange(count // step, dtype=jnp.int32)
+
+    def inner_product(summed, item):
+        query_block, grad_block, first = item
+        query_pos = first + jnp.arange(step, dtype=jnp.int32)
+        lse_rows = lax.dynamic_slice_in_dim(lse_all, first, step, 1)
+        delta_rows = lax.dynamic_slice_in_dim(delta_all, first, step, 1)
+        parts = key_back(
+            query_block,
+            grad_block,
+            lse_rows,
+            delta_rows,
+            query_pos,
+            key_heads,
+            value_heads,
+            here,
+            ends,
+            scale,
+        )
+        return ((summed[0] + parts[0], summed[1] + parts[1]), None)
+
+    items = (
+        queries.reshape(count // step, step, HEADS, head_size),
+        grads.reshape(count // step, step, HEADS, head_size),
+        firsts,
+    )
+    key_grad, value_grad = lax.scan(inner_product, (zero_heads, zero_heads), items)[0]
+    key_grad = key_grad.reshape(rows, width)
+    value_grad = value_grad.reshape(rows, width)
+    mixed_grad_c = jnp.concatenate(
+        [query_grad.reshape(rows, width), key_grad, value_grad], axis=1
+    ).astype(jnp.bfloat16)
+    attention_normed_gradient = jnp.einsum(
+        "te,de->td", mixed_grad_c, project_in, preferred_element_type=jnp.float32
+    )
+    attention_norm_gradient, attention_gain_share = norm_backward(
+        attention_normed_gradient,
+        attention_centered_normalized,
+        attention_inverse_deviation,
+        attention_norm_gain,
+    )
+    incoming_gradient = incoming_gradient + attention_norm_gradient
+    grad_in_b = incoming_gradient.astype(jnp.bfloat16)
+    incoming_gradient, gain_two_part, slope_b = feed_back_only(
+        incoming_gradient, saved_b, gain_second, up_first, down_first
+    )
+    grad_low = incoming_gradient.astype(jnp.bfloat16)
+    gated_grad = jnp.einsum("te,de->td", grad_low, mixer_out, preferred_element_type=jnp.float32)
+    query_grad_a = gated_grad * response
+    response_grad = gated_grad * query_a
+    skip_part = jnp.sum(response_grad * product_kv, axis=0)
+    chan_grad = lax.all_to_all(
+        response_grad.T.reshape(blocks, channels, rows).astype(jnp.bfloat16),
+        "seq",
+        split_axis=0,
+        concat_axis=2,
+        tiled=True,
+    ).astype(jnp.float32)[0]
+    grad_re, grad_im = forward_spectrum(chan_grad, tables, blocks, rows)
+    signal_grad = inverse_signal(
+        ker_re * grad_re + ker_im * grad_im,
+        ker_re * grad_im - ker_im * grad_re,
+        tables,
+        blocks,
+        rows,
+    )
+    kernel_grad = inverse_signal(
+        sig_re * grad_re + sig_im * grad_im,
+        sig_re * grad_im - sig_im * grad_re,
+        tables,
+        blocks,
+        rows,
+    )
+    coef_part, rate_part = mode_grads(coef_here, rate_here, kernel_grad.T)
+    returned = lax.all_to_all(
+        signal_grad.reshape(1, channels, total).astype(jnp.bfloat16),
+        "seq",
+        split_axis=2,
+        concat_axis=0,
+        tiled=True,
+    ).astype(jnp.float32)
+    kv_grad = returned.reshape(width, rows).T + skip_gain * response_grad
+    shifted_grad = kv_grad * value_a
+    value_grad_a = kv_grad * shifted
+    later = shifted_2(shortened(shifted_grad[: lags - 1]), "seq", -1)
+    grad_ext = jnp.concatenate([shifted_grad, later], axis=0)
+    key_grad_a = jnp.zeros_like(key_a)
+    tap_rows = []
+    for lag in range(lags):
+        key_grad_a = key_grad_a + shift_taps[lag] * grad_ext[lag : lag + rows]
+        tap_rows.append(
+            jnp.sum(shifted_grad * key_ext[lags - 1 - lag : lags - 1 - lag + rows], axis=0)
+        )
+    taps_part = jnp.stack(tap_rows)
+    mixed_grad_a = jnp.concatenate([query_grad_a, key_grad_a, value_grad_a], axis=1).astype(
+        jnp.bfloat16
+    )
+    mixer_normed_gradient = jnp.einsum(
+        "te,de->td", mixed_grad_a, mixer_in, preferred_element_type=jnp.float32
+    )
+    mixer_norm_gradient, mixer_gain_share = norm_backward(
+        mixer_normed_gradient, mixer_centered_normalized, mixer_inverse_deviation, mixer_norm_gain
+    )
+    token_grad = (incoming_gradient + mixer_norm_gradient)[None]
+    groups = (
+        (saved_d[2], by_core(slope_d, 4), by_core(cotangent[0], 4), saved_d[4]),
+        (attention_normed_rows, pair_columns(mixed_grad_c, grad_low_c), attended),
+        (saved_b[2], by_core(slope_b, 4), by_core(grad_in_b, 4), saved_b[4]),
+        (mixer_normed_rows, pair_columns(mixed_grad_a, grad_low), gated),
+    )
+    layer_d, pair_c, layer_b, pair_a = weight_sums((LAYER, PAIR, LAYER, PAIR), groups, 0)
+    up_two, down_two = untile_layer(layer_d)
+    in_c, out_c = untile_pair(pair_c)
+    up_one, down_one = untile_layer(layer_b)
+    in_a, out_a = untile_pair(pair_a)
+    taps = lax.psum_scatter(taps_part, "seq", scatter_dimension=1, tiled=True)
+    taps = lax.psum_scatter(taps.astype(jnp.bfloat16), "batch", scatter_dimension=0, tiled=True).astype(jnp.float32)
+    shares = jnp.stack([mixer_gain_share, skip_part, gain_two_part, attention_gain_share, gain_four_part])
+    shares = lax.psum_scatter(shares, "seq", scatter_dimension=1, tiled=True)
+    shares, coef_part, rate_part = lax.psum((shares, coef_part, rate_part), "batch")
+    return (
+        block_out,
+        token_grad,
+        shares[0],
+        in_a,
+        taps,
+        coef_part,
+        rate_part,
+        shares[1],
+        out_a,
+        shares[2],
+        up_one,
+        down_one,
+        shares[3],
+        in_c,
+        out_c,
+        shares[4],
+        up_two,
+        down_two,
+    )
+
+
 def solution(mesh):
     in_specs = (
         P("batch", "seq", None),
@@ -585,4 +1183,5 @@
         P("seq", "batch"),
         P("seq", "batch"),
     )
-    return jax.shard_map(shards, mesh=mesh, in_specs=in_specs, out_specs=out_specs, check_vma=False)
+    fast = mesh.shape["seq"] == 8 and mesh.shape["batch"] == 4
+    return jax.shard_map(shards_fast if fast else shards, mesh=mesh, in_specs=in_specs, out_specs=out_specs, check_vma=False)

time: 1940 us -> 834 us (0.43)
  waiting for transfers between devices: 1180 us -> 96.2 us
  other arithmetic: 330 us -> 62.6 us
  Pallas kernels: 0 us -> 187 us
  local copies, waits for them, and re-layouts: 85.3 us -> 222 us
  blocking collectives: 146 us -> 89.3 us
  matrix products: 155 us -> 125 us
    reduce_scatter x11 -> x1, waiting for transfers between devices: 1060 us -> 16.8 us  [shards_fast(): lax.psum_scatter(taps.astype(jnp.bfloat16), 'batch', scatter_dimension=0,...]
    pallas_call x0 -> x3, Pallas kernels: none -> 187 us  [the longest x1 173 us: weight_sums(): pl.pallas_call(functools.partial(weight_sum_kernel, kinds), out_shape=[ja...]
    add x68 -> x2, other arithmetic: 119 us -> 5.74 us  [the longest x1 5.74 us: shards_fast(): key_grad_a = key_grad_a + shift_taps[lag] * grad_ext[lag:lag + rows]]
    another operation x65 -> x71, local copies, waits for them, and re-layouts: 0.67 us -> 93.9 us  [the longest x65 86.8 us: shards_fast(): taps_part = jnp.stack(tap_rows)]
    neg x128 -> x0, other arithmetic: 90.3 us -> none  [the longest x64 45.4 us: step(): -decay[:, None] * times[None, :]]
    mul x64 -> x1, other arithmetic: 44.8 us -> 0.15 us  [shards_fast(): query_grad_a = gated_grad * response]
    unnamed x1 -> x0, blocking collectives: 35.1 us -> none
    dot_general x20 -> x12, matrix products: 63.8 us -> 29.5 us  [the longest x2 8.71 us: feed_back_only(): jnp.einsum('td,fd->tf', grad_low, w_down, preferred_element_type=jnp.floa...]
  transfers between devices with their start and end apart: 25 -> 12, of which waited for: 16 -> 5; matrix products, arithmetic and copies ran while one was open for 23% -> 30% of each run, Pallas kernels for 0% -> 23%
where the time goes in v1:
time: 834 us; the launch traced here: 822 us
  local copies, waits for them, and re-layouts  222 us (27%)
  Pallas kernels  187 us (22%)
  matrix products  125 us (15%)
  waiting for transfers between devices  96.2 us (12%)
  blocking collectives  89.3 us (11%)
  other arithmetic  62.6 us (8%)
  starting transfers between devices  22.5 us (3%)
  between operations  17.2 us (2%)
    pallas_call x1, Pallas kernels, weight_sums(): pl.pallas_call(functools.partial(weight_sum_kernel, kinds), out_shape=[ja...  173 us
    another operation x65, local copies, waits for them, and re-layouts, shards_fast(): taps_part = jnp.stack(tap_rows)  86.8 us
    dot_general x36, matrix products, mult(): jnp.einsum(form, left, right, precision=HIGH, preferred_element_type=jnp....  47.7 us
    all_gather x1, waiting for transfers between devices, shards_fast(): lax.all_gather(value_flat, 'seq', axis=0, tiled=True)  36.5 us
    all_gather x1, waiting for transfers between devices, shards_fast(): lax.all_gather(key_flat, 'seq', axis=0, tiled=True)  35.7 us
    all_gather x1, blocking collectives, shards_fast(): lax.all_gather(delta, 'seq', axis=1, tiled=True)  32.6 us
    all_gather x1, blocking collectives, shards_fast(): lax.all_gather(lse, 'seq', axis=1, tiled=True)  32.3 us
    unnamed x372, local copies, waits for them, and re-layouts  27.2 us
  transfers between devices with their start and end apart: 12, of which 5 were waited for; matrix products, arithmetic and copies ran while one was open for 30% of the time, Pallas kernels for 23%

profile of v1, /device:TPU:0, one launch (start us, length us, event | category | flops | bytes accessed | tf_op | source)
XLA Modules:
  0.0 822.5 jit_solution(573597789233842)
XLA Ops:
  11.2 2.7 fusion.648
  14.7 5.5 collective-permute-start
  24.8 5.7 shard_map.322
  34.4 2.1 fusion.463
  42.3 6.2 convert_bitcast_fusion.4
  50.3 4.3 all-to-all-start
  54.8 2.5 fusion.51
  59.3 3.1 all-to-all-done
  68.9 2.1 multiply_subtract_fusion.3
  81.4 3.8 reduce.129
  85.2 2.1 reshape.598
  87.2 11.8 %all_to_all.48 = bf16[8,2,6144]{2,1,0:T(2,128)(2,1)} all-to-all(bf16[8,2,6144]{2,1,0:T(2,128)(2,1)} %reshape.598), channel_id=1, replica_groups=mesh['seq'=8,'batch'=4] {'seq'}, dimensions={0} | all-to-all | bytes 393216 | tf_op jit(solution)/shard_map/all_to_all | solution.py:924
  111.1 4.8 multiply_convert_fusion.5
  126.4 35.7 %all-gather.5.cloned.1.call-done = bf16[1024,768]{1,0:T(8,128)(2,1)} async-done(((bf16[128,768]{1,0:T(8,128)(2,1)}), bf16[1024,768]{1,0:T(8,128)(2,1)}) %all-gather.5.cloned.1.call-update) | async-done | bytes 1572880 | tf_op jit(solution)/shard_map/all_gather | solution.py:960
  162.0 2.6 copy.243
  164.6 2.7 select_reduce_fusion
  171.3 36.5 %all-gather.7.cloned.1.call-done = bf16[1024,768]{1,0:T(8,128)(2,1)} async-done(((bf16[128,768]{1,0:T(8,128)(2,1)}), bf16[1024,768]{1,0:T(8,128)(2,1)}) %all-gather.7.cloned.1.call-update) | async-done | bytes 1572880 | tf_op jit(solution)/shard_map/all_gather | solution.py:961
  207.8 2.6 copy.244
  210.4 5.7 fusion.353
  217.0 4.7 multiply_convert_fusion.4
  221.7 4.4 fusion.32
  226.1 2.3 multiply_reduce_fusion.64
  244.9 3.4 reshape.501
  250.1 2.6 copy.256
  252.7 3.1 reshape.502.refs_1_
  257.1 2.6 copy.246
  260.8 32.6 %all_gather.25 = f32[12,1024]{1,0:T(8,128)} all-gather(f32[12,128]{1,0:T(8,128)S(1)} %fusion.351), channel_id=1, replica_groups=mesh['seq'=8,'batch'=4] {'seq'}, dimensions={1}, use_global_device_ids=true | all-gather | bytes 55296 | tf_op jit(solution)/shard_map/all_gather | solution.py:996
  293.4 32.3 %all_gather.23 = f32[12,1024]{1,0:T(8,128)} all-gather(f32[12,128]{1,0:T(8,128)} %get-tuple-element.293), channel_id=1, replica_groups=mesh['seq'=8,'batch'=4] {'seq'}, dimensions={1}, use_global_device_ids=true | all-gather | bytes 55296 | tf_op jit(solution)/shard_map/all_gather | solution.py:995
  325.8 4.2 fusion.44
  330.1 3.8 fusion.649
  333.8 7.4 fusion.38
  341.2 2.8 copy.248
  344.0 5.1 fusion.2
  349.1 8.8 %fusion.37 = bf16[12,64,128]{2,1,0:T(8,128)(2,1)} fusion(bf16[1024,12,64]{0,2,1:T(8,128)(2,1)} %bitcast.394, f32[12,1024,128]{2,1,0:T(8,128)} %fusion.649, f32[12,1024]{1,0:T(8,128)} %all_gather.25, f32[12,1024]{1,0:T(8,128)} %all_gather.23, pred[1024,128]{1,0:T(8,128)(4,1)} %fusion.85, bf16[1024,12,64]{0,2,1:T(8,128)(2,1)} %bitcast.415, ...), kind=kOutput, calls=%fused_computation.317 | convolution fusion | flops 412286976 | bytes 10059776 | tf_op jit(solution)/shard_map/while/body/eval_jaxpr/hqk,qhd->khd/dot_general | solution.py:170
  358.0 3.4 multiply_reduce_fusion.65
  362.9 4.3 fusion.25
  367.3 2.3 multiply_reduce_fusion.66
  371.2 3.0 multiply_reduce_fusion.67
  376.0 3.3 reshape.505
  384.4 4.5 all-to-all-start.2
  391.9 3.1 copy.260
  395.0 3.1 reshape.504.refs_5_
  398.1 2.6 copy.261
  400.8 3.1 reshape.506.refs_8_
  418.0 2.6 multiply_add_fusion
  428.3 2.1 copy.252
  430.4 3.8 reduce.130
  434.2 2.1 reshape.600
  436.2 5.9 all-to-all-start.3
  442.2 2.2 fusion.399
  449.5 2.0 copy.271
  451.5 8.8 %shard_map.324 = (f32[64,96]{1,0:T(8,128)}, f32[64,96]{1,0:T(8,128)}) custom-call(f32[64,96]{1,0:T(8,128)} %get-tuple-element.323.coef_ref, f32[64,96]{1,0:T(8,128)} %get-tuple-element.322.rate_ref, f32[1024,96]{1,0:T(8,128)} %bitcast.406), custom_call_target="tpu_custom_call" | custom-call | tf_op jit(solution)/shard_map/pallas_call | solution.py:843
  468.0 4.2 multiply_reduce_fusion
  480.7 3.3 collective-permute-done.1
  484.4 5.7 fusion.104
  490.2 3.3 fusion.99
  574.3 10.9 %stack.283 = f32[64,768]{1,0:T(8,128)} concatenate(f32[1,768]{1,0:T(1,128)} %stack.219, f32[1,768]{1,0:T(1,128)} %stack.220, f32[1,768]{1,0:T(1,128)} %stack.221, f32[1,768]{1,0:T(1,128)} %stack.222, f32[1,768]{1,0:T(1,128)} %stack.223, f32[1,768]{1,0:T(1,128)} %stack.224, f32[1,768]{1,0:T(1,128)} %stack.225, f32[1,768]{1,0:T(1,128)} %stack.226, f32[1,768]{1,0:T(1,128)} %stack.227, ...), dimensions={0} | concatenate | bytes 393216 | tf_op jit(solution)/shard_map/stack | solution.py:1095
  589.1 2.1 copy.264
  591.3 2.1 maximum_bitcast_fusion.1
  593.4 3.1 copy.266
  596.4 3.2 reshape.509.refs_12_
  599.6 172.9 %shard_map.323 = (f32[1152,128]{1,0:T(8,128)}, f32[576,128]{1,0:T(8,128)}, f32[1152,128]{1,0:T(8,128)}, f32[576,128]{1,0:T(8,128)}) custom-call(bf16[128,768]{1,0:T(8,128)(2,1)} %copy-done.53, bf16[2,128,1536]{2,1,0:T(8,128)(2,1)} %reshape.502.refs_1_, bf16[2,128,384]{2,1,0:T(8,128)(2,1)} %copy.267.refs_2_, bf16[128,3072]{1,0:T(8,128)(2,1)} %get-tuple-element.315.refs_3_, ...), custom_call_target="tpu_custom_call" | custom-call | tf_op jit(solution)/shard_map/pallas_call | solution.py:743
  782.8 12.5 %all-reduce = (f32[5,96]{1,0:T(8,128)S(1)}, f32[64,96]{1,0:T(8,128)}, f32[64,96]{1,0:T(8,128)}) all-reduce(f32[5,96]{1,0:T(8,128)S(1)} %copy.278, f32[64,96]{1,0:T(8,128)} %get-tuple-element.104, f32[64,96]{1,0:T(8,128)} %get-tuple-element.105), channel_id=1, replica_groups=mesh['seq'=8,'batch'=4] {'batch'}, use_global_device_ids=true, to_apply=%region_28.29 | all-reduce | flops 12768 | bytes 102144 | tf_op jit(solution)/shard_map/psum | solution.py:1121
  797.3 16.8 %reduce-scatter.8.cloned.1.call-done = bf16[16,96]{1,0:T(8,128)(2,1)} async-done(((bf16[64,96]{1,0:T(8,128)(2,1)}), bf16[16,96]{1,0:T(8,128)(2,1)}) %reduce-scatter.8.cloned.1.call-update) | async-done | bytes 3088 | tf_op jit(solution)/shard_map/reduce_scatter | solution.py:1118
  (606 shorter events, 240.1 us)
Async XLA Ops:
  7.2 110.9 %copy-start = (bf16[768,2304]{1,0:T(8,128)(2,1)S(1)}, bf16[768,2304]{1,0:T(8,128)(2,1)}, u32[]{:S(2)}) copy-start(bf16[768,2304]{1,0:T(8,128)(2,1)} %param.32) | copy-start | bytes 10616836
  11.2 9.7 %copy-start.65 = (f32[64,768]{1,0:T(8,128)S(1)}, f32[64,768]{1,0:T(8,128)}, u32[]{:S(2)}) copy-start(f32[64,768]{1,0:T(8,128)} %param.23) | copy-start | bytes 589828
  14.0 6.2 copy-start.14
  14.7 26.3 %collective-permute-start = (bf16[63,768]{1,0:T(8,128)(2,1)}, bf16[63,768]{1,0:T(8,128)(2,1)}, u32[]{:S(2)}, u32[]{:S(2)}) collective-permute-start(bf16[63,768]{1,0:T(8,128)(2,1)} %slice.3049), channel_id=1, source_target_pairs={{0,4},{4,8},{8,12},{12,16},{16,20},{20,24},{24,28},{1,5},{5,9},{9,... | collective-permute-start | bytes 290312 | tf_op jit(solution)/shard_map/ppermute | solution.py:21
  40.9 7.6 copy-start.137
  40.9 7.6 copy-start.138
  40.9 7.6 copy-start.139
  40.9 7.6 copy-start.140
  40.9 7.6 copy-start.141
  40.9 7.6 copy-start.142
  40.9 7.6 copy-start.143
  41.9 6.7 copy-start.9
  50.3 12.1 %all-to-all-start = ((bf16[8,96,128]{2,1,0:T(8,128)(2,1)}), bf16[8,96,128]{2,1,0:T(8,128)(2,1)}, u32[]{:S(2)}, u32[]{:S(2)}) async-start(bf16[8,96,128]{2,1,0:T(8,128)(2,1)} %bitcast.442), calls=%async_computation | async-start | bytes 393216 | tf_op jit(solution)/shard_map/all_to_all | solution.py:907
  54.5 107.5 %all-gather.5.cloned.1.call-start = ((), (), s32[]{:S(2)}) async-start(), calls=%async_computation.7 | async-start | bytes 1769472 | tf_op jit(solution)/shard_map/all_gather | solution.py:960
  109.7 6.2 copy-start.11
  109.7 6.2 slice-start.2
  119.7 88.2 %all-gather.7.cloned.1.call-start = ((), (), s32[]{:S(2)}) async-start(), calls=%async_computation.8 | async-start | bytes 1769472 | tf_op jit(solution)/shard_map/all_gather | solution.py:961
  120.4 136.7 %all-gather.9.cloned.1.call-start = ((), (), s32[]{:S(2)}) async-start(), calls=%async_computation.9 | async-start | bytes 1769472 | tf_op jit(solution)/shard_map/all_gather | solution.py:998
  125.9 215.3 %all-gather.11.cloned.1.call-start = ((), (), s32[]{:S(2)}) async-start(), calls=%async_computation.10 | async-start | bytes 1769472 | tf_op jit(solution)/shard_map/all_gather | solution.py:999
  210.4 5.7 copy-start.16
  210.4 5.7 copy-start.32
  216.6 11.8 %copy-start.13 = (f32[128,768]{1,0:T(8,128)}, f32[128,768]{1,0:T(8,128)S(1)}, u32[]{:S(2)}) copy-start(f32[128,768]{1,0:T(8,128)S(1)} %get-tuple-element.314) | copy-start | bytes 1179652
  217.0 9.1 %slice-start = ((s8[4718592]{0:T(1024)(128)(4,1)}), s8[4194304]{0:T(1024)(128)(4,1)S(1)}, s32[]{:S(2)}) async-start(s8[4718592]{0:T(1024)(128)(4,1)} %bitcast.396), calls=%async_computation.14 | async-start | bytes 8388608
  260.8 65.0 %copy-start.148 = (f32[12,128]{1,0:T(8,128)}, f32[12,128]{1,0:T(8,128)S(1)}, u32[]{:S(2)}) copy-start(f32[12,128]{1,0:T(8,128)S(1)} %fusion.351) | copy-start | bytes 18436
  358.0 9.2 %slice-start.4 = ((s8[4718592]{0:T(1024)(128)(4,1)}), s8[4194304]{0:T(1024)(128)(4,1)S(1)}, s32[]{:S(2)}) async-start(s8[4718592]{0:T(1024)(128)(4,1)} %bitcast.400), calls=%async_computation.18 | async-start | bytes 8388608
  361.6 5.6 copy-start.57
  384.4 26.7 %all-to-all-start.2 = ((bf16[8,96,128]{2,1,0:T(8,128)(2,1)}), bf16[8,96,128]{2,1,0:T(8,128)(2,1)}, u32[]{:S(2)}, u32[]{:S(2)}) async-start(bf16[8,96,128]{2,1,0:T(8,128)(2,1)} %bitcast.440), calls=%async_computation.2 | async-start | bytes 393216 | tf_op jit(solution)/shard_map/all_to_all | solution.py:1053
  436.2 24.1 %all-to-all-start.3 = ((bf16[8,2,6144]{2,1,0:T(2,128)(2,1)}), bf16[8,2,6144]{2,1,0:T(2,128)(2,1)}, u32[]{:S(2)}, u32[]{:S(2)}) async-start(bf16[8,2,6144]{2,1,0:T(2,128)(2,1)} %reshape.600), calls=%async_computation.3 | async-start | bytes 393216 | tf_op jit(solution)/shard_map/all_to_all | solution.py:1076
  442.2 339.7 %reduce-scatter.10.cloned.1.call-start = ((), (), s32[]{:S(2)}) async-start(), calls=%async_computation.12 | async-start | bytes 442368
  472.1 11.9 %copy-start.1 = (f32[128,768]{1,0:T(8,128)}, f32[128,768]{1,0:T(8,128)S(1)}, u32[]{:S(2)}) copy-start(f32[128,768]{1,0:T(8,128)S(1)} %get-tuple-element.262) | copy-start | bytes 1179652
  477.6 6.5 collective-permute-start.1
  479.1 5.0 copy-start.68
  479.1 5.0 copy-start.70
  479.1 5.0 copy-start.72
  479.2 5.0 copy-start.74
  479.2 5.0 copy-start.76
  479.2 5.0 copy-start.78
  479.2 5.0 copy-start.80
  479.2 5.0 copy-start.82
  479.2 5.0 copy-start.84
  479.2 5.0 copy-start.86
  479.2 5.0 copy-start.88
  479.2 5.0 copy-start.90
  479.2 5.0 copy-start.92
  479.3 5.0 copy-start.94
  479.3 5.0 copy-start.96
  479.3 5.0 copy-start.98
  479.3 5.0 copy-start.100
  479.3 5.0 copy-start.102
  479.3 5.0 copy-start.104
  479.3 5.0 copy-start.106
  479.3 5.0 copy-start.108
  479.3 5.0 copy-start.110
  479.3 5.0 copy-start.112
  479.4 5.0 copy-start.114
  479.4 5.0 copy-start.116
  479.4 5.0 copy-start.118
  479.4 10.7 %copy-start.35 = (bf16[768,2304]{1,0:T(8,128)(2,1)S(1)}, bf16[768,2304]{1,0:T(8,128)(2,1)}, u32[]{:S(2)}) copy-start(bf16[768,2304]{1,0:T(8,128)(2,1)} %param.22) | copy-start | bytes 10616836
  479.6 13.9 %copy-start.58 = (bf16[128,768]{1,0:T(8,128)(2,1)}, bf16[128,768]{1,0:T(8,128)(2,1)S(1)}, u32[]{:S(2)}) copy-start(bf16[128,768]{1,0:T(8,128)(2,1)S(1)} %get-tuple-element.300) | copy-start | bytes 589828
  479.6 13.9 %copy-start.59 = (bf16[128,768]{1,0:T(8,128)(2,1)}, bf16[128,768]{1,0:T(8,128)(2,1)S(1)}, u32[]{:S(2)}) copy-start(bf16[128,768]{1,0:T(8,128)(2,1)S(1)} %get-tuple-element.301) | copy-start | bytes 589828
  479.6 10.5 %copy-start.30 = (bf16[1,128,768]{2,1,0:T(8,128)(2,1)S(1)}, bf16[1,128,768]{2,1,0:T(8,128)(2,1)}, u32[]{:S(2)}) copy-start(bf16[1,128,768]{2,1,0:T(8,128)(2,1)} %param.19) | copy-start | bytes 589828
  493.5 80.2 %copy-start.153 = (f32[768]{0:T(1024)S(1)}, f32[768]{0:T(1024)}, u32[]{:S(2)}) copy-start(f32[768]{0:T(1024)} %get-tuple-element.123) | copy-start | bytes 9220
  497.1 298.2 %reduce-scatter.12.cloned.1.call-start = ((), (), s32[]{:S(2)}) async-start(), calls=%async_computation.13 | async-start | bytes 442368
  587.1 227.0 %reduce-scatter.8.cloned.1.call-start = ((), (), s32[]{:S(2)}) async-start(), calls=%async_computation.11 | async-start | bytes 20480 | tf_op jit(solution)/shard_map/reduce_scatter | solution.py:1118
  (125 other events, 407.5 us)
Sparse Core Ops, SparseCore 0:
  119.8 42.2 all-gather.4
  164.8 42.9 all-gather.6
  210.6 42.9 all-gather.8
  256.2 43.1 all-gather.10
  497.2 62.7 reduce-scatter.9
  587.2 63.1 reduce-scatter.11
  796.9 17.1 reduce-scatter.7

commit v2 on v0

--- a/solution.py
+++ b/solution.py
@@ -1,8 +1,13 @@
+import functools
 import math
 
 import jax
 import jax.numpy as jnp
+import ml_dtypes
+import numpy as np
 from jax import lax
+from jax.experimental import pallas as pl
+from jax.experimental.pallas import tpu as pltpu
 from jax.sharding import PartitionSpec as P
 
 HEADS = 12
@@ -543,6 +548,1129 @@
     )
 
 
+MESH = pl.DeviceIdType.MESH
+BF = jnp.bfloat16
+F32 = jnp.float32
+ROWS, WIDE, RANKS = (128, 768, 8)
+SPAN = ROWS * RANKS
+BLOCK = 128
+OWNERS = 6
+NT = (((1,), (1,)), ((), ()))
+TN = (((0,), (0,)), ((), ()))
+ROOT = math.sqrt(2.0 / math.pi)
+CUBIC = 0.044715
+
+
+def flip(value):
+    return 1 - value
+
+
+def mm(left, right):
+    return jnp.dot(left, right, preferred_element_type=F32)
+
+
+def mm_nt(left, right):
+    return lax.dot_general(left, right, NT, preferred_element_type=F32)
+
+
+def mm_tn(left, right):
+    return lax.dot_general(left, right, TN, preferred_element_type=F32)
+
+
+def is_owner(rank):
+    return jnp.logical_and(rank >= 1, rank <= OWNERS)
+
+
+def rows_of(rank):
+    return pl.ds(pl.multiple_of(ROWS * rank, ROWS), ROWS)
+
+
+def lanes_of(block):
+    return pl.ds(pl.multiple_of(BLOCK * block, BLOCK), BLOCK)
+
+
+class Spread:
+    def __init__(self, net, source, target, outward, only=None):
+        self.net, self.source, self.target, self.outward = net, source, target, outward
+        self.base = net.take(RANKS - 1)
+
+    def copy(self, step, source, target, rank):
+        at = self.base + step - 1
+        return pltpu.make_async_remote_copy(
+            src_ref=source,
+            dst_ref=target,
+            send_sem=self.net.send_sem.at[at],
+            recv_sem=self.net.recv_sem.at[at],
+            device_id=(rank, self.net.b),
+            device_id_type=MESH,
+        )
+
+    def each_send(self, act, chosen=None):
+        me = self.net.s
+        for step in range(1, RANKS):
+            rank = lax.rem(me + step, RANKS)
+            go = is_owner(rank) if self.outward else is_owner(me)
+            if chosen is not None:
+                go = jnp.logical_and(go, chosen(rank))
+
+            @pl.when(go)
+            def _(step=step, rank=rank):
+                if self.outward:
+                    act(self.copy(step, self.source(rank - 1), self.target(me), rank))
+                else:
+                    act(self.copy(step, self.source(rank), self.target(me - 1), rank))
+
+    def start(self, chosen=None):
+        self.each_send(lambda copy: copy.start(), chosen)
+
+    def own(self):
+        me = self.net.s
+
+        @pl.when(is_owner(me))
+        def _():
+            if self.outward:
+                self.target(me)[...] = self.source(me - 1)[...]
+            else:
+                self.target(me - 1)[...] = self.source(me)[...]
+
+    def wait_recv(self):
+        me = self.net.s
+        for step in range(1, RANKS):
+            rank = lax.rem(me + RANKS - step, RANKS)
+
+            @pl.when(is_owner(me) if self.outward else is_owner(rank))
+            def _(step=step, rank=rank):
+                landed = self.target(rank if self.outward else rank - 1)
+                self.copy(step, landed, landed, rank).wait_recv()
+
+    def wait_send(self):
+        self.each_send(lambda copy: copy.wait_send())
+
+
+class Net:
+    def __init__(self, send_sem, recv_sem):
+        self.send_sem, self.recv_sem = send_sem, recv_sem
+        self.s = lax.axis_index("seq")
+        self.b = lax.axis_index("batch")
+        self.used = 0
+        self.waiting = []
+
+    def take(self, count):
+        at = self.used
+        self.used += count
+        return at
+
+    def spread(self, source, target, outward):
+        made = Spread(self, source, target, outward)
+        self.waiting.append(made)
+        return made
+
+    def greet(self, others=()):
+        barrier = pltpu.get_barrier_semaphore()
+        for step in range(1, RANKS):
+            pl.semaphore_signal(
+                barrier, inc=1, device_id=(lax.rem(self.s + step, RANKS), self.b), device_id_type=MESH
+            )
+        for other in others:
+            pl.semaphore_signal(barrier, inc=1, device_id=other, device_id_type=MESH)
+        pl.semaphore_wait(barrier, RANKS - 1 + len(others))
+
+    def finish(self):
+        for made in self.waiting:
+            made.wait_send()
+
+
+class Beside:
+    def __init__(self, net, source, target, steps):
+        self.net, self.steps = net, steps
+        self.at = net.take(1)
+        other = jnp.clip(net.s + steps, 0, RANKS - 1)
+        self.copy = pltpu.make_async_remote_copy(
+            src_ref=source,
+            dst_ref=target,
+            send_sem=net.send_sem.at[self.at],
+            recv_sem=net.recv_sem.at[self.at],
+            device_id=(other, net.b),
+            device_id_type=MESH,
+        )
+        last = RANKS - 1 if steps > 0 else 0
+        first = 0 if steps > 0 else RANKS - 1
+        self.sends = net.s != last
+        self.takes = net.s != first
+        net.waiting.append(self)
+
+    def start(self):
+        @pl.when(self.sends)
+        def _():
+            self.copy.start()
+
+    def wait_recv(self):
+        @pl.when(self.takes)
+        def _():
+            self.copy.wait_recv()
+
+    def wait_send(self):
+        @pl.when(self.sends)
+        def _():
+            self.copy.wait_send()
+
+
+def pieces(value):
+    cent = value - jnp.mean(value, axis=-1, keepdims=True)
+    inverse = lax.rsqrt(jnp.mean(cent * cent, axis=-1, keepdims=True) + 1e-05)
+    return cent * inverse, inverse
+
+
+def pieces_back(incoming, normal, inverse, gain):
+    share = jnp.sum(incoming * normal, axis=0, keepdims=True)
+    scaled = incoming * gain
+    first = jnp.mean(scaled, axis=-1, keepdims=True)
+    second = jnp.mean(scaled * normal, axis=-1, keepdims=True)
+    return inverse * (scaled - first - normal * second), share
+
+
+def gelu_parts(u):
+    square = u * u
+    bend = jnp.tanh(ROOT * u * (1.0 + CUBIC * square))
+    half = 0.5 * (1.0 + bend)
+    value = u * half
+    slope = half + 0.5 * u * (1.0 - bend * bend) * (ROOT * (1.0 + 3.0 * CUBIC * square))
+    return value, slope
+
+
+def split(value):
+    high = value.astype(BF)
+    return high, (value - high.astype(F32)).astype(BF)
+
+
+def transform(r, high, low, re_out, im_out):
+    @pl.loop(0, 4)
+    def _(at):
+        rows = pl.ds(pl.multiple_of(256 * at, 256), 256)
+        for main, rest, out, sign in ((r.cos_high, r.cos_low, re_out, 1.0), (r.sin_high, r.sin_low, im_out, -1.0)):
+            total = mm(main[rows, :], high) + mm(rest[rows, :], high)
+            if low is not None:
+                total = total + mm(main[rows, :], low)
+            out[rows, :] = sign * total
+
+
+def inverse(r, re, im, out):
+    re_high, re_low = split(re)
+    im_high, im_low = split(im)
+    r.pack_re[:, 0:128] = re_high
+    r.pack_re[:, 128:256] = re_low
+    r.pack_im[:, 0:128] = im_high
+    r.pack_im[:, 128:256] = im_low
+
+    @pl.loop(0, 4)
+    def _(at):
+        rows = pl.ds(pl.multiple_of(256 * at, 256), 256)
+        both = mm(r.cos_high[rows, :], r.pack_re[...]) - mm(r.sin_high[rows, :], r.pack_im[...])
+        rest = mm(r.cos_low[rows, :], r.pack_re[:, 0:128]) - mm(r.sin_low[rows, :], r.pack_im[:, 0:128])
+        out[rows, :] = ((both[:, 0:128] + both[:, 128:256] + rest) * (1.0 / SPAN)).astype(out.dtype)
+
+
+def modes(coef_ref, rate_ref, out_ref):
+    blocks, width = out_ref.shape[0] // 8, out_ref.shape[1]
+    row = lax.broadcasted_iota(jnp.int32, (8, width), 0).astype(F32)
+    out_ref[...] = jnp.zeros_like(out_ref)
+
+    @pl.loop(0, 8)
+    def _(group):
+        some = pl.ds(pl.multiple_of(8 * group, 8), 8)
+        rate, coef = rate_ref[some, :], coef_ref[some, :]
+        falls = [coef[n : n + 1] * jnp.exp(-rate[n : n + 1] * row) for n in range(8)]
+        steps = [jnp.exp(-rate[n : n + 1] * jnp.maximum(row, 8.0)) for n in range(8)]
+
+        def step(at, falls):
+            rows = pl.ds(pl.multiple_of(8 * at, 8), 8)
+            out_ref[rows, :] += sum(falls[1:], falls[0])
+            return tuple(fall * factor for fall, factor in zip(falls, steps))
+
+        lax.fori_loop(0, blocks, step, tuple(falls), unroll=4)
+
+
+def modes_back(coef_ref, rate_ref, grad_ref, coef_out, rate_out):
+    blocks, width = grad_ref.shape[0] // 8, grad_ref.shape[1]
+    row = lax.broadcasted_iota(jnp.int32, (8, width), 0).astype(F32)
+
+    @pl.loop(0, 8)
+    def _(group):
+        some = pl.ds(pl.multiple_of(8 * group, 8), 8)
+        rate, coef = rate_ref[some, :], coef_ref[some, :]
+        steps = [jnp.exp(-rate[n : n + 1] * jnp.maximum(row, 8.0)) for n in range(8)]
+        zero = jnp.minimum(row, 0.0)
+
+        def step(at, carry):
+            totals, slopes = carry
+            here = grad_ref[pl.ds(pl.multiple_of(8 * (blocks - 1 - at), 8), 8), :]
+            slopes = tuple(slope * factor + total for slope, factor, total in zip(slopes, steps, totals))
+            totals = tuple(total * factor + here for total, factor in zip(totals, steps))
+            return totals, slopes
+
+        totals, slopes = lax.fori_loop(0, blocks, step, ((zero,) * 8, (zero,) * 8), unroll=2)
+        coef_rows, rate_rows = [], []
+        for n in range(8):
+            fall = jnp.exp(-rate[n : n + 1] * row)
+            coef_rows.append(jnp.sum(fall * totals[n], axis=0, keepdims=True))
+            late = jnp.sum(fall * (8.0 * steps[n] * slopes[n] + row * totals[n]), axis=0, keepdims=True)
+            rate_rows.append(-coef[n : n + 1] * late)
+        coef_out[some, :] = jnp.concatenate(coef_rows, axis=0)
+        rate_out[some, :] = jnp.concatenate(rate_rows, axis=0)
+
+
+def shift_forward(keys, taps, value, shifted):
+    @pl.loop(0, OWNERS)
+    def _(block):
+        lanes = lanes_of(block)
+        near = keys[:, lanes]
+        total = jnp.zeros((ROWS, BLOCK), F32)
+        for rest in range(8):
+            turned = pltpu.roll(near, rest, 0) if rest else near
+            for part in range(8):
+                total = total + taps[8 * part + rest : 8 * part + rest + 1, lanes] * turned[64 - 8 * part : 192 - 8 * part]
+        shifted[:, lanes] = total
+
+
+def shift_back(grads, keys, taps, key_grad, taps_grad):
+    @pl.loop(0, OWNERS)
+    def _(block):
+        lanes = lanes_of(block)
+        ahead, near = grads[:, lanes], keys[:, lanes]
+        here = ahead[0:ROWS]
+        total = jnp.zeros((ROWS, BLOCK), F32)
+        rows = {}
+        for rest in range(8):
+            later = pltpu.roll(ahead, 192 - rest, 0) if rest else ahead
+            turned = pltpu.roll(near, rest, 0) if rest else near
+            for part in range(8):
+                lag = 8 * part + rest
+                total = total + taps[lag : lag + 1, lanes] * later[8 * part : 8 * part + ROWS]
+                taps_grad[lag : lag + 1, lanes] = jnp.sum(here * turned[64 - 8 * part : 192 - 8 * part], axis=0, keepdims=True)
+        key_grad[:, lanes] = total
+
+
+def head_lanes(shape, head):
+    return lax.broadcasted_iota(jnp.int32, shape, 1) // 64 == head
+
+
+def document_start(ends, first, count):
+    at = first + lax.broadcasted_iota(jnp.int32, (count, 1), 0)
+    begin = jnp.zeros((count, 1), jnp.int32)
+    for index in range(3):
+        begin = jnp.where(at >= ends[index], ends[index], begin)
+    return at, begin
+
+
+def allowed_pairs(ends, part):
+    query_at, begin = document_start(ends, 256 * part, 256)
+    key_at = lax.broadcasted_iota(jnp.int32, (256, 256 * (part + 1)), 1)
+    return jnp.logical_and(key_at <= query_at, key_at >= begin)
+
+
+def attention_forward(r, part):
+    rows, keys = slice(256 * part, 256 * part + 256), slice(0, 256 * part + 256)
+    mask = allowed_pairs(r.ends, part)
+
+    @pl.loop(0, 2)
+    def _(head):
+        lanes = head_lanes((256, BLOCK), head)
+        query = jnp.where(lanes, r.qkv[0, rows, :].astype(F32) * 0.125, 0.0).astype(BF)
+        scores = jnp.where(mask, mm_nt(query, r.qkv[1, keys, :]), NEGATIVE)
+        top = jnp.max(scores, axis=1, keepdims=True)
+        weights = jnp.exp(scores - top)
+        mass = jnp.sum(weights, axis=1, keepdims=True)
+        mixed = mm(weights.astype(BF), r.qkv[2, keys, :]) / mass
+        r.attended_full[rows, :] = jnp.where(lanes, mixed, r.attended_full[rows, :])
+        r.lse[rows, :] = jnp.where(lanes, top + jnp.log(mass), r.lse[rows, :])
+
+    r.attended_low[rows, :] = r.attended_full[rows, :].astype(BF)
+
+
+def attention_back(r, part):
+    rows, keys = slice(256 * part, 256 * part + 256), slice(0, 256 * part + 256)
+    mask = allowed_pairs(r.ends, part)
+
+    @pl.loop(0, 2)
+    def _(head):
+        lanes = head_lanes((256, BLOCK), head)
+        query = jnp.where(lanes, r.qkv[0, rows, :].astype(F32) * 0.125, 0.0).astype(BF)
+        whole = r.att_grad[rows, :].astype(F32)
+        grads = jnp.where(lanes, whole, 0.0)
+        delta = jnp.sum(grads * r.attended_full[rows, :], axis=1, keepdims=True)
+        lse = jnp.sum(jnp.where(lanes, r.lse[rows, :], 0.0), axis=1, keepdims=True) * (1.0 / 64.0)
+        grads = grads.astype(BF)
+        scores = mm_nt(query, r.qkv[1, keys, :])
+        probs = jnp.where(mask, jnp.exp(scores - lse), 0.0)
+        score_grad = (probs * (mm_nt(grads, r.qkv[2, keys, :]) - delta)).astype(BF)
+        query_grad = mm(score_grad, r.qkv[1, keys, :]) * 0.125
+        r.query_grad[rows, :] = jnp.where(lanes, query_grad, r.query_grad[rows, :])
+        r.key_grad[keys, :] += mm_tn(score_grad, query)
+        r.value_grad[keys, :] += mm_tn(probs.astype(BF), grads)
+
+    r.qkv_grad[0, rows, :] = r.query_grad[rows, :].astype(BF)
+    r.qkv_grad[1, rows, :] = r.key_grad[rows, :].astype(BF)
+    r.qkv_grad[2, rows, :] = r.value_grad[rows, :].astype(BF)
+
+
+def load(r, sems, names):
+    copies = {}
+    for index, name in enumerate(names):
+        copies[name] = pltpu.make_async_copy(getattr(r, name + "_hbm"), getattr(r, name), sems.at[index])
+        copies[name].start()
+    return copies
+
+
+TABLES = ("cos_high", "sin_high", "cos_low", "sin_low")
+
+
+def kernel_a(r):
+    net = Net(r.send_sem, r.recv_sem)
+    wait = load(r, r.load_sem, ("mixer_in",) + TABLES + ("mixer_out", "up_first", "down_first", "project_in"))
+    me = net.s
+    stream = r.tokens[0].astype(F32)
+    normal, _ = pieces(stream)
+    r.normed_a[...] = (normal * r.mixer_norm_gain[...]).astype(BF)
+    wait["mixer_in"].wait()
+    r.key_ext[64:192, :] = mm(r.normed_a[...], r.mixer_in[:, WIDE : 2 * WIDE])
+    r.rim_out[...] = r.key_ext[128:192, :].astype(BF)
+    net.greet()
+    rim = Beside(net, r.rim_out, r.rim_in, 1)
+    rim.start()
+
+    @pl.when(me == 0)
+    def _():
+        r.rim_in[...] = jnp.zeros_like(r.rim_in)
+
+    r.query_a[...] = mm(r.normed_a[...], r.mixer_in[:, 0:WIDE])
+    r.value_a[...] = mm(r.normed_a[...], r.mixer_in[:, 2 * WIDE :])
+    rim.wait_recv()
+    r.key_ext[0:64, :] = r.rim_in[...].astype(F32)
+    shift_forward(r.key_ext, r.shift_taps, None, r.shifted)
+    r.product_low[...] = (r.shifted[...] * r.value_a[...]).astype(BF)
+    go = net.spread(lambda block: r.product_low.at[:, lanes_of(block)], lambda rank: r.signal.at[rows_of(rank), :], True)
+    go.start()
+    go.own()
+    modes(r.coef, r.rate, r.mode_rows)
+    high, low = split(r.mode_rows[...])
+    for name in TABLES:
+        wait[name].wait()
+    transform(r, high, low, r.kernel_re, r.kernel_im)
+    turned = r.kernel_re[...] * r.phase_cos[...] - r.kernel_im[...] * r.phase_sin[...]
+    r.kernel_im[...] = r.kernel_im[...] * r.phase_cos[...] + r.kernel_re[...] * r.phase_sin[...]
+    r.kernel_re[...] = turned
+    go.wait_recv()
+    transform(r, r.signal[...], None, r.signal_re, r.signal_im)
+    inverse(
+        r,
+        r.signal_re[...] * r.kernel_re[...] - r.signal_im[...] * r.kernel_im[...],
+        r.signal_re[...] * r.kernel_im[...] + r.signal_im[...] * r.kernel_re[...],
+        r.conv,
+    )
+    back = net.spread(lambda rank: r.conv.at[rows_of(rank), :], lambda block: r.conv_home.at[:, lanes_of(block)], False)
+    back.start()
+    back.own()
+    for name in ("mixer_out", "up_first", "down_first", "project_in"):
+        wait[name].wait()
+    back.wait_recv()
+    r.response[...] = r.conv_home[...].astype(F32) + r.skip_gain[...] * (r.shifted[...] * r.value_a[...])
+    r.gated[...] = (r.query_a[...] * r.response[...]).astype(BF)
+    stream_b = r.tokens[0].astype(F32) + mm(r.gated[...], r.mixer_out[...])
+    r.stream_b[...] = stream_b
+    normal, _ = pieces(stream_b)
+    r.normed_b[...] = (normal * r.gain_second[...]).astype(BF)
+    r.stream_c[...] = stream_b
+    for chunk in range(4):
+        lanes = slice(WIDE * chunk, WIDE * chunk + WIDE)
+        raised = mm(r.normed_b[...], r.up_first[:, lanes])
+        r.raised_b[:, lanes] = raised
+        active = gelu_parts(raised)[0].astype(BF)
+        r.active_b[:, lanes] = active
+        r.stream_c[...] += mm(active, r.down_first[lanes, :])
+    normal, _ = pieces(r.stream_c[...])
+    r.normed_c[...] = (normal * r.attention_norm_gain[...]).astype(BF)
+    for index in range(3):
+        r.mixed_c[index] = mm(r.normed_c[...], r.project_in[:, WIDE * index : WIDE * index + WIDE]).astype(BF)
+    go = net.spread(lambda block: r.mixed_c.at[:, :, lanes_of(block)], lambda rank: r.qkv.at[:, rows_of(rank), :], True)
+    go.start()
+    go.own()
+    go.wait_recv()
+    back = net.spread(lambda rank: r.attended_low.at[rows_of(rank), :], lambda block: r.attended.at[:, lanes_of(block)], False)
+    for part in (3, 2, 1, 0):
+        attention_forward(r, part)
+        back.start(lambda rank, part=part: rank // 2 == part)
+    back.own()
+    back.wait_recv()
+    net.finish()
+
+
+def kernel_b(r):
+    net = Net(r.send_sem, r.recv_sem)
+    wait = load(r, r.load_sem, ("project_out", "up_second", "down_second"))
+    wait["project_out"].wait()
+    stream_d = r.stream_c[...] + mm(r.attended[...], r.project_out[...])
+    normal, inverse_d = pieces(stream_d)
+    r.normed_d[...] = (normal * r.gain_fourth[...]).astype(BF)
+    r.total[...] = stream_d
+    wait["up_second"].wait()
+    wait["down_second"].wait()
+    for chunk in range(4):
+        lanes = slice(WIDE * chunk, WIDE * chunk + WIDE)
+        raised = mm(r.normed_d[...], r.up_second[:, lanes])
+        active, slope = gelu_parts(raised)
+        active = active.astype(BF)
+        r.active_d[:, lanes] = active
+        r.total[...] += mm(active, r.down_second[lanes, :])
+        slope = (slope * mm_nt(r.cotangent[0], r.down_second[lanes, :])).astype(BF)
+        r.slope_d[chunk % 2, :, WIDE * (chunk // 2) : WIDE * (chunk // 2) + WIDE] = slope
+        back = mm_nt(slope, r.up_second[:, lanes])
+        if chunk == 0:
+            r.grad_d[...] = back
+        else:
+            r.grad_d[...] += back
+    r.block_out[0] = r.total[...].astype(BF)
+    grad, r.gain_four[...] = pieces_back(r.grad_d[...], normal, inverse_d, r.gain_fourth[...])
+    grad = r.cotangent[0].astype(F32) + grad
+    r.grad_d[...] = grad
+    r.grad_d_low[...] = grad.astype(BF)
+    r.att_grad_home[...] = mm_nt(r.grad_d_low[...], r.project_out[...]).astype(BF)
+    net.greet()
+    go = net.spread(lambda block: r.att_grad_home.at[:, lanes_of(block)], lambda rank: r.att_grad.at[rows_of(rank), :], True)
+    go.start()
+    go.own()
+    r.key_grad[...] = jnp.zeros_like(r.key_grad)
+    r.value_grad[...] = jnp.zeros_like(r.value_grad)
+    go.wait_recv()
+    back = net.spread(
+        lambda rank: r.qkv_grad.at[:, rows_of(rank), :], lambda block: r.mixed_grad_c.at[:, :, lanes_of(block)], False
+    )
+    for part in (3, 2, 1, 0):
+        attention_back(r, part)
+        back.start(lambda rank, part=part: rank // 2 == part)
+    back.own()
+    back.wait_recv()
+    net.finish()
+
+
+def kernel_c(r):
+    net = Net(r.send_sem, r.recv_sem)
+    wait = load(r, r.load_sem, ("project_in", "up_first", "down_first", "mixer_out") + TABLES)
+    normal, inverse_c = pieces(r.stream_c[...])
+    wait["project_in"].wait()
+    grad = mm_nt(r.mixed_grad_c[0], r.project_in[:, 0:WIDE])
+    for index in range(1, 3):
+        grad = grad + mm_nt(r.mixed_grad_c[index], r.project_in[:, WIDE * index : WIDE * index + WIDE])
+    grad, r.gain_three[...] = pieces_back(grad, normal, inverse_c, r.attention_norm_gain[...])
+    grad = grad + r.grad_d[...]
+    r.grad_c[...] = grad
+    r.grad_c_low[...] = grad.astype(BF)
+    wait["up_first"].wait()
+    wait["down_first"].wait()
+    for chunk in range(4):
+        lanes = slice(WIDE * chunk, WIDE * chunk + WIDE)
+        slope = gelu_parts(r.raised_b[:, lanes])[1]
+        slope = (slope * mm_nt(r.grad_c_low[...], r.down_first[lanes, :])).astype(BF)
+        r.slope_b[chunk % 2, :, WIDE * (chunk // 2) : WIDE * (chunk // 2) + WIDE] = slope
+        back = mm_nt(slope, r.up_first[:, lanes])
+        if chunk == 0:
+            r.grad_b[...] = back
+        else:
+            r.grad_b[...] += back
+    normal, inverse_b = pieces(r.stream_b[...])
+    grad, r.gain_two[...] = pieces_back(r.grad_b[...], normal, inverse_b, r.gain_second[...])
+    grad = grad + r.grad_c[...]
+    r.grad_b[...] = grad
+    r.grad_b_low[...] = grad.astype(BF)
+    wait["mixer_out"].wait()
+    gated_grad = mm_nt(r.grad_b_low[...], r.mixer_out[...])
+    r.query_grad_a[...] = (gated_grad * r.response[...]).astype(BF)
+    response_grad = gated_grad * r.query_a[...]
+    r.response_grad[...] = response_grad
+    r.response_grad_low[...] = response_grad.astype(BF)
+    net.greet()
+    go = net.spread(
+        lambda block: r.response_grad_low.at[:, lanes_of(block)], lambda rank: r.conv_grad.at[rows_of(rank), :], True
+    )
+    go.start()
+    go.own()
+    r.skip_part[...] = jnp.sum(response_grad * (r.shifted[...] * r.value_a[...]), axis=0, keepdims=True)
+    for name in TABLES:
+        wait[name].wait()
+    go.wait_recv()
+    transform(r, r.conv_grad[...], None, r.grad_re, r.grad_im)
+    inverse(
+        r,
+        r.grad_re[...] * r.kernel_re[...] + r.grad_im[...] * r.kernel_im[...],
+        r.grad_im[...] * r.kernel_re[...] - r.grad_re[...] * r.kernel_im[...],
+        r.signal_grad,
+    )
+    back = net.spread(
+        lambda rank: r.signal_grad.at[rows_of(rank), :], lambda block: r.signal_grad_home.at[:, lanes_of(block)], False
+    )
+    back.start()
+    back.own()
+    re = r.grad_re[...] * r.signal_re[...] + r.grad_im[...] * r.signal_im[...]
+    im = r.grad_im[...] * r.signal_re[...] - r.grad_re[...] * r.signal_im[...]
+    inverse(
+        r,
+        re * r.phase_cos[...] + im * r.phase_sin[...],
+        im * r.phase_cos[...] - re * r.phase_sin[...],
+        r.kernel_grad,
+    )
+    modes_back(r.coef, r.rate, r.kernel_grad, r.coef_part, r.rate_part)
+    back.wait_recv()
+    net.finish()
+
+
+def kernel_d(r):
+    net = Net(r.send_sem, r.recv_sem)
+    wait = load(r, r.load_sem, ("mixer_in",))
+    signal_grad = r.signal_grad_home[...].astype(F32) + r.skip_gain[...] * r.response_grad[...]
+    r.grad_ext[0:ROWS, :] = signal_grad * r.value_a[...]
+    r.rim_out[...] = r.grad_ext[0:64, :].astype(BF)
+    net.greet()
+    rim = Beside(net, r.rim_out, r.rim_in, -1)
+    rim.start()
+    r.mixed_grad_a[0] = r.query_grad_a[...]
+    r.mixed_grad_a[2] = (signal_grad * r.shifted[...]).astype(BF)
+
+    @pl.when(net.s == RANKS - 1)
+    def _():
+        r.rim_in[...] = jnp.zeros_like(r.rim_in)
+
+    rim.wait_recv()
+    r.grad_ext[ROWS:192, :] = r.rim_in[...].astype(F32)
+    shift_back(r.grad_ext, r.key_ext, r.shift_taps, r.key_grad_a, r.taps_part)
+    r.mixed_grad_a[1] = r.key_grad_a[...].astype(BF)
+    wait["mixer_in"].wait()
+    grad = mm_nt(r.mixed_grad_a[0], r.mixer_in[:, 0:WIDE])
+    for index in range(1, 3):
+        grad = grad + mm_nt(r.mixed_grad_a[index], r.mixer_in[:, WIDE * index : WIDE * index + WIDE])
+    normal, inverse_a = pieces(r.tokens[0].astype(F32))
+    grad, r.gain_one[...] = pieces_back(grad, normal, inverse_a, r.mixer_norm_gain[...])
+    r.token_grad[0] = r.grad_b[...] + grad
+    net.finish()
+
+
+class Refs:
+    pass
+
+
+def call(body, identity, inputs, hbm, smem, outs, scratch, copies, loads):
+    names = list(inputs) + [name + "_hbm" for name in hbm] + list(smem) + list(outs) + list(scratch) + list(hbm)
+    names += ["send_sem", "recv_sem", "load_sem"]
+
+    def run(*refs):
+        r = Refs()
+        for name, ref in zip(names, refs):
+            setattr(r, name, ref)
+        body(r)
+
+    vmem = pl.BlockSpec(memory_space=pltpu.VMEM)
+    results = pl.pallas_call(
+        run,
+        out_shape=[jax.ShapeDtypeStruct(shape, kind) for shape, kind in outs.values()],
+        in_specs=[vmem] * len(inputs)
+        + [pl.BlockSpec(memory_space=pl.ANY)] * len(hbm)
+        + [pl.BlockSpec(memory_space=pltpu.SMEM)] * len(smem),
+        out_specs=[vmem] * len(outs),
+        scratch_shapes=[pltpu.VMEM(shape, kind) for shape, kind in scratch.values()]
+        + [pltpu.VMEM(array.shape, array.dtype) for array in hbm.values()]
+        + [pltpu.SemaphoreType.DMA((copies,)), pltpu.SemaphoreType.DMA((copies,)), pltpu.SemaphoreType.DMA((loads,))],
+        compiler_params=pltpu.CompilerParams(
+            collective_id=identity, has_side_effects=True, vmem_limit_bytes=60 * 2**20
+        ),
+    )(*inputs.values(), *hbm.values(), *smem.values())
+    return dict(zip(outs, results))
+
+
+def odd_tables():
+    odd = 2 * np.arange(SPAN, dtype=np.int64) + 1
+    angle = (np.outer(odd, odd) % (8 * SPAN)) * (math.pi / (4 * SPAN))
+    tables = {}
+    for name, table in (("cos", np.cos(angle)), ("sin", np.sin(angle))):
+        high = table.astype(ml_dtypes.bfloat16)
+        tables[name + "_high"] = jnp.asarray(high)
+        tables[name + "_low"] = jnp.asarray((table - high.astype(np.float64)).astype(ml_dtypes.bfloat16))
+    phase = (odd * (math.pi / (4 * SPAN)))[:, None] * np.ones((1, BLOCK))
+    return tables, jnp.asarray(np.cos(phase), F32), jnp.asarray(np.sin(phase), F32)
+
+
+LAYER, PAIR = (0, 1)
+GIVEN = (4, 3)
+OWN = (5, 3)
+
+
+def weight_sum_kernel(kinds, *refs):
+    refs = list(refs)
+    given = [[refs.pop(0) for _ in range(GIVEN[kind])] for kind in kinds]
+    outs = [refs.pop(0) for _ in kinds]
+    own_of = [[refs.pop(0) for _ in range(OWN[kind])] for kind in kinds]
+    sums_of = [[refs.pop(0) for _ in range(7)] for kind in kinds]
+    send_sem, recv_sem = refs
+    s = lax.axis_index("seq")
+    b = lax.axis_index("batch")
+    z, x = s // 2, lax.rem(s, 2)
+    y, c = b // 2, lax.rem(b, 2)
+    zh, zl = z // 2, lax.rem(z, 2)
+    sibling = (s, 2 * y + flip(c))
+    by_x = (2 * z + flip(x), b)
+    by_y = (s, 2 * flip(y) + c)
+    by_l = (2 * (2 * zh + flip(zl)) + x, b)
+    by_h = (2 * (2 * flip(zh) + zl) + x, b)
+    barrier = pltpu.get_barrier_semaphore()
+    for other in (sibling, by_x, by_y, by_l, by_h):
+        pl.semaphore_signal(barrier, inc=1, device_id=other, device_id_type=MESH)
+    pl.semaphore_wait(barrier, 5)
+    started = []
+
+    def send(source, target, other):
+        at = len(started)
+        copy = pltpu.make_async_remote_copy(
+            src_ref=source,
+            dst_ref=target,
+            send_sem=send_sem.at[at],
+            recv_sem=recv_sem.at[at],
+            device_id=other,
+            device_id_type=MESH,
+        )
+        copy.start()
+        started.append(copy)
+        return copy
+
+    shared = []
+    for kind, inputs, own in zip(kinds, given, own_of):
+        mine = []
+        own[0][:, 0:128] = inputs[0][...].T
+        mine.append(send(own[0].at[:, 0:128], own[0].at[:, 128:256], sibling))
+        own[1][0:128, :] = inputs[1][c]
+        mine.append(send(inputs[1].at[flip(c)], own[1].at[128:256, :], sibling))
+        if kind == LAYER:
+            own[3][...] = inputs[2][...].T
+            for at in range(2):
+                rows = pl.ds(pl.multiple_of(192 * (2 * at + c), 64), 192)
+                own[2][192 * at : 192 * at + 192, 0:128] = own[3][rows, :]
+                rows = pl.ds(pl.multiple_of(192 * (2 * at + flip(c)), 64), 192)
+                mine.append(send(own[3].at[rows, :], own[2].at[192 * at : 192 * at + 192, 128:256], sibling))
+            own[4][0:128, :] = inputs[3][...]
+            mine.append(send(inputs[3], own[4].at[128:256, :], sibling))
+        else:
+            own[2][:, 0:128] = inputs[2][...].T
+            mine.append(send(own[2].at[:, 0:128], own[2].at[:, 128:256], sibling))
+        shared.append(mine)
+
+    stages = []
+    for kind, own, sums, mine in zip(kinds, own_of, sums_of, shared):
+        for copy in mine:
+            copy.wait_recv()
+        grads, near_a, near_b, next_a, next_b, third, fourth = sums
+        half = grads.shape[4] // 2
+
+        def place(product, at, tile):
+            for block in range(8):
+                grads[block % 2, at, block // 4, (block // 2) % 2, pl.ds(pl.multiple_of(96 * tile, 16), 96), :] = product[
+                    96 * block : 96 * block + 96
+                ].astype(BF)
+
+        if kind == LAYER:
+
+            @pl.loop(0, 6)
+            def _(step):
+                at, chunk = step // 3, lax.rem(step, 3)
+                lanes = pl.ds(pl.multiple_of(256 * step, 256), 256)
+                product = jnp.dot(own[0][...], own[1][:, lanes], preferred_element_type=F32)
+                place(product[:, 0:128], at, 2 * chunk)
+                place(product[:, 128:256], at, 2 * chunk + 1)
+
+            @pl.loop(0, 8)
+            def _(block):
+                lanes = pl.ds(pl.multiple_of(384 * block, 384), 384)
+                product = jnp.dot(own[2][...], own[4][:, lanes], preferred_element_type=F32)
+                for at in range(2):
+                    for tile in range(3):
+                        grads[
+                            lax.rem(block, 2), at, block // 4, lax.rem(block // 2, 2), 576 + 192 * tile : 768 + 192 * tile, :
+                        ] = product[192 * at : 192 * at + 192, 128 * tile : 128 * tile + 128].astype(BF)
+
+        else:
+
+            @pl.loop(0, 2)
+            def _(at):
+                for chunk in range(3):
+                    lanes = pl.ds(pl.multiple_of(768 * at + 256 * chunk, 256), 256)
+                    right = own[1][:, lanes]
+                    if chunk < 2:
+                        product = jnp.dot(own[0][...], right, preferred_element_type=F32)
+                    else:
+                        first = lax.broadcasted_iota(jnp.int32, right.shape, 1) < 64
+                        zero = jnp.zeros_like(right)
+                        product = jnp.dot(own[0][...], jnp.where(first, right, zero), preferred_element_type=F32)
+                        product += jnp.dot(own[2][...], jnp.where(first, zero, right), preferred_element_type=F32)
+                    place(product[:, 0:128], at, 2 * chunk)
+                    place(product[:, 128:256], at, 2 * chunk + 1)
+
+        stages.append(
+            [
+                send(grads.at[flip(x), :, :, :, 0:half, :], near_a, by_x),
+                send(grads.at[:, flip(y), :, :, half:, :], near_b, by_y),
+            ]
+        )
+
+    for index, sums in enumerate(sums_of):
+        grads, near_a, near_b, next_a, next_b, third, fourth = sums
+        half = grads.shape[4] // 2
+        for copy in stages[index]:
+            copy.wait_recv()
+
+        @pl.loop(0, 8)
+        def _(step):
+            high, mid, low = step // 4, lax.rem(step // 2, 2), lax.rem(step, 2)
+            grads[x, high, mid, low, 0:half, :] += near_a[high, mid, low]
+            grads[high, y, mid, low, half:, :] += near_b[high, mid, low]
+
+        stages[index] = [
+            send(grads.at[x, flip(y), :, :, 0:half, :], next_a, by_y),
+            send(grads.at[flip(x), y, :, :, half:, :], next_b, by_x),
+        ]
+    for index, sums in enumerate(sums_of):
+        grads, near_a, near_b, next_a, next_b, third, fourth = sums
+        half = grads.shape[4] // 2
+        for copy in stages[index]:
+            copy.wait_recv()
+
+        @pl.loop(0, 4)
+        def _(step):
+            mid, low = step // 2, lax.rem(step, 2)
+            grads[x, y, mid, low, 0:half, :] += next_a[mid, low]
+            grads[x, y, mid, low, half:, :] += next_b[mid, low]
+
+        stages[index] = [send(grads.at[x, y, :, flip(zl), :, :], third, by_l)]
+    for index, sums in enumerate(sums_of):
+        grads, near_a, near_b, next_a, next_b, third, fourth = sums
+        for copy in stages[index]:
+            copy.wait_recv()
+
+        @pl.loop(0, 2)
+        def _(mid):
+            grads[x, y, mid, zl] += third[mid]
+
+        stages[index] = [send(grads.at[x, y, flip(zh), zl], fourth, by_h)]
+    for index, sums in enumerate(sums_of):
+        grads, near_a, near_b, next_a, next_b, third, fourth = sums
+        for copy in stages[index]:
+            copy.wait_recv()
+        outs[index][...] = grads[x, y, zh, zl].astype(F32) + fourth[...].astype(F32)
+    for copy in started:
+        copy.wait_send()
+
+
+def weight_sums(kinds, groups, identity):
+    lengths = [1152 if kind == LAYER else 576 for kind in kinds]
+    own, sums = [], []
+    for kind, length in zip(kinds, lengths):
+        own += [pltpu.VMEM((768, 256), BF), pltpu.VMEM((256, 1536), BF)]
+        if kind == LAYER:
+            own += [pltpu.VMEM((384, 256), BF), pltpu.VMEM((768, 128), BF), pltpu.VMEM((256, 3072), BF)]
+        else:
+            own += [pltpu.VMEM((768, 256), BF)]
+        half = length // 2
+        sums += [
+            pltpu.VMEM((2, 2, 2, 2, length, 128), BF),
+            pltpu.VMEM((2, 2, 2, half, 128), BF),
+            pltpu.VMEM((2, 2, 2, half, 128), BF),
+            pltpu.VMEM((2, 2, half, 128), BF),
+            pltpu.VMEM((2, 2, half, 128), BF),
+            pltpu.VMEM((2, length, 128), BF),
+            pltpu.VMEM((length, 128), BF),
+        ]
+    copies = sum(GIVEN[kind] + (7 if kind == LAYER else 6) for kind in kinds)
+    flat = [array for group in groups for array in group]
+    vmem = pl.BlockSpec(memory_space=pltpu.VMEM)
+    return pl.pallas_call(
+        functools.partial(weight_sum_kernel, kinds),
+        out_shape=[jax.ShapeDtypeStruct((length, 128), F32) for length in lengths],
+        in_specs=[vmem] * len(flat),
+        out_specs=[vmem] * len(kinds),
+        scratch_shapes=own + sums + [pltpu.SemaphoreType.DMA((copies,)), pltpu.SemaphoreType.DMA((copies,))],
+        compiler_params=pltpu.CompilerParams(
+            collective_id=identity, has_side_effects=True, vmem_limit_bytes=60 * 2**20
+        ),
+    )(*flat)
+
+
+def pair_columns(wide, narrow):
+    parts = jnp.concatenate([wide.reshape(128, 4, 576), narrow.reshape(128, 4, 192)], axis=2)
+    return parts.reshape(128, 2, 2, 768).transpose(2, 0, 1, 3).reshape(2, 128, 1536)
+
+
+def untile_layer(block):
+    up = block[:576].reshape(6, 96, 128).transpose(1, 0, 2).reshape(96, 768)
+    down = block[576:].reshape(3, 192, 128).transpose(0, 2, 1).reshape(384, 192)
+    return up, down
+
+
+def untile_pair(block):
+    both = block.reshape(6, 96, 128).transpose(1, 0, 2).reshape(96, 768)
+    return both[:, :576], both[:, 576:]
+
+
+def shards_fast(
+    tokens,
+    doc_lengths,
+    mixer_norm_gain,
+    mixer_in,
+    shift_taps,
+    mode_coef,
+    mode_rate,
+    skip_gain,
+    mixer_out,
+    gain_second,
+    up_first,
+    down_first,
+    attention_norm_gain,
+    project_in,
+    project_out,
+    gain_fourth,
+    up_second,
+    down_second,
+    cotangent,
+):
+    rank = lax.axis_index("seq")
+    mixer_norm_gain, skip_gain, gain_second, attention_norm_gain, gain_fourth = (
+        gain[None] for gain in (mixer_norm_gain, skip_gain, gain_second, attention_norm_gain, gain_fourth)
+    )
+    ends = jnp.cumsum(doc_lengths[0]).astype(jnp.int32)
+    first = BLOCK * jnp.clip(rank - 1, 0, OWNERS - 1)
+    coef = lax.dynamic_slice_in_dim(mode_coef, first, BLOCK, 1)
+    rate = lax.dynamic_slice_in_dim(mode_rate, first, BLOCK, 1)
+    tables, phase_cos, phase_sin = odd_tables()
+    home = (ROWS, WIDE)
+    span = (SPAN, BLOCK)
+    a = call(
+        kernel_a,
+        1,
+        dict(
+            tokens=tokens,
+            mixer_norm_gain=mixer_norm_gain,
+            shift_taps=shift_taps,
+            coef=coef,
+            rate=rate,
+            skip_gain=skip_gain,
+            gain_second=gain_second,
+            attention_norm_gain=attention_norm_gain,
+            phase_cos=phase_cos,
+            phase_sin=phase_sin,
+        ),
+        dict(mixer_in=mixer_in, **tables, mixer_out=mixer_out, up_first=up_first, down_first=down_first, project_in=project_in),
+        dict(ends=ends),
+        dict(
+            normed_a=(home, BF),
+            query_a=(home, F32),
+            value_a=(home, F32),
+            key_ext=((192, WIDE), F32),
+            shifted=(home, F32),
+            response=(home, F32),
+            gated=(home, BF),
+            stream_b=(home, F32),
+            normed_b=(home, BF),
+            raised_b=((ROWS, 4 * WIDE), F32),
+            active_b=((ROWS, 4 * WIDE), BF),
+            stream_c=(home, F32),
+            normed_c=(home, BF),
+            attended=(home, BF),
+            qkv=((3, *span), BF),
+            lse=(span, F32),
+            attended_full=(span, F32),
+            kernel_re=(span, F32),
+            kernel_im=(span, F32),
+            signal_re=(span, F32),
+            signal_im=(span, F32),
+        ),
+        dict(
+            rim_out=((64, WIDE), BF),
+            rim_in=((64, WIDE), BF),
+            product_low=(home, BF),
+            signal=(span, BF),
+            mode_rows=(span, F32),
+            conv=(span, BF),
+            conv_home=(home, BF),
+            pack_re=((SPAN, 256), BF),
+            pack_im=((SPAN, 256), BF),
+            mixed_c=((3, *home), BF),
+            attended_low=(span, BF),
+        ),
+        29,
+        9,
+    )
+    b = call(
+        kernel_b,
+        2,
+        dict(
+            stream_c=a["stream_c"],
+            attended=a["attended"],
+            gain_fourth=gain_fourth,
+            cotangent=cotangent,
+            qkv=a["qkv"],
+            lse=a["lse"],
+            attended_full=a["attended_full"],
+        ),
+        dict(project_out=project_out, up_second=up_second, down_second=down_second),
+        dict(ends=ends),
+        dict(
+            block_out=((1, *home), BF),
+            normed_d=(home, BF),
+            active_d=((ROWS, 4 * WIDE), BF),
+            slope_d=((2, ROWS, 2 * WIDE), BF),
+            grad_d=(home, F32),
+            grad_d_low=(home, BF),
+            gain_four=((1, WIDE), F32),
+            mixed_grad_c=((3, *home), BF),
+        ),
+        dict(
+            total=(home, F32),
+            att_grad_home=(home, BF),
+            att_grad=(span, BF),
+            query_grad=(span, F32),
+            key_grad=(span, F32),
+            value_grad=(span, F32),
+            qkv_grad=((3, *span), BF),
+        ),
+        14,
+        3,
+    )
+    c = call(
+        kernel_c,
+        3,
+        dict(
+            stream_c=a["stream_c"],
+            stream_b=a["stream_b"],
+            mixed_grad_c=b["mixed_grad_c"],
+            attention_norm_gain=attention_norm_gain,
+            gain_second=gain_second,
+            grad_d=b["grad_d"],
+            raised_b=a["raised_b"],
+            response=a["response"],
+            query_a=a["query_a"],
+            shifted=a["shifted"],
+            value_a=a["value_a"],
+            kernel_re=a["kernel_re"],
+            kernel_im=a["kernel_im"],
+            signal_re=a["signal_re"],
+            signal_im=a["signal_im"],
+            phase_cos=phase_cos,
+            phase_sin=phase_sin,
+            coef=coef,
+            rate=rate,
+        ),
+        dict(project_in=project_in, up_first=up_first, down_first=down_first, mixer_out=mixer_out, **tables),
+        dict(),
+        dict(
+            gain_three=((1, WIDE), F32),
+            gain_two=((1, WIDE), F32),
+            skip_part=((1, WIDE), F32),
+            grad_c_low=(home, BF),
+            slope_b=((2, ROWS, 2 * WIDE), BF),
+            grad_b=(home, F32),
+            grad_b_low=(home, BF),
+            query_grad_a=(home, BF),
+            response_grad=(home, F32),
+            signal_grad_home=(home, BF),
+            coef_part=((64, BLOCK), F32),
+            rate_part=((64, BLOCK), F32),
+        ),
+        dict(
+            grad_c=(home, F32),
+            response_grad_low=(home, BF),
+            conv_grad=(span, BF),
+            grad_re=(span, F32),
+            grad_im=(span, F32),
+            signal_grad=(span, BF),
+            kernel_grad=(span, F32),
+            pack_re=((SPAN, 256), BF),
+            pack_im=((SPAN, 256), BF),
+        ),
+        14,
+        8,
+    )
+    d = call(
+        kernel_d,
+        4,
+        dict(
+            tokens=tokens,
+            mixer_norm_gain=mixer_norm_gain,
+            shift_taps=shift_taps,
+            skip_gain=skip_gain,
+            signal_grad_home=c["signal_grad_home"],
+            response_grad=c["response_grad"],
+            value_a=a["value_a"],
+            shifted=a["shifted"],
+            key_ext=a["key_ext"],
+            query_grad_a=c["query_grad_a"],
+            grad_b=c["grad_b"],
+        ),
+        dict(mixer_in=mixer_in),
+        dict(),
+        dict(
+            mixed_grad_a=((3, *home), BF),
+            taps_part=((64, WIDE), F32),
+            gain_one=((1, WIDE), F32),
+            token_grad=((1, *home), F32),
+        ),
+        dict(
+            grad_ext=((192, WIDE), F32),
+            rim_out=((64, WIDE), BF),
+            rim_in=((64, WIDE), BF),
+            key_grad_a=(home, F32),
+        ),
+        1,
+        1,
+    )
+    mixed_grad_a = d["mixed_grad_a"].transpose(1, 0, 2).reshape(ROWS, 3 * WIDE)
+    mixed_grad_c = b["mixed_grad_c"].transpose(1, 0, 2).reshape(ROWS, 3 * WIDE)
+    groups = (
+        (b["normed_d"], b["slope_d"], cotangent[0], b["active_d"]),
+        (a["normed_c"], pair_columns(mixed_grad_c, b["grad_d_low"]), a["attended"]),
+        (a["normed_b"], c["slope_b"], c["grad_c_low"], a["active_b"]),
+        (a["normed_a"], pair_columns(mixed_grad_a, c["grad_b_low"]), a["gated"]),
+    )
+    layer_d, pair_c, layer_b, pair_a = weight_sums((LAYER, PAIR, LAYER, PAIR), groups, 0)
+    up_two, down_two = untile_layer(layer_d)
+    in_c, out_c = untile_pair(pair_c)
+    up_one, down_one = untile_layer(layer_b)
+    in_a, out_a = untile_pair(pair_a)
+    owner = is_owner(rank)
+    modes_part = jnp.concatenate([c["coef_part"], c["rate_part"]], axis=0)
+    modes_part = lax.dynamic_update_slice_in_dim(
+        jnp.zeros((128, WIDE), F32), jnp.where(owner, modes_part, 0.0), first, 1
+    )
+    small = jnp.concatenate(
+        [d["taps_part"], modes_part, d["gain_one"], c["skip_part"], c["gain_two"], c["gain_three"], b["gain_four"]], axis=0
+    )
+    small = lax.psum_scatter(small, "seq", scatter_dimension=1, tiled=True)
+    taps = lax.psum_scatter(small[0:64].astype(BF), "batch", scatter_dimension=0, tiled=True).astype(F32)
+    rest = lax.psum(small[64:], "batch")
+    return (
+        b["block_out"],
+        d["token_grad"],
+        rest[128],
+        in_a,
+        taps,
+        rest[0:64],
+        rest[64:128],
+        rest[129],
+        out_a,
+        rest[130],
+        up_one,
+        down_one,
+        rest[131],
+        in_c,
+        out_c,
+        rest[132],
+        up_two,
+        down_two,
+    )
+
+
 def solution(mesh):
     in_specs = (
         P("batch", "seq", None),
@@ -585,4 +1713,5 @@
         P("seq", "batch"),
         P("seq", "batch"),
     )
-    return jax.shard_map(shards, mesh=mesh, in_specs=in_specs, out_specs=out_specs, check_vma=False)
+    fast = mesh.shape["seq"] == RANKS and mesh.shape["batch"] == 4
+    return jax.shard_map(shards_fast if fast else shards, mesh=mesh, in_specs=in_specs, out_specs=out_specs, check_vma=False)

time: 1940 us -> 424 us (0.22)
  waiting for transfers between devices: 1180 us -> 16 us
  Pallas kernels: 0 us -> 340 us
  other arithmetic: 330 us -> 3.5 us
  matrix products: 155 us -> 0 us
  blocking collectives: 146 us -> 12.5 us
  local copies, waits for them, and re-layouts: 85.3 us -> 29.5 us
    reduce_scatter x11 -> x1, waiting for transfers between devices: 1060 us -> 16 us  [shards_fast(): lax.psum_scatter(small[0:64].astype(BF), 'batch', scatter_dimension=0, ti...]
    pallas_call x0 -> x5, Pallas kernels: none -> 340 us  [the longest x1 173 us: weight_sums(): pl.pallas_call(functools.partial(weight_sum_kernel, kinds), out_shape=[ja...]
    dot_general x66 -> x0, matrix products: 155 us -> none  [the longest x36 43.7 us: mult(): jnp.einsum(form, left, right, precision=HIGH, preferred_element_type=jnp....]
    add x69 -> x0, other arithmetic: 120 us -> none  [the longest x64 119 us: step(): total + scale[:, None] * jnp.exp(-decay[:, None] * times[None, :])]
    all_gather x4 -> x0, waiting for transfers between devices: 91.8 us -> none  [the longest x1 36.5 us: shards(): lax.all_gather(value_flat, 'seq', axis=0, tiled=True)]
    neg x128 -> x0, other arithmetic: 90.3 us -> none  [the longest x64 45.4 us: step(): -decay[:, None] * times[None, :]]
    all_gather x2 -> x0, blocking collectives: 65.2 us -> none  [the longest x1 32.7 us: shards(): lax.all_gather(lse, 'seq', axis=1, tiled=True)]
    mul x65 -> x0, other arithmetic: 45.4 us -> none  [the longest x64 44.8 us: step(): -scale * jnp.sum(fall * times[None, :], axis=1)]
  transfers between devices with their start and end apart: 25 -> 2, of which waited for: 16 -> 1; matrix products, arithmetic and copies ran while one was open for 23% -> 3% of each run, Pallas kernels for 0% -> 42%
where the time goes in v2:
time: 424 us; the launch traced here: 416 us
  Pallas kernels  340 us (80%)
  local copies, waits for them, and re-layouts  29.5 us (7%)
  waiting for transfers between devices  16 us (4%)
  between operations  14.8 us (3%)
  blocking collectives  12.5 us (3%)
    pallas_call x1, Pallas kernels, weight_sums(): pl.pallas_call(functools.partial(weight_sum_kernel, kinds), out_shape=[ja...  173 us
    pallas_call x4, Pallas kernels, call(): pl.pallas_call(run, out_shape=[jax.ShapeDtypeStruct(shape, kind) for shap...  166 us
    reduce_scatter x1, waiting for transfers between devices, shards_fast(): lax.psum_scatter(small[0:64].astype(BF), 'batch', scatter_dimension=0, ti...  16 us
    psum x1, blocking collectives, shards_fast(): rest = lax.psum(small[64:], 'batch')  12.5 us
  transfers between devices with their start and end apart: 2, of which 1 were waited for; matrix products, arithmetic and copies ran while one was open for 3% of the time, Pallas kernels for 42%

profile of v2, /device:TPU:0, one launch (start us, length us, event | category | flops | bytes accessed | tf_op | source)
XLA Modules:
  0.0 416.4 jit_solution(9416013684440314300)
XLA Ops:
  7.2 0.0 reduce-scatter.7.cloned.1.call-start
  7.2 1.3 broadcast_in_dim.22.refs_1_
  8.5 1.3 broadcast_in_dim.23.refs_5_.refs_3_
  9.8 1.3 broadcast_in_dim.24.refs_6_.refs_4_
  11.0 1.3 broadcast_in_dim.25.refs_7_.refs_3_
  12.3 1.3 reduce-window.9
  13.6 1.3 broadcast_in_dim.26.refs_2_
  14.9 1.4 constant_dynamic-slice_fusion
  16.3 71.3 %shard_map.376 = (bf16[128,768]{1,0:T(8,128)(2,1)}, f32[128,768]{1,0:T(8,128)}, f32[128,768]{1,0:T(8,128)}, f32[192,768]{1,0:T(8,128)}, f32[128,768]{1,0:T(8,128...) custom-call(bf16[1,128,768]{2,1,0:T(8,128)(2,1)} %refs_0_.3, ...), custom_call_target="tpu_custom_call" | custom-call | tf_op jit(solution)/shard_map/pallas_call | solution.py:1170
  87.6 41.6 %shard_map.377 = (bf16[1,128,768]{2,1,0:T(8,128)(2,1)}, bf16[128,768]{1,0:T(8,128)(2,1)}, bf16[128,3072]{1,0:T(8,128)(2,1)}, bf16[2,128,1536]{2,1,0:T(8,128)(2,1...) custom-call(f32[128,768]{1,0:T(8,128)} %get-tuple-element.67.refs_0_, ...), custom_call_target="tpu_custom_call" | custom-call | tf_op jit(solution)/shard_map/pallas_call | solution.py:1170
  129.2 32.8 %shard_map.378 = (f32[1,768]{1,0:T(1,128)}, f32[1,768]{1,0:T(1,128)}, f32[1,768]{1,0:T(1,128)}, bf16[128,768]{1,0:T(8,128)(2,1)}, bf16[2,128,1536]{2,1,0:T(8,128...) custom-call(f32[128,768]{1,0:T(8,128)} %get-tuple-element.67.refs_0_, ...), custom_call_target="tpu_custom_call" | custom-call | tf_op jit(solution)/shard_map/pallas_call | solution.py:1170
  162.1 0.8 fusion
  162.9 0.0 copy-start.11
  162.9 0.0 copy-start.12
  162.9 20.7 %shard_map.379 = (bf16[3,128,768]{2,1,0:T(8,128)(2,1)}, f32[64,768]{1,0:T(8,128)}, f32[1,768]{1,0:T(1,128)}, f32[1,128,768]{2,1,0:T(8,128)}) custom-call(bf16[1,128,768]{2,1,0:T(8,128)(2,1)} %refs_0_.3, f32[1,768]{1,0:T(1,128)} %broadcast_in_dim.22.refs_1_, f32[64,768]{1,0:T(8,128)} %refs_2_.3, f32[1,768]{1,0:T(1,128)} %broadcast_in_dim.23.refs_5_.refs_3_, ...), custom_call_target="tpu_custom_call" | custom-call | tf_op jit(solution)/shard_map/pallas_call | solution.py:1170
  183.6 0.0 copy-start.2
  183.6 0.0 copy-done.9
  183.6 1.8 concatenate.23
  185.5 1.2 copy.75
  186.6 0.0 reduce-scatter.7.cloned.1.call-update
  186.6 0.3 reduce-scatter.5.cloned.1.call-start
  186.9 0.0 copy-done.2
  187.0 0.3 copy.66
  187.3 0.2 copy.67
  187.4 0.1 maximum_bitcast_fusion.1
  187.5 0.0 copy-start.7
  187.5 0.8 copy.68
  188.3 1.4 reshape.120.refs_12_
  189.7 0.0 copy-done
  189.7 0.3 copy.63
  190.0 0.2 copy.64
  190.2 0.1 maximum_bitcast_fusion
  190.3 0.8 copy.65
  191.1 1.4 reshape.119.refs_5_
  192.5 173.3 %shard_map.380 = (f32[1152,128]{1,0:T(8,128)}, f32[576,128]{1,0:T(8,128)}, f32[1152,128]{1,0:T(8,128)}, f32[576,128]{1,0:T(8,128)}) custom-call(bf16[128,768]{1,0:T(8,128)(2,1)} %get-tuple-element.99.refs_0_, bf16[2,128,1536]{2,1,0:T(8,128)(2,1)} %get-tuple-element.100.refs_1_, bf16[128,768]{1,0:T(8,128)(2,1)} %bitcast.83, ...), custom_call_target="tpu_custom_call" | custom-call | tf_op jit(solution)/shard_map/pallas_call | solution.py:1389
  365.8 1.2 copy.69
  367.1 0.1 copy.96
  367.1 0.7 slice.71
  367.8 0.7 slice.76
  368.6 0.2 copy.72
  368.7 0.1 copy.93
  368.8 0.7 slice.79
  369.5 0.7 slice.80
  370.3 0.2 copy.74
  370.5 0.7 copy.91
  371.3 0.2 copy.73
  371.4 0.8 copy.92
  372.3 0.0 copy-start.4
  372.3 0.2 copy.71
  372.5 0.7 copy.94
  373.2 0.2 copy.70
  373.4 0.8 copy.95
  374.2 1.0 slice.69
  375.2 0.8 slice.72
  376.0 0.1 copy.77
  376.1 12.5 %psum.7 = f32[133,96]{1,0:T(8,128)S(1)} all-reduce(f32[133,96]{1,0:T(8,128)S(1)} %copy.77), channel_id=1, replica_groups=mesh['seq'=8,'batch'=4] {'batch'}, use_global_device_ids=true, to_apply=%region_2.3 | all-reduce | flops 12768 | bytes 102144 | tf_op jit(solution)/shard_map/psum | solution.py:1651
  388.6 0.6 fusion.3
  389.2 0.7 copy.78
  389.9 0.0 reduce-scatter.5.cloned.1.call-update
  389.9 0.5 slice_bitcast_fusion
  390.5 16.0 %reduce-scatter.5.cloned.1.call-done = bf16[16,96]{1,0:T(8,128)(2,1)} async-done(((bf16[64,96]{1,0:T(8,128)(2,1)}), bf16[16,96]{1,0:T(8,128)(2,1)}) %reduce-scatter.5.cloned.1.call-update) | async-done | bytes 3088 | tf_op jit(solution)/shard_map/reduce_scatter | solution.py:1650
  406.5 1.3 convert_element_type.4
  407.7 0.7 copy.100
  408.4 0.7 copy.101
  (22 shorter events, 0.1 us)
Async XLA Ops:
  7.2 367.0 %reduce-scatter.7.cloned.1.call-start = ((), (), s32[]{:S(2)}) async-start(), calls=%async_computation.3 | async-start | bytes 884736
  162.9 20.7 %copy-start.9 = (f32[1,768]{1,0:T(1,128)S(1)}, f32[1,768]{1,0:T(1,128)}, u32[]{:S(2)}) copy-start(f32[1,768]{1,0:T(1,128)} %get-tuple-element.98) | copy-start | bytes 9220
  162.9 20.7 %copy-start.10 = (f32[1,768]{1,0:T(1,128)S(1)}, f32[1,768]{1,0:T(1,128)}, u32[]{:S(2)}) copy-start(f32[1,768]{1,0:T(1,128)} %get-tuple-element.97) | copy-start | bytes 9220
  162.9 20.7 %copy-start.11 = (f32[1,768]{1,0:T(1,128)S(1)}, f32[1,768]{1,0:T(1,128)}, u32[]{:S(2)}) copy-start(f32[1,768]{1,0:T(1,128)} %get-tuple-element.96) | copy-start | bytes 9220
  162.9 20.7 %copy-start.12 = (f32[1,768]{1,0:T(1,128)S(1)}, f32[1,768]{1,0:T(1,128)}, u32[]{:S(2)}) copy-start(f32[1,768]{1,0:T(1,128)} %get-tuple-element.95) | copy-start | bytes 9220
  183.6 3.4 copy-start.2
  183.6 3.6 copy-start.8
  186.6 219.8 %reduce-scatter.5.cloned.1.call-start = ((), (), s32[]{:S(2)}) async-start(), calls=%async_computation.2 | async-start | bytes 20480 | tf_op jit(solution)/shard_map/reduce_scatter | solution.py:1650
  187.4 2.3 copy-start
  187.5 2.5 copy-start.7
  365.8 2.8 copy-start.5
  365.8 4.4 %copy-start.3 = (f32[1152,128]{1,0:T(8,128)S(1)}, f32[1152,128]{1,0:T(8,128)}, u32[]{:S(2)}) copy-start(f32[1152,128]{1,0:T(8,128)} %get-tuple-element.115) | copy-start | bytes 1769476
  369.5 2.7 copy-start.1
  372.2 35.5 %copy-start.6 = (bf16[1,128,768]{2,1,0:T(8,128)(2,1)S(1)}, bf16[1,128,768]{2,1,0:T(8,128)(2,1)}, u32[]{:S(2)}) copy-start(bf16[1,128,768]{2,1,0:T(8,128)(2,1)} %get-tuple-element.147) | copy-start | bytes 589828
  372.3 36.2 %copy-start.4 = (f32[1,128,768]{2,1,0:T(8,128)S(1)}, f32[1,128,768]{2,1,0:T(8,128)}, u32[]{:S(2)}) copy-start(f32[1,128,768]{2,1,0:T(8,128)} %get-tuple-element.148) | copy-start | bytes 1179652
Sparse Core Ops, SparseCore 0:
  186.8 62.8 reduce-scatter.6
  390.1 16.3 reduce-scatter.4

commit v3 on v2

--- a/solution.py
+++ b/solution.py
@@ -1,4 +1,3 @@
-import functools
 import math
 
 import jax
@@ -652,6 +651,15 @@
         self.send_sem, self.recv_sem = send_sem, recv_sem
         self.s = lax.axis_index("seq")
         self.b = lax.axis_index("batch")
+        self.y, self.c = self.b // 2, lax.rem(self.b, 2)
+        z, self.x = self.s // 2, lax.rem(self.s, 2)
+        self.high, self.low = z // 2, lax.rem(z, 2)
+        self.sibling = (self.s, 2 * self.y + flip(self.c))
+        self.by_y = (self.s, 2 * flip(self.y) + self.c)
+        self.by_both = (self.s, 2 * flip(self.y) + flip(self.c))
+        self.by_x = (2 * z + flip(self.x), self.b)
+        self.by_low = (2 * (2 * self.high + flip(self.low)) + self.x, self.b)
+        self.by_high = (2 * (2 * flip(self.high) + self.low) + self.x, self.b)
         self.used = 0
         self.waiting = []
 
@@ -665,15 +673,41 @@
         self.waiting.append(made)
         return made
 
-    def greet(self, others=()):
+    def send(self, source, target, other):
+        at = self.take(1)
+        copy = pltpu.make_async_remote_copy(
+            src_ref=source,
+            dst_ref=target,
+            send_sem=self.send_sem.at[at],
+            recv_sem=self.recv_sem.at[at],
+            device_id=other,
+            device_id_type=MESH,
+        )
+        copy.start()
+        self.waiting.append(copy)
+        return copy
+
+    def hello(self):
         barrier = pltpu.get_barrier_semaphore()
         for step in range(1, RANKS):
             pl.semaphore_signal(
                 barrier, inc=1, device_id=(lax.rem(self.s + step, RANKS), self.b), device_id_type=MESH
             )
-        for other in others:
+        for other in (self.sibling, self.by_y, self.by_both):
             pl.semaphore_signal(barrier, inc=1, device_id=other, device_id_type=MESH)
-        pl.semaphore_wait(barrier, RANKS - 1 + len(others))
+
+    def ready(self):
+        pl.semaphore_wait(pltpu.get_barrier_semaphore(), RANKS + 2)
+
+    def turn_of(self, step, y, c):
+        return (2 * y + flip(c), 2 * flip(y) + c, 2 * flip(y) + flip(c), 2 * y + c)[step]
+
+    def order(self):
+        owners = (self.sibling, self.by_y, self.by_both, None)
+        return [(self.turn_of(step, self.y, self.c), owners[step]) for step in range(4)]
+
+    def drop(self, copy):
+        self.waiting = [made for made in self.waiting if made is not copy]
 
     def finish(self):
         for made in self.waiting:
@@ -743,15 +777,25 @@
     return high, (value - high.astype(F32)).astype(BF)
 
 
-def transform(r, high, low, re_out, im_out):
+def transform(r, signal, re_out, im_out):
     @pl.loop(0, 4)
     def _(at):
         rows = pl.ds(pl.multiple_of(256 * at, 256), 256)
-        for main, rest, out, sign in ((r.cos_high, r.cos_low, re_out, 1.0), (r.sin_high, r.sin_low, im_out, -1.0)):
-            total = mm(main[rows, :], high) + mm(rest[rows, :], high)
-            if low is not None:
-                total = total + mm(main[rows, :], low)
-            out[rows, :] = sign * total
+        re_out[rows, :] = mm(r.cos_table[rows, :], signal)
+        im_out[rows, :] = -mm(r.sin_table[rows, :], signal)
+
+
+def transform_two(r, signal, re_out, im_out):
+    high, low = split(signal)
+    r.pack_re[:, 0:128] = high
+    r.pack_re[:, 128:256] = low
+
+    @pl.loop(0, 4)
+    def _(at):
+        rows = pl.ds(pl.multiple_of(256 * at, 256), 256)
+        re, im = mm(r.cos_table[rows, :], r.pack_re[...]), mm(r.sin_table[rows, :], r.pack_re[...])
+        re_out[rows, :] = re[:, 0:128] + re[:, 128:256]
+        im_out[rows, :] = -(im[:, 0:128] + im[:, 128:256])
 
 
 def inverse(r, re, im, out):
@@ -765,9 +809,8 @@
     @pl.loop(0, 4)
     def _(at):
         rows = pl.ds(pl.multiple_of(256 * at, 256), 256)
-        both = mm(r.cos_high[rows, :], r.pack_re[...]) - mm(r.sin_high[rows, :], r.pack_im[...])
-        rest = mm(r.cos_low[rows, :], r.pack_re[:, 0:128]) - mm(r.sin_low[rows, :], r.pack_im[:, 0:128])
-        out[rows, :] = ((both[:, 0:128] + both[:, 128:256] + rest) * (1.0 / SPAN)).astype(out.dtype)
+        both = mm(r.cos_table[rows, :], r.pack_re[...]) - mm(r.sin_table[rows, :], r.pack_im[...])
+        out[rows, :] = ((both[:, 0:128] + both[:, 128:256]) * (1.0 / SPAN)).astype(out.dtype)
 
 
 def modes(coef_ref, rate_ref, out_ref):
@@ -913,30 +956,288 @@
     r.qkv_grad[2, rows, :] = r.value_grad[rows, :].astype(BF)
 
 
-def load(r, sems, names):
-    copies = {}
-    for index, name in enumerate(names):
-        copies[name] = pltpu.make_async_copy(getattr(r, name + "_hbm"), getattr(r, name), sems.at[index])
-        copies[name].start()
-    return copies
-
-
-TABLES = ("cos_high", "sin_high", "cos_low", "sin_low")
+class Gather:
+    def __init__(self, net, source, target):
+        self.net, self.target = net, target
+        here = target(net.y, net.c)
+        self.first = net.send(source, here, net.sibling)
+        self.across = net.send(source, here, net.by_y)
+
+    def forward(self):
+        self.across.wait_recv()
+        landed = self.target(flip(self.net.y), self.net.c)
+        self.second = self.net.send(landed, landed, self.net.sibling)
+
+    def wait(self):
+        self.first.wait_recv()
+        self.second.wait_recv()
+
+    def free(self):
+        for copy in (self.first, self.across, self.second):
+            copy.wait_send()
+            self.net.drop(copy)
+
+
+class Locals:
+    def __init__(self, sems):
+        self.sems, self.used, self.waiting = sems, 0, []
+
+    def start(self, source, target):
+        copy = pltpu.make_async_copy(source, target, self.sems.at[self.used])
+        self.used += 1
+        copy.start()
+        return copy
+
+    def put(self, source, target):
+        self.waiting.append(self.start(source, target))
+
+    def finish(self):
+        for copy in self.waiting:
+            copy.wait()
+
+
+LAYER, PAIR = (0, 1)
+LENGTH = (1152, 576)
+
+
+class Sum:
+    def __init__(self, r, net, name, kind):
+        self.net, self.kind = net, kind
+        for part in ("right", "grads", "near_a", "near_b", "next_a", "next_b", "own", "third"):
+            setattr(self, part, getattr(r, name + "_" + part))
+        if kind == LAYER:
+            self.across = getattr(r, name + "_across")
+        self.half = LENGTH[kind] // 2
+        self.shared = []
+
+    def give(self, kept, step, columns, other):
+        own = self.right.at[rows_of(self.net.b), :]
+        if other is None:
+            own[...] = columns
+        else:
+            kept[step] = columns
+            self.shared.append(self.net.send(kept.at[step], own, other))
+
+    def share_pairs(self, pairs):
+        own = self.right.at[rows_of(self.net.b), :]
+        for index, other in self.net.order():
+            if other is None:
+                own[...] = pairs[index]
+            else:
+                self.shared.append(self.net.send(pairs.at[index], own, other))
+
+    def free(self, copies):
+        for copy in copies:
+            copy.wait_send()
+            self.net.drop(copy)
+
+    def free_rows(self):
+        self.free(self.shared[:3])
+
+    def free_columns(self):
+        self.free(self.shared[-3:])
+
+    def share_rows(self, turned):
+        net = self.net
+        own = pl.ds(pl.multiple_of(192 * net.b, 64), 192)
+        self.across[:, lanes_of(net.b)] = turned[own, :]
+        for index, other in self.net.order()[:3]:
+            rows = pl.ds(pl.multiple_of(192 * index, 64), 192)
+            self.shared.append(net.send(turned.at[rows, :], self.across.at[:, lanes_of(net.b)], other))
+
+    def wait_shared(self):
+        for copy in self.shared:
+            copy.wait_recv()
+
+    def place(self, product, tile):
+        for block in range(8):
+            at = pl.ds(pl.multiple_of(96 * tile, 16), 96)
+            self.grads[block % 2, (block // 2) % 2, block // 4, at, :] = product[96 * block : 96 * block + 96].astype(BF)
+
+    def product(self, left, second):
+        self.wait_shared()
+        if self.kind == LAYER:
+
+            @pl.loop(0, 3)
+            def _(chunk):
+                lanes = pl.ds(pl.multiple_of(256 * chunk, 256), 256)
+                product = mm(left[...], self.right[:, lanes])
+                self.place(product[:, 0:128], 2 * chunk)
+                self.place(product[:, 128:256], 2 * chunk + 1)
+
+            @pl.loop(0, 8)
+            def _(block):
+                lanes = pl.ds(pl.multiple_of(384 * block, 384), 384)
+                product = mm(self.across[...], second[:, lanes])
+                for tile in range(3):
+                    self.grads[
+                        lax.rem(block, 2), lax.rem(block // 2, 2), block // 4, 576 + 192 * tile : 768 + 192 * tile, :
+                    ] = product[:, 128 * tile : 128 * tile + 128].astype(BF)
+
+        else:
+
+            @pl.loop(0, 2)
+            def _(chunk):
+                lanes = pl.ds(pl.multiple_of(256 * chunk, 256), 256)
+                product = mm(left[...], self.right[:, lanes])
+                self.place(product[:, 0:128], 2 * chunk)
+                self.place(product[:, 128:256], 2 * chunk + 1)
+
+            right = self.right[:, 512:768]
+            first = lax.broadcasted_iota(jnp.int32, right.shape, 1) < 64
+            zero = jnp.zeros_like(right)
+            product = mm(left[...], jnp.where(first, right, zero)) + mm(second[...], jnp.where(first, zero, right))
+            self.place(product[:, 0:128], 4)
+            self.place(product[:, 128:256], 5)
+
+        net, half = self.net, self.half
+        self.moving = [
+            net.send(self.grads.at[flip(net.x), :, :, 0:half, :], self.near_a, net.by_x),
+            net.send(self.grads.at[:, flip(net.low), :, half:, :], self.near_b, net.by_low),
+        ]
+
+    def arrive(self):
+        for copy in self.moving:
+            copy.wait_recv()
+
+    def second(self):
+        net, half, grads = self.net, self.half, self.grads
+        self.arrive()
+
+        @pl.loop(0, 4)
+        def _(step):
+            one, two = step // 2, lax.rem(step, 2)
+            grads[net.x, one, two, 0:half, :] += self.near_a[one, two]
+            grads[one, net.low, two, half:, :] += self.near_b[one, two]
+
+        self.moving = [
+            net.send(grads.at[net.x, flip(net.low), :, 0:half, :], self.next_a, net.by_low),
+            net.send(grads.at[flip(net.x), net.low, :, half:, :], self.next_b, net.by_x),
+        ]
+
+    def last(self):
+        net, half, grads = self.net, self.half, self.grads
+        self.arrive()
+
+        @pl.loop(0, 2)
+        def _(step):
+            grads[net.x, net.low, step, 0:half, :] += self.next_a[step]
+            grads[net.x, net.low, step, half:, :] += self.next_b[step]
+
+        self.moving = [net.send(grads.at[net.x, net.low, flip(net.high)], self.third, net.by_high)]
+
+    def end(self, near):
+        net = self.net
+        near.put(self.grads.at[net.x, net.low, net.high], self.own)
+        self.arrive()
+
+
+def sum_scratch(name, kind):
+    length = LENGTH[kind]
+    half = length // 2
+    made = {
+        name + "_right": ((512, WIDE), BF),
+        name + "_grads": ((2, 2, 2, length, 128), BF),
+        name + "_near_a": ((2, 2, half, 128), BF),
+        name + "_near_b": ((2, 2, half, 128), BF),
+        name + "_next_a": ((2, half, 128), BF),
+        name + "_next_b": ((2, half, 128), BF),
+    }
+    if kind == LAYER:
+        made[name + "_across"] = ((192, 512), BF)
+    return made
+
+
+def pair_columns(wide, narrow, out):
+    first = lax.broadcasted_iota(jnp.int32, (ROWS, BLOCK), 1) < 64
+
+    def tile(at):
+        at = at % (3 * WIDE)
+        return wide[at // WIDE, :, at % WIDE : at % WIDE + BLOCK].astype(F32)
+
+    def turned(at):
+        return jnp.where(first, pltpu.roll(tile(at - BLOCK), 64, 1), pltpu.roll(tile(at), 64, 1))
+
+    def thin(at):
+        return narrow[:, at : at + BLOCK].astype(F32)
+
+    def thin_turned(at):
+        upper = pltpu.roll(thin(at), 64, 1)
+        return jnp.where(first, pltpu.roll(thin(at - BLOCK), 64, 1), upper) if at else upper
+
+    for block in range(4):
+        start = 576 * block
+        if block % 2 == 0:
+            for part in range(4):
+                out[block, :, BLOCK * part : BLOCK * part + BLOCK] = tile(start + BLOCK * part).astype(BF)
+            lower, upper, rest = tile(start + 512), thin_turned(192 * block), thin_turned(192 * block + BLOCK)
+        else:
+            for part in range(4):
+                out[block, :, BLOCK * part : BLOCK * part + BLOCK] = turned(start + 64 + BLOCK * part).astype(BF)
+            lower, upper, rest = turned(start + 576), thin(192 * block - 64), thin(192 * block + 64)
+        out[block, :, 512:640] = jnp.where(first, lower, upper).astype(BF)
+        out[block, :, 640:768] = rest.astype(BF)
+
+
+def turn(blocks, out):
+    for block in range(4):
+        out[:, BLOCK * block : BLOCK * block + BLOCK] = blocks[BLOCK * block : BLOCK * block + BLOCK, :].T
+
+
+TABLES = ("cos_table", "sin_table")
+KEPT = (
+    "qkv",
+    "lse",
+    "attended_full",
+    "bend_b",
+    "stream_b",
+    "response",
+    "query_a",
+    "shifted",
+    "value_a",
+    "key_ext",
+    "kernel_re",
+    "kernel_im",
+    "signal_re",
+    "signal_im",
+)
+LEFTS = ("normed_a", "gated", "normed_b", "active_b", "normed_c")
 
 
 def kernel_a(r):
     net = Net(r.send_sem, r.recv_sem)
-    wait = load(r, r.load_sem, ("mixer_in",) + TABLES + ("mixer_out", "up_first", "down_first", "project_in"))
+    near = Locals(r.local_sem)
+    net.hello()
+    wait = {}
+    for name in ("mixer_in",) + TABLES + ("mixer_out", "up_first", "down_first", "project_in"):
+        wait[name] = near.start(getattr(r, name + "_hbm"), getattr(r, name))
+    r.ends[0] = r.doc_lengths[0, 0]
+    r.ends[1] = r.ends[0] + r.doc_lengths[0, 1]
+    r.ends[2] = r.ends[1] + r.doc_lengths[0, 2]
+
+    def keep(*names):
+        for name in names:
+            near.put(getattr(r, name), getattr(r, name + "_kept"))
+
+    gathers = []
+
+    def gather(name):
+        all_of = getattr(r, name + "_all")
+        mine = getattr(r, name)
+        near.put(mine, all_of.at[rows_of(net.b), :])
+        gathers.append(Gather(net, mine, lambda y, c: all_of.at[rows_of(2 * y + c), :]))
+
     me = net.s
     stream = r.tokens[0].astype(F32)
     normal, _ = pieces(stream)
-    r.normed_a[...] = (normal * r.mixer_norm_gain[...]).astype(BF)
+    r.normed_a[...] = (normal * r.mixer_norm_gain[...][None]).astype(BF)
     wait["mixer_in"].wait()
     r.key_ext[64:192, :] = mm(r.normed_a[...], r.mixer_in[:, WIDE : 2 * WIDE])
     r.rim_out[...] = r.key_ext[128:192, :].astype(BF)
-    net.greet()
+    net.ready()
     rim = Beside(net, r.rim_out, r.rim_in, 1)
     rim.start()
+    gather("normed_a")
 
     @pl.when(me == 0)
     def _():
@@ -944,6 +1245,7 @@
 
     r.query_a[...] = mm(r.normed_a[...], r.mixer_in[:, 0:WIDE])
     r.value_a[...] = mm(r.normed_a[...], r.mixer_in[:, 2 * WIDE :])
+    keep("query_a", "value_a")
     rim.wait_recv()
     r.key_ext[0:64, :] = r.rim_in[...].astype(F32)
     shift_forward(r.key_ext, r.shift_taps, None, r.shifted)
@@ -951,16 +1253,20 @@
     go = net.spread(lambda block: r.product_low.at[:, lanes_of(block)], lambda rank: r.signal.at[rows_of(rank), :], True)
     go.start()
     go.own()
+    keep("key_ext", "shifted")
+    block = lanes_of(jnp.clip(me - 1, 0, OWNERS - 1))
+    r.coef[...] = r.mode_coef[:, block]
+    r.rate[...] = r.mode_rate[:, block]
     modes(r.coef, r.rate, r.mode_rows)
-    high, low = split(r.mode_rows[...])
     for name in TABLES:
         wait[name].wait()
-    transform(r, high, low, r.kernel_re, r.kernel_im)
+    transform_two(r, r.mode_rows[...], r.kernel_re, r.kernel_im)
     turned = r.kernel_re[...] * r.phase_cos[...] - r.kernel_im[...] * r.phase_sin[...]
     r.kernel_im[...] = r.kernel_im[...] * r.phase_cos[...] + r.kernel_re[...] * r.phase_sin[...]
     r.kernel_re[...] = turned
+    keep("kernel_re", "kernel_im")
     go.wait_recv()
-    transform(r, r.signal[...], None, r.signal_re, r.signal_im)
+    transform(r, r.signal[...], r.signal_re, r.signal_im)
     inverse(
         r,
         r.signal_re[...] * r.kernel_re[...] - r.signal_im[...] * r.kernel_im[...],
@@ -970,76 +1276,139 @@
     back = net.spread(lambda rank: r.conv.at[rows_of(rank), :], lambda block: r.conv_home.at[:, lanes_of(block)], False)
     back.start()
     back.own()
+    turned = r.signal_re[...] * r.phase_cos[...] - r.signal_im[...] * r.phase_sin[...]
+    r.signal_im[...] = -(r.signal_im[...] * r.phase_cos[...] + r.signal_re[...] * r.phase_sin[...])
+    r.signal_re[...] = turned
+    keep("signal_re", "signal_im")
     for name in ("mixer_out", "up_first", "down_first", "project_in"):
         wait[name].wait()
     back.wait_recv()
-    r.response[...] = r.conv_home[...].astype(F32) + r.skip_gain[...] * (r.shifted[...] * r.value_a[...])
+    r.response[...] = r.conv_home[...].astype(F32) + r.skip_gain[...][None] * (r.shifted[...] * r.value_a[...])
     r.gated[...] = (r.query_a[...] * r.response[...]).astype(BF)
+    gather("gated")
     stream_b = r.tokens[0].astype(F32) + mm(r.gated[...], r.mixer_out[...])
     r.stream_b[...] = stream_b
     normal, _ = pieces(stream_b)
-    r.normed_b[...] = (normal * r.gain_second[...]).astype(BF)
+    r.normed_b[...] = (normal * r.gain_second[...][None]).astype(BF)
+    gather("normed_b")
     r.stream_c[...] = stream_b
     for chunk in range(4):
         lanes = slice(WIDE * chunk, WIDE * chunk + WIDE)
-        raised = mm(r.normed_b[...], r.up_first[:, lanes])
-        r.raised_b[:, lanes] = raised
-        active = gelu_parts(raised)[0].astype(BF)
+        active, bend = gelu_parts(mm(r.normed_b[...], r.up_first[:, lanes]))
+        r.bend_b[:, lanes] = bend.astype(BF)
+        active = active.astype(BF)
         r.active_b[:, lanes] = active
         r.stream_c[...] += mm(active, r.down_first[lanes, :])
     normal, _ = pieces(r.stream_c[...])
-    r.normed_c[...] = (normal * r.attention_norm_gain[...]).astype(BF)
+    r.normed_c[...] = (normal * r.attention_norm_gain[...][None]).astype(BF)
     for index in range(3):
         r.mixed_c[index] = mm(r.normed_c[...], r.project_in[:, WIDE * index : WIDE * index + WIDE]).astype(BF)
     go = net.spread(lambda block: r.mixed_c.at[:, :, lanes_of(block)], lambda rank: r.qkv.at[:, rows_of(rank), :], True)
     go.start()
     go.own()
+    keep("response", "stream_b", "bend_b")
+    gather("active_b")
+    gather("normed_c")
+    for made in gathers[:3]:
+        made.forward()
     go.wait_recv()
+    keep("qkv")
     back = net.spread(lambda rank: r.attended_low.at[rows_of(rank), :], lambda block: r.attended.at[:, lanes_of(block)], False)
     for part in (3, 2, 1, 0):
         attention_forward(r, part)
         back.start(lambda rank, part=part: rank // 2 == part)
     back.own()
+    keep("lse", "attended_full")
+    for made in gathers[3:]:
+        made.forward()
     back.wait_recv()
+    for made in gathers:
+        made.wait()
     net.finish()
+    near.finish()
 
 
 def kernel_b(r):
     net = Net(r.send_sem, r.recv_sem)
-    wait = load(r, r.load_sem, ("project_out", "up_second", "down_second"))
+    near = Locals(r.local_sem)
+    net.hello()
+    wait = {}
+
+    def fetch(name, into=None):
+        wait[name] = near.start(getattr(r, name + "_hbm"), getattr(r, into or name))
+
+    for name, into in (("project_out", "out_weight"), ("up_second", "up"), ("down_second", "down")):
+        fetch(name, into)
+    for name in KEPT[:10]:
+        fetch(name)
+    fetch("project_in", "in_weight")
+    fetch("normed_c_all", "pair_one")
+    for name in TABLES:
+        fetch(name)
+    r.ends[0] = r.doc_lengths[0, 0]
+    r.ends[1] = r.ends[0] + r.doc_lengths[0, 1]
+    r.ends[2] = r.ends[1] + r.doc_lengths[0, 2]
+    sum_d, sum_c = Sum(r, net, "sum_d", LAYER), Sum(r, net, "sum_c", PAIR)
+    sum_b, sum_a = Sum(r, net, "sum_b", LAYER), Sum(r, net, "sum_a", PAIR)
+    own_rows = rows_of(net.b)
+
+    gain_d = r.gain_fourth[...][None]
     wait["project_out"].wait()
-    stream_d = r.stream_c[...] + mm(r.attended[...], r.project_out[...])
+    stream_d = r.stream_c[...] + mm(r.attended[...], r.out_weight[...])
     normal, inverse_d = pieces(stream_d)
-    r.normed_d[...] = (normal * r.gain_fourth[...]).astype(BF)
+    normed_d = (normal * gain_d).astype(BF)
+    r.layer_left[own_rows, :] = normed_d
     r.total[...] = stream_d
+    r.turned[...] = r.cotangent[0].T
+    r.pair_two[own_rows, :] = r.attended[...]
+    net.ready()
+    gather_att = Gather(net, r.pair_two.at[own_rows, :], lambda y, c: r.pair_two.at[rows_of(2 * y + c), :])
+    gather_d = Gather(net, r.layer_left.at[own_rows, :], lambda y, c: r.layer_left.at[rows_of(2 * y + c), :])
+    sum_d.share_rows(r.turned)
     wait["up_second"].wait()
     wait["down_second"].wait()
-    for chunk in range(4):
-        lanes = slice(WIDE * chunk, WIDE * chunk + WIDE)
-        raised = mm(r.normed_d[...], r.up_second[:, lanes])
+    gathers = []
+    for step, (index, other) in enumerate(net.order()):
+        lanes = pl.ds(pl.multiple_of(WIDE * index, WIDE), WIDE)
+        raised = mm(r.layer_left[own_rows, :], r.up[:, lanes])
         active, slope = gelu_parts(raised)
         active = active.astype(BF)
-        r.active_d[:, lanes] = active
-        r.total[...] += mm(active, r.down_second[lanes, :])
-        slope = (slope * mm_nt(r.cotangent[0], r.down_second[lanes, :])).astype(BF)
-        r.slope_d[chunk % 2, :, WIDE * (chunk // 2) : WIDE * (chunk // 2) + WIDE] = slope
-        back = mm_nt(slope, r.up_second[:, lanes])
-        if chunk == 0:
+        r.layer_second[own_rows, lanes] = active
+
+        def spot(y, c, step=step):
+            at = pl.ds(pl.multiple_of(WIDE * net.turn_of(step, y, c), WIDE), WIDE)
+            return r.layer_second.at[rows_of(2 * y + c), at]
+
+        gathers.append(Gather(net, spot(net.y, net.c), spot))
+        r.total[...] += mm(active, r.down[lanes, :])
+        slope = (slope * mm_nt(r.cotangent[0], r.down[lanes, :])).astype(BF)
+        sum_d.give(r.slopes, step, slope, other)
+        back = mm_nt(slope, r.up[:, lanes])
+        if step == 0:
             r.grad_d[...] = back
         else:
             r.grad_d[...] += back
-    r.block_out[0] = r.total[...].astype(BF)
-    grad, r.gain_four[...] = pieces_back(r.grad_d[...], normal, inverse_d, r.gain_fourth[...])
+    grad, gain_four = pieces_back(r.grad_d[...], normal, inverse_d, gain_d)
     grad = r.cotangent[0].astype(F32) + grad
     r.grad_d[...] = grad
     r.grad_d_low[...] = grad.astype(BF)
-    r.att_grad_home[...] = mm_nt(r.grad_d_low[...], r.project_out[...]).astype(BF)
-    net.greet()
+    r.att_grad_home[...] = mm_nt(r.grad_d_low[...], r.out_weight[...]).astype(BF)
     go = net.spread(lambda block: r.att_grad_home.at[:, lanes_of(block)], lambda rank: r.att_grad.at[rows_of(rank), :], True)
     go.start()
     go.own()
+    fetch("up_first", "up")
+    fetch("down_first", "down")
+    fetch("mixer_out", "out_weight")
+    r.block_out[0] = r.total[...].astype(BF)
+
     r.key_grad[...] = jnp.zeros_like(r.key_grad)
     r.value_grad[...] = jnp.zeros_like(r.value_grad)
+    gather_att.forward()
+    gather_d.forward()
+    gathers[0].forward()
+    gathers[1].forward()
+    for name in ("qkv", "lse", "attended_full"):
+        wait[name].wait()
     go.wait_recv()
     back = net.spread(
         lambda rank: r.qkv_grad.at[:, rows_of(rank), :], lambda block: r.mixed_grad_c.at[:, :, lanes_of(block)], False
@@ -1048,60 +1417,89 @@
         attention_back(r, part)
         back.start(lambda rank, part=part: rank // 2 == part)
     back.own()
-    back.wait_recv()
-    net.finish()
-
-
-def kernel_c(r):
-    net = Net(r.send_sem, r.recv_sem)
-    wait = load(r, r.load_sem, ("project_in", "up_first", "down_first", "mixer_out") + TABLES)
+    for name, into in (
+        ("kernel_re", "lse"),
+        ("kernel_im", "attended_full"),
+        ("signal_re", "query_grad"),
+        ("signal_im", "key_grad"),
+    ):
+        fetch(name, into)
+    gathers[2].forward()
+    gathers[3].forward()
+    gather_d.wait()
+    turn(r.layer_left, r.turned_one)
+    for made in gathers:
+        made.wait()
+    sum_d.product(r.turned_one, r.layer_second)
+    for made in [gather_d] + gathers:
+        made.free()
+    fetch("normed_b_all", "layer_left")
+    fetch("active_b_all", "layer_second")
+
     normal, inverse_c = pieces(r.stream_c[...])
     wait["project_in"].wait()
-    grad = mm_nt(r.mixed_grad_c[0], r.project_in[:, 0:WIDE])
+    back.wait_recv()
+    grad = mm_nt(r.mixed_grad_c[0], r.in_weight[:, 0:WIDE])
     for index in range(1, 3):
-        grad = grad + mm_nt(r.mixed_grad_c[index], r.project_in[:, WIDE * index : WIDE * index + WIDE])
-    grad, r.gain_three[...] = pieces_back(grad, normal, inverse_c, r.attention_norm_gain[...])
+        grad = grad + mm_nt(r.mixed_grad_c[index], r.in_weight[:, WIDE * index : WIDE * index + WIDE])
+    fetch("mixer_in", "in_weight")
+    grad, gain_three = pieces_back(grad, normal, inverse_c, r.attention_norm_gain[...][None])
     grad = grad + r.grad_d[...]
-    r.grad_c[...] = grad
+    r.total[...] = grad
     r.grad_c_low[...] = grad.astype(BF)
+    sum_d.free_rows()
+    r.turned[...] = r.grad_c_low[...].T
+    sum_b.share_rows(r.turned)
+    sum_d.free_columns()
     wait["up_first"].wait()
     wait["down_first"].wait()
-    for chunk in range(4):
-        lanes = slice(WIDE * chunk, WIDE * chunk + WIDE)
-        slope = gelu_parts(r.raised_b[:, lanes])[1]
-        slope = (slope * mm_nt(r.grad_c_low[...], r.down_first[lanes, :])).astype(BF)
-        r.slope_b[chunk % 2, :, WIDE * (chunk // 2) : WIDE * (chunk // 2) + WIDE] = slope
-        back = mm_nt(slope, r.up_first[:, lanes])
-        if chunk == 0:
-            r.grad_b[...] = back
+    wait["bend_b"].wait()
+    for step, (index, other) in enumerate(net.order()):
+        lanes = pl.ds(pl.multiple_of(WIDE * index, WIDE), WIDE)
+        slope = (r.bend_b[:, lanes].astype(F32) * mm_nt(r.grad_c_low[...], r.down[lanes, :])).astype(BF)
+        sum_b.give(r.slopes, step, slope, other)
+        part = mm_nt(slope, r.up[:, lanes])
+        if step == 0:
+            r.grad_b[...] = part
         else:
-            r.grad_b[...] += back
+            r.grad_b[...] += part
+    for name in ("stream_b", "response", "query_a", "shifted", "value_a", "key_ext", "mixer_out"):
+        wait[name].wait()
     normal, inverse_b = pieces(r.stream_b[...])
-    grad, r.gain_two[...] = pieces_back(r.grad_b[...], normal, inverse_b, r.gain_second[...])
-    grad = grad + r.grad_c[...]
+    grad, gain_two = pieces_back(r.grad_b[...], normal, inverse_b, r.gain_second[...][None])
+    grad = grad + r.total[...]
     r.grad_b[...] = grad
     r.grad_b_low[...] = grad.astype(BF)
-    wait["mixer_out"].wait()
-    gated_grad = mm_nt(r.grad_b_low[...], r.mixer_out[...])
-    r.query_grad_a[...] = (gated_grad * r.response[...]).astype(BF)
+    gated_grad = mm_nt(r.grad_b_low[...], r.out_weight[...])
+    r.mixed_grad_a[0] = (gated_grad * r.response[...]).astype(BF)
     response_grad = gated_grad * r.query_a[...]
     r.response_grad[...] = response_grad
     r.response_grad_low[...] = response_grad.astype(BF)
-    net.greet()
     go = net.spread(
         lambda block: r.response_grad_low.at[:, lanes_of(block)], lambda rank: r.conv_grad.at[rows_of(rank), :], True
     )
     go.start()
     go.own()
-    r.skip_part[...] = jnp.sum(response_grad * (r.shifted[...] * r.value_a[...]), axis=0, keepdims=True)
-    for name in TABLES:
+    skip_part = jnp.sum(response_grad * (r.shifted[...] * r.value_a[...]), axis=0, keepdims=True)
+    pair_columns(r.mixed_grad_c, r.grad_d_low, r.pairs)
+    sum_c.share_pairs(r.pairs)
+    wait["normed_c_all"].wait()
+    turn(r.pair_one, r.turned_one)
+    gather_att.wait()
+    turn(r.pair_two, r.turned_two)
+    gather_att.free()
+    fetch("normed_a_all", "pair_one")
+    fetch("gated_all", "pair_two")
+
+    for name in TABLES + ("kernel_re", "kernel_im", "signal_re", "signal_im"):
         wait[name].wait()
+    kernel_re, kernel_im, signal_re, signal_im = r.lse, r.attended_full, r.query_grad, r.key_grad
     go.wait_recv()
-    transform(r, r.conv_grad[...], None, r.grad_re, r.grad_im)
+    transform(r, r.conv_grad[...], r.grad_re, r.grad_im)
     inverse(
         r,
-        r.grad_re[...] * r.kernel_re[...] + r.grad_im[...] * r.kernel_im[...],
-        r.grad_im[...] * r.kernel_re[...] - r.grad_re[...] * r.kernel_im[...],
+        r.grad_re[...] * kernel_re[...] + r.grad_im[...] * kernel_im[...],
+        r.grad_im[...] * kernel_re[...] - r.grad_re[...] * kernel_im[...],
         r.signal_grad,
     )
     back = net.spread(
@@ -1109,56 +1507,155 @@
     )
     back.start()
     back.own()
-    re = r.grad_re[...] * r.signal_re[...] + r.grad_im[...] * r.signal_im[...]
-    im = r.grad_im[...] * r.signal_re[...] - r.grad_re[...] * r.signal_im[...]
-    inverse(
-        r,
-        re * r.phase_cos[...] + im * r.phase_sin[...],
-        im * r.phase_cos[...] - re * r.phase_sin[...],
-        r.kernel_grad,
-    )
-    modes_back(r.coef, r.rate, r.kernel_grad, r.coef_part, r.rate_part)
+    sum_d.second()
+    sum_c.product(r.turned_one, r.turned_two)
     back.wait_recv()
-    net.finish()
-
-
-def kernel_d(r):
-    net = Net(r.send_sem, r.recv_sem)
-    wait = load(r, r.load_sem, ("mixer_in",))
-    signal_grad = r.signal_grad_home[...].astype(F32) + r.skip_gain[...] * r.response_grad[...]
+
+    signal_grad = r.signal_grad_home[...].astype(F32) + r.skip_gain[...][None] * r.response_grad[...]
     r.grad_ext[0:ROWS, :] = signal_grad * r.value_a[...]
     r.rim_out[...] = r.grad_ext[0:64, :].astype(BF)
-    net.greet()
     rim = Beside(net, r.rim_out, r.rim_in, -1)
     rim.start()
-    r.mixed_grad_a[0] = r.query_grad_a[...]
     r.mixed_grad_a[2] = (signal_grad * r.shifted[...]).astype(BF)
 
     @pl.when(net.s == RANKS - 1)
     def _():
         r.rim_in[...] = jnp.zeros_like(r.rim_in)
 
+    wait["normed_b_all"].wait()
+    turn(r.layer_left, r.turned_one)
+    wait["active_b_all"].wait()
+    sum_b.product(r.turned_one, r.layer_second)
     rim.wait_recv()
     r.grad_ext[ROWS:192, :] = r.rim_in[...].astype(F32)
-    shift_back(r.grad_ext, r.key_ext, r.shift_taps, r.key_grad_a, r.taps_part)
-    r.mixed_grad_a[1] = r.key_grad_a[...].astype(BF)
+    shift_back(r.grad_ext, r.key_ext, r.shift_taps, r.total, r.taps)
+    r.mixed_grad_a[1] = r.total[...].astype(BF)
+    sum_c.free_columns()
+    pair_columns(r.mixed_grad_a, r.grad_b_low, r.pairs)
+    sum_a.share_pairs(r.pairs)
     wait["mixer_in"].wait()
-    grad = mm_nt(r.mixed_grad_a[0], r.mixer_in[:, 0:WIDE])
+    grad = mm_nt(r.mixed_grad_a[0], r.in_weight[:, 0:WIDE])
     for index in range(1, 3):
-        grad = grad + mm_nt(r.mixed_grad_a[index], r.mixer_in[:, WIDE * index : WIDE * index + WIDE])
+        grad = grad + mm_nt(r.mixed_grad_a[index], r.in_weight[:, WIDE * index : WIDE * index + WIDE])
     normal, inverse_a = pieces(r.tokens[0].astype(F32))
-    grad, r.gain_one[...] = pieces_back(grad, normal, inverse_a, r.mixer_norm_gain[...])
+    grad, gain_one = pieces_back(grad, normal, inverse_a, r.mixer_norm_gain[...][None])
     r.token_grad[0] = r.grad_b[...] + grad
+
+    gains = jnp.concatenate([gain_one, skip_part, gain_two, gain_three, gain_four, jnp.zeros((3, WIDE), F32)], axis=0)
+    for block in range(4):
+        r.small[block // 2, block % 2, 0:16, :] = r.taps[16 * block : 16 * block + 16, :]
+        r.small[block // 2, block % 2, 16:24, :] = gains
+    swap = net.send(r.small.at[:, flip(net.c)], r.small_c, net.sibling)
+    wait["normed_a_all"].wait()
+    turn(r.pair_one, r.turned_one)
+    wait["gated_all"].wait()
+    turn(r.pair_two, r.turned_two)
+    sum_a.product(r.turned_one, r.turned_two)
+    swap.wait_recv()
+    r.small[:, net.c] += r.small_c[...]
+    swap = net.send(r.small.at[flip(net.y), net.c], r.small_swap.at[0], net.by_y)
+    sum_d.last()
+    sum_c.second()
+    swap.wait_recv()
+    r.small_sum[0] = r.small[net.y, net.c] + r.small_swap[0]
+    swap = net.send(r.small_sum.at[0], r.small_swap.at[1], net.by_x)
+
+    re = r.grad_re[...] * signal_re[...] - r.grad_im[...] * signal_im[...]
+    im = r.grad_re[...] * signal_im[...] + r.grad_im[...] * signal_re[...]
+    inverse(r, re, im, r.value_grad)
+    block = lanes_of(jnp.clip(net.s - 1, 0, OWNERS - 1))
+    r.coef[...] = r.mode_coef[:, block]
+    r.rate[...] = r.mode_rate[:, block]
+    modes_back(r.coef, r.rate, r.value_grad, r.mode_part.at[0, 0:64], r.mode_part.at[0, 64:128])
+    mode = net.send(r.mode_part.at[0], r.mode_swap.at[0], net.sibling)
+    sum_b.second()
+    mode.wait_recv()
+    r.mode_part[1] = r.mode_part[0] + r.mode_swap[0]
+    mode = net.send(r.mode_part.at[1], r.mode_swap.at[1], net.by_y)
+    swap.wait_recv()
+    r.small_sum[1] = r.small_sum[0] + r.small_swap[1]
+    swap = net.send(r.small_sum.at[1], r.small_swap.at[2], net.by_low)
+    sum_d.end(near)
+    sum_c.last()
+    sum_a.second()
+    mode.wait_recv()
+    r.mode_part[2] = r.mode_part[1] + r.mode_swap[1]
+    back = net.spread(lambda rank: r.mode_part.at[2], lambda block: r.mode_home.at[:, lanes_of(block)], False)
+    back.start()
+    back.own()
+    swap.wait_recv()
+    r.small_sum[2] = r.small_sum[1] + r.small_swap[2]
+    swap = net.send(r.small_sum.at[2], r.small_swap.at[3], net.by_high)
+    sum_b.last()
+    sum_a.last()
+    sum_c.end(near)
+    turn_back = lax.rem(WIDE - 96 * net.s, WIDE)
+    back.wait_recv()
+    r.mode_out[...] = pltpu.roll(r.mode_home[...], turn_back, 1)[:, 0:128]
+    swap.wait_recv()
+    r.small_out[...] = pltpu.roll(r.small_sum[2] + r.small_swap[3], turn_back, 1)[:, 0:128]
+    sum_b.end(near)
+    sum_a.end(near)
     net.finish()
+    near.finish()
+
+
+def kernel_z(*refs):
+    block_in, token_in, mode, small = refs[:4]
+    sums = refs[4:12]
+    (
+        block_out,
+        token_grad,
+        gain_one,
+        mixer_in,
+        taps,
+        coef,
+        rate,
+        skip,
+        mixer_out,
+        gain_two,
+        up_first,
+        down_first,
+        gain_three,
+        project_in,
+        project_out,
+        gain_four,
+        up_second,
+        down_second,
+    ) = refs[12:]
+    block_out[...] = block_in[...]
+    token_grad[...] = token_in[...]
+    taps[...] = small[0:16, 0:96]
+    for at, out in enumerate((gain_one, skip, gain_two, gain_three, gain_four)):
+        out[...] = small[16 + at, 0:96]
+    coef[...] = mode[0:64, 0:96]
+    rate[...] = mode[64:128, 0:96]
+
+    def block(index, first, count):
+        rows = slice(first, first + count)
+        return sums[2 * index][rows, :].astype(F32) + sums[2 * index + 1][rows, :].astype(F32)
+
+    for index, up, down in ((0, up_second, down_second), (2, up_first, down_first)):
+        for tile in range(6):
+            up[:, 128 * tile : 128 * tile + 128] = block(index, 96 * tile, 96)
+        for tile in range(3):
+            down[128 * tile : 128 * tile + 128, :] = block(index, 576 + 192 * tile, 192).T
+    for index, wide, narrow in ((1, project_in, project_out), (3, mixer_in, mixer_out)):
+        for tile in range(4):
+            wide[:, 128 * tile : 128 * tile + 128] = block(index, 96 * tile, 96)
+        mixed = block(index, 384, 96)
+        wide[:, 512:576] = mixed[:, 0:64]
+        narrow[:, 0:64] = mixed[:, 64:128]
+        narrow[:, 64:192] = block(index, 480, 96)
 
 
 class Refs:
     pass
 
 
-def call(body, identity, inputs, hbm, smem, outs, scratch, copies, loads):
-    names = list(inputs) + [name + "_hbm" for name in hbm] + list(smem) + list(outs) + list(scratch) + list(hbm)
-    names += ["send_sem", "recv_sem", "load_sem"]
+def call(body, identity, inputs, hbm, smem, outs, hbm_outs, scratch, semaphores):
+    names = list(inputs) + [name + "_hbm" for name in hbm] + list(smem) + list(outs) + list(hbm_outs) + list(scratch)
+    names += ["ends", "send_sem", "recv_sem", "local_sem"]
 
     def run(*refs):
         r = Refs()
@@ -1169,249 +1666,34 @@
     vmem = pl.BlockSpec(memory_space=pltpu.VMEM)
     results = pl.pallas_call(
         run,
-        out_shape=[jax.ShapeDtypeStruct(shape, kind) for shape, kind in outs.values()],
+        out_shape=[jax.ShapeDtypeStruct(shape, kind) for shape, kind in (*outs.values(), *hbm_outs.values())],
         in_specs=[vmem] * len(inputs)
         + [pl.BlockSpec(memory_space=pl.ANY)] * len(hbm)
         + [pl.BlockSpec(memory_space=pltpu.SMEM)] * len(smem),
-        out_specs=[vmem] * len(outs),
+        out_specs=[vmem] * len(outs) + [pl.BlockSpec(memory_space=pl.ANY)] * len(hbm_outs),
         scratch_shapes=[pltpu.VMEM(shape, kind) for shape, kind in scratch.values()]
-        + [pltpu.VMEM(array.shape, array.dtype) for array in hbm.values()]
-        + [pltpu.SemaphoreType.DMA((copies,)), pltpu.SemaphoreType.DMA((copies,)), pltpu.SemaphoreType.DMA((loads,))],
+        + [pltpu.SMEM((3,), jnp.int32)]
+        + [pltpu.SemaphoreType.DMA((semaphores[0],)), pltpu.SemaphoreType.DMA((semaphores[0],))]
+        + [pltpu.SemaphoreType.DMA((semaphores[1],))],
         compiler_params=pltpu.CompilerParams(
-            collective_id=identity, has_side_effects=True, vmem_limit_bytes=60 * 2**20
+            collective_id=identity, has_side_effects=True, vmem_limit_bytes=VMEM_BYTES
         ),
     )(*inputs.values(), *hbm.values(), *smem.values())
-    return dict(zip(outs, results))
+    return dict(zip((*outs, *hbm_outs), results))
+
+
+VMEM_BYTES = 66_900_000
 
 
 def odd_tables():
     odd = 2 * np.arange(SPAN, dtype=np.int64) + 1
     angle = (np.outer(odd, odd) % (8 * SPAN)) * (math.pi / (4 * SPAN))
-    tables = {}
-    for name, table in (("cos", np.cos(angle)), ("sin", np.sin(angle))):
-        high = table.astype(ml_dtypes.bfloat16)
-        tables[name + "_high"] = jnp.asarray(high)
-        tables[name + "_low"] = jnp.asarray((table - high.astype(np.float64)).astype(ml_dtypes.bfloat16))
     phase = (odd * (math.pi / (4 * SPAN)))[:, None] * np.ones((1, BLOCK))
+    tables = {
+        "cos_table": jnp.asarray(np.cos(angle).astype(ml_dtypes.bfloat16)),
+        "sin_table": jnp.asarray(np.sin(angle).astype(ml_dtypes.bfloat16)),
+    }
     return tables, jnp.asarray(np.cos(phase), F32), jnp.asarray(np.sin(phase), F32)
-
-
-LAYER, PAIR = (0, 1)
-GIVEN = (4, 3)
-OWN = (5, 3)
-
-
-def weight_sum_kernel(kinds, *refs):
-    refs = list(refs)
-    given = [[refs.pop(0) for _ in range(GIVEN[kind])] for kind in kinds]
-    outs = [refs.pop(0) for _ in kinds]
-    own_of = [[refs.pop(0) for _ in range(OWN[kind])] for kind in kinds]
-    sums_of = [[refs.pop(0) for _ in range(7)] for kind in kinds]
-    send_sem, recv_sem = refs
-    s = lax.axis_index("seq")
-    b = lax.axis_index("batch")
-    z, x = s // 2, lax.rem(s, 2)
-    y, c = b // 2, lax.rem(b, 2)
-    zh, zl = z // 2, lax.rem(z, 2)
-    sibling = (s, 2 * y + flip(c))
-    by_x = (2 * z + flip(x), b)
-    by_y = (s, 2 * flip(y) + c)
-    by_l = (2 * (2 * zh + flip(zl)) + x, b)
-    by_h = (2 * (2 * flip(zh) + zl) + x, b)
-    barrier = pltpu.get_barrier_semaphore()
-    for other in (sibling, by_x, by_y, by_l, by_h):
-        pl.semaphore_signal(barrier, inc=1, device_id=other, device_id_type=MESH)
-    pl.semaphore_wait(barrier, 5)
-    started = []
-
-    def send(source, target, other):
-        at = len(started)
-        copy = pltpu.make_async_remote_copy(
-            src_ref=source,
-            dst_ref=target,
-            send_sem=send_sem.at[at],
-            recv_sem=recv_sem.at[at],
-            device_id=other,
-            device_id_type=MESH,
-        )
-        copy.start()
-        started.append(copy)
-        return copy
-
-    shared = []
-    for kind, inputs, own in zip(kinds, given, own_of):
-        mine = []
-        own[0][:, 0:128] = inputs[0][...].T
-        mine.append(send(own[0].at[:, 0:128], own[0].at[:, 128:256], sibling))
-        own[1][0:128, :] = inputs[1][c]
-        mine.append(send(inputs[1].at[flip(c)], own[1].at[128:256, :], sibling))
-        if kind == LAYER:
-            own[3][...] = inputs[2][...].T
-            for at in range(2):
-                rows = pl.ds(pl.multiple_of(192 * (2 * at + c), 64), 192)
-                own[2][192 * at : 192 * at + 192, 0:128] = own[3][rows, :]
-                rows = pl.ds(pl.multiple_of(192 * (2 * at + flip(c)), 64), 192)
-                mine.append(send(own[3].at[rows, :], own[2].at[192 * at : 192 * at + 192, 128:256], sibling))
-            own[4][0:128, :] = inputs[3][...]
-            mine.append(send(inputs[3], own[4].at[128:256, :], sibling))
-        else:
-            own[2][:, 0:128] = inputs[2][...].T
-            mine.append(send(own[2].at[:, 0:128], own[2].at[:, 128:256], sibling))
-        shared.append(mine)
-
-    stages = []
-    for kind, own, sums, mine in zip(kinds, own_of, sums_of, shared):
-        for copy in mine:
-            copy.wait_recv()
-        grads, near_a, near_b, next_a, next_b, third, fourth = sums
-        half = grads.shape[4] // 2
-
-        def place(product, at, tile):
-            for block in range(8):
-                grads[block % 2, at, block // 4, (block // 2) % 2, pl.ds(pl.multiple_of(96 * tile, 16), 96), :] = product[
-                    96 * block : 96 * block + 96
-                ].astype(BF)
-
-        if kind == LAYER:
-
-            @pl.loop(0, 6)
-            def _(step):
-                at, chunk = step // 3, lax.rem(step, 3)
-                lanes = pl.ds(pl.multiple_of(256 * step, 256), 256)
-                product = jnp.dot(own[0][...], own[1][:, lanes], preferred_element_type=F32)
-                place(product[:, 0:128], at, 2 * chunk)
-                place(product[:, 128:256], at, 2 * chunk + 1)
-
-            @pl.loop(0, 8)
-            def _(block):
-                lanes = pl.ds(pl.multiple_of(384 * block, 384), 384)
-                product = jnp.dot(own[2][...], own[4][:, lanes], preferred_element_type=F32)
-                for at in range(2):
-                    for tile in range(3):
-                        grads[
-                            lax.rem(block, 2), at, block // 4, lax.rem(block // 2, 2), 576 + 192 * tile : 768 + 192 * tile, :
-                        ] = product[192 * at : 192 * at + 192, 128 * tile : 128 * tile + 128].astype(BF)
-
-        else:
-
-            @pl.loop(0, 2)
-            def _(at):
-                for chunk in range(3):
-                    lanes = pl.ds(pl.multiple_of(768 * at + 256 * chunk, 256), 256)
-                    right = own[1][:, lanes]
-                    if chunk < 2:
-                        product = jnp.dot(own[0][...], right, preferred_element_type=F32)
-                    else:
-                        first = lax.broadcasted_iota(jnp.int32, right.shape, 1) < 64
-                        zero = jnp.zeros_like(right)
-                        product = jnp.dot(own[0][...], jnp.where(first, right, zero), preferred_element_type=F32)
-                        product += jnp.dot(own[2][...], jnp.where(first, zero, right), preferred_element_type=F32)
-                    place(product[:, 0:128], at, 2 * chunk)
-                    place(product[:, 128:256], at, 2 * chunk + 1)
-
-        stages.append(
-            [
-                send(grads.at[flip(x), :, :, :, 0:half, :], near_a, by_x),
-                send(grads.at[:, flip(y), :, :, half:, :], near_b, by_y),
-            ]
-        )
-
-    for index, sums in enumerate(sums_of):
-        grads, near_a, near_b, next_a, next_b, third, fourth = sums
-        half = grads.shape[4] // 2
-        for copy in stages[index]:
-            copy.wait_recv()
-
-        @pl.loop(0, 8)
-        def _(step):
-            high, mid, low = step // 4, lax.rem(step // 2, 2), lax.rem(step, 2)
-            grads[x, high, mid, low, 0:half, :] += near_a[high, mid, low]
-            grads[high, y, mid, low, half:, :] += near_b[high, mid, low]
-
-        stages[index] = [
-            send(grads.at[x, flip(y), :, :, 0:half, :], next_a, by_y),
-            send(grads.at[flip(x), y, :, :, half:, :], next_b, by_x),
-        ]
-    for index, sums in enumerate(sums_of):
-        grads, near_a, near_b, next_a, next_b, third, fourth = sums
-        half = grads.shape[4] // 2
-        for copy in stages[index]:
-            copy.wait_recv()
-
-        @pl.loop(0, 4)
-        def _(step):
-            mid, low = step // 2, lax.rem(step, 2)
-            grads[x, y, mid, low, 0:half, :] += next_a[mid, low]
-            grads[x, y, mid, low, half:, :] += next_b[mid, low]
-
-        stages[index] = [send(grads.at[x, y, :, flip(zl), :, :], third, by_l)]
-    for index, sums in enumerate(sums_of):
-        grads, near_a, near_b, next_a, next_b, third, fourth = sums
-        for copy in stages[index]:
-            copy.wait_recv()
-
-        @pl.loop(0, 2)
-        def _(mid):
-            grads[x, y, mid, zl] += third[mid]
-
-        stages[index] = [send(grads.at[x, y, flip(zh), zl], fourth, by_h)]
-    for index, sums in enumerate(sums_of):
-        grads, near_a, near_b, next_a, next_b, third, fourth = sums
-        for copy in stages[index]:
-            copy.wait_recv()
-        outs[index][...] = grads[x, y, zh, zl].astype(F32) + fourth[...].astype(F32)
-    for copy in started:
-        copy.wait_send()
-
-
-def weight_sums(kinds, groups, identity):
-    lengths = [1152 if kind == LAYER else 576 for kind in kinds]
-    own, sums = [], []
-    for kind, length in zip(kinds, lengths):
-        own += [pltpu.VMEM((768, 256), BF), pltpu.VMEM((256, 1536), BF)]
-        if kind == LAYER:
-            own += [pltpu.VMEM((384, 256), BF), pltpu.VMEM((768, 128), BF), pltpu.VMEM((256, 3072), BF)]
-        else:
-            own += [pltpu.VMEM((768, 256), BF)]
-        half = length // 2
-        sums += [
-            pltpu.VMEM((2, 2, 2, 2, length, 128), BF),
-            pltpu.VMEM((2, 2, 2, half, 128), BF),
-            pltpu.VMEM((2, 2, 2, half, 128), BF),
-            pltpu.VMEM((2, 2, half, 128), BF),
-            pltpu.VMEM((2, 2, half, 128), BF),
-            pltpu.VMEM((2, length, 128), BF),
-            pltpu.VMEM((length, 128), BF),
-        ]
-    copies = sum(GIVEN[kind] + (7 if kind == LAYER else 6) for kind in kinds)
-    flat = [array for group in groups for array in group]
-    vmem = pl.BlockSpec(memory_space=pltpu.VMEM)
-    return pl.pallas_call(
-        functools.partial(weight_sum_kernel, kinds),
-        out_shape=[jax.ShapeDtypeStruct((length, 128), F32) for length in lengths],
-        in_specs=[vmem] * len(flat),
-        out_specs=[vmem] * len(kinds),
-        scratch_shapes=own + sums + [pltpu.SemaphoreType.DMA((copies,)), pltpu.SemaphoreType.DMA((copies,))],
-        compiler_params=pltpu.CompilerParams(
-            collective_id=identity, has_side_effects=True, vmem_limit_bytes=60 * 2**20
-        ),
-    )(*flat)
-
-
-def pair_columns(wide, narrow):
-    parts = jnp.concatenate([wide.reshape(128, 4, 576), narrow.reshape(128, 4, 192)], axis=2)
-    return parts.reshape(128, 2, 2, 768).transpose(2, 0, 1, 3).reshape(2, 128, 1536)
-
-
-def untile_layer(block):
-    up = block[:576].reshape(6, 96, 128).transpose(1, 0, 2).reshape(96, 768)
-    down = block[576:].reshape(3, 192, 128).transpose(0, 2, 1).reshape(384, 192)
-    return up, down
-
-
-def untile_pair(block):
-    both = block.reshape(6, 96, 128).transpose(1, 0, 2).reshape(96, 768)
-    return both[:, :576], both[:, 576:]
 
 
 def shards_fast(
@@ -1435,26 +1717,39 @@
     down_second,
     cotangent,
 ):
-    rank = lax.axis_index("seq")
-    mixer_norm_gain, skip_gain, gain_second, attention_norm_gain, gain_fourth = (
-        gain[None] for gain in (mixer_norm_gain, skip_gain, gain_second, attention_norm_gain, gain_fourth)
-    )
-    ends = jnp.cumsum(doc_lengths[0]).astype(jnp.int32)
-    first = BLOCK * jnp.clip(rank - 1, 0, OWNERS - 1)
-    coef = lax.dynamic_slice_in_dim(mode_coef, first, BLOCK, 1)
-    rate = lax.dynamic_slice_in_dim(mode_rate, first, BLOCK, 1)
     tables, phase_cos, phase_sin = odd_tables()
-    home = (ROWS, WIDE)
+    home, thrice, tall = (ROWS, WIDE), (3, ROWS, WIDE), (ROWS, 4 * WIDE)
     span = (SPAN, BLOCK)
+    kept = dict(
+        query_a=(home, F32),
+        value_a=(home, F32),
+        key_ext=((192, WIDE), F32),
+        shifted=(home, F32),
+        response=(home, F32),
+        stream_b=(home, F32),
+        bend_b=(tall, BF),
+        qkv=((3, *span), BF),
+        lse=(span, F32),
+        attended_full=(span, F32),
+        kernel_re=(span, F32),
+        kernel_im=(span, F32),
+        signal_re=(span, F32),
+        signal_im=(span, F32),
+    )
+    lefts = dict(normed_a=(home, BF), gated=(home, BF), normed_b=(home, BF), active_b=(tall, BF), normed_c=(home, BF))
+    modes_scratch = dict(coef=((64, BLOCK), F32), rate=((64, BLOCK), F32))
+    packs = dict(pack_re=((SPAN, 256), BF), pack_im=((SPAN, 256), BF))
+    rims = dict(rim_out=((64, WIDE), BF), rim_in=((64, WIDE), BF))
+    table_scratch = dict(cos_table=((SPAN, SPAN), BF), sin_table=((SPAN, SPAN), BF))
     a = call(
         kernel_a,
-        1,
+        0,
         dict(
             tokens=tokens,
             mixer_norm_gain=mixer_norm_gain,
             shift_taps=shift_taps,
-            coef=coef,
-            rate=rate,
+            mode_coef=mode_coef,
+            mode_rate=mode_rate,
             skip_gain=skip_gain,
             gain_second=gain_second,
             attention_norm_gain=attention_norm_gain,
@@ -1462,212 +1757,164 @@
             phase_sin=phase_sin,
         ),
         dict(mixer_in=mixer_in, **tables, mixer_out=mixer_out, up_first=up_first, down_first=down_first, project_in=project_in),
-        dict(ends=ends),
+        dict(doc_lengths=doc_lengths),
+        dict(stream_c=(home, F32), attended=(home, BF)),
         dict(
-            normed_a=(home, BF),
-            query_a=(home, F32),
-            value_a=(home, F32),
-            key_ext=((192, WIDE), F32),
-            shifted=(home, F32),
-            response=(home, F32),
-            gated=(home, BF),
-            stream_b=(home, F32),
-            normed_b=(home, BF),
-            raised_b=((ROWS, 4 * WIDE), F32),
-            active_b=((ROWS, 4 * WIDE), BF),
-            stream_c=(home, F32),
-            normed_c=(home, BF),
-            attended=(home, BF),
-            qkv=((3, *span), BF),
-            lse=(span, F32),
-            attended_full=(span, F32),
-            kernel_re=(span, F32),
-            kernel_im=(span, F32),
-            signal_re=(span, F32),
-            signal_im=(span, F32),
+            **{name + "_kept": made for name, made in kept.items()},
+            **{name + "_all": ((4 * shape[0], shape[1]), kind) for name, (shape, kind) in lefts.items()},
         ),
         dict(
-            rim_out=((64, WIDE), BF),
-            rim_in=((64, WIDE), BF),
+            **kept,
+            **lefts,
+            **modes_scratch,
+            **packs,
+            **rims,
+            **table_scratch,
             product_low=(home, BF),
             signal=(span, BF),
             mode_rows=(span, F32),
             conv=(span, BF),
             conv_home=(home, BF),
-            pack_re=((SPAN, 256), BF),
-            pack_im=((SPAN, 256), BF),
-            mixed_c=((3, *home), BF),
+            mixed_c=(thrice, BF),
             attended_low=(span, BF),
+            mixer_in=((WIDE, 3 * WIDE), BF),
+            mixer_out=((WIDE, WIDE), BF),
+            up_first=((WIDE, 4 * WIDE), BF),
+            down_first=((4 * WIDE, WIDE), BF),
+            project_in=((WIDE, 3 * WIDE), BF),
         ),
-        29,
-        9,
-    )
+        (48, 32),
+    )
+    kinds = dict(sum_d=LAYER, sum_c=PAIR, sum_b=LAYER, sum_a=PAIR)
+    sum_outs, sums = {}, {}
+    for name, kind in kinds.items():
+        sum_outs[name + "_own"] = ((LENGTH[kind], 128), BF)
+        sum_outs[name + "_third"] = ((LENGTH[kind], 128), BF)
+        sums.update(sum_scratch(name, kind))
     b = call(
         kernel_b,
-        2,
+        1,
         dict(
+            tokens=tokens,
+            cotangent=cotangent,
             stream_c=a["stream_c"],
             attended=a["attended"],
+            mixer_norm_gain=mixer_norm_gain,
+            shift_taps=shift_taps,
+            mode_coef=mode_coef,
+            mode_rate=mode_rate,
+            skip_gain=skip_gain,
+            gain_second=gain_second,
+            attention_norm_gain=attention_norm_gain,
             gain_fourth=gain_fourth,
-            cotangent=cotangent,
-            qkv=a["qkv"],
-            lse=a["lse"],
-            attended_full=a["attended_full"],
         ),
-        dict(project_out=project_out, up_second=up_second, down_second=down_second),
-        dict(ends=ends),
+        dict(
+            project_out=project_out,
+            up_second=up_second,
+            down_second=down_second,
+            **{name: a[name + "_kept"] for name in kept},
+            **{name + "_all": a[name + "_all"] for name in lefts},
+            **tables,
+            project_in=project_in,
+            up_first=up_first,
+            down_first=down_first,
+            mixer_out=mixer_out,
+            mixer_in=mixer_in,
+        ),
+        dict(doc_lengths=doc_lengths),
         dict(
             block_out=((1, *home), BF),
-            normed_d=(home, BF),
-            active_d=((ROWS, 4 * WIDE), BF),
-            slope_d=((2, ROWS, 2 * WIDE), BF),
+            token_grad=((1, *home), F32),
+            mode_out=((128, 128), F32),
+            small_out=((24, 128), F32),
+        ),
+        sum_outs,
+        dict(
+            **{name: made for name, made in kept.items() if not name.startswith(("kernel", "signal"))},
+            **modes_scratch,
+            **packs,
+            **rims,
+            **table_scratch,
+            **sums,
+            up=((WIDE, 4 * WIDE), BF),
+            down=((4 * WIDE, WIDE), BF),
+            in_weight=((WIDE, 3 * WIDE), BF),
+            out_weight=((WIDE, WIDE), BF),
+            layer_left=((512, WIDE), BF),
+            layer_second=((512, 4 * WIDE), BF),
+            pair_one=((512, WIDE), BF),
+            pair_two=((512, WIDE), BF),
+            turned_one=((WIDE, 512), BF),
+            turned_two=((WIDE, 512), BF),
+            turned=((WIDE, ROWS), BF),
+            slopes=(thrice, BF),
+            pairs=((4, *home), BF),
+            total=(home, F32),
             grad_d=(home, F32),
             grad_d_low=(home, BF),
-            gain_four=((1, WIDE), F32),
-            mixed_grad_c=((3, *home), BF),
-        ),
-        dict(
-            total=(home, F32),
             att_grad_home=(home, BF),
             att_grad=(span, BF),
             query_grad=(span, F32),
             key_grad=(span, F32),
             value_grad=(span, F32),
             qkv_grad=((3, *span), BF),
-        ),
-        14,
-        3,
-    )
-    c = call(
-        kernel_c,
-        3,
-        dict(
-            stream_c=a["stream_c"],
-            stream_b=a["stream_b"],
-            mixed_grad_c=b["mixed_grad_c"],
-            attention_norm_gain=attention_norm_gain,
-            gain_second=gain_second,
-            grad_d=b["grad_d"],
-            raised_b=a["raised_b"],
-            response=a["response"],
-            query_a=a["query_a"],
-            shifted=a["shifted"],
-            value_a=a["value_a"],
-            kernel_re=a["kernel_re"],
-            kernel_im=a["kernel_im"],
-            signal_re=a["signal_re"],
-            signal_im=a["signal_im"],
-            phase_cos=phase_cos,
-            phase_sin=phase_sin,
-            coef=coef,
-            rate=rate,
-        ),
-        dict(project_in=project_in, up_first=up_first, down_first=down_first, mixer_out=mixer_out, **tables),
-        dict(),
-        dict(
-            gain_three=((1, WIDE), F32),
-            gain_two=((1, WIDE), F32),
-            skip_part=((1, WIDE), F32),
+            mixed_grad_c=(thrice, BF),
             grad_c_low=(home, BF),
-            slope_b=((2, ROWS, 2 * WIDE), BF),
             grad_b=(home, F32),
             grad_b_low=(home, BF),
-            query_grad_a=(home, BF),
+            mixed_grad_a=(thrice, BF),
             response_grad=(home, F32),
-            signal_grad_home=(home, BF),
-            coef_part=((64, BLOCK), F32),
-            rate_part=((64, BLOCK), F32),
-        ),
-        dict(
-            grad_c=(home, F32),
             response_grad_low=(home, BF),
             conv_grad=(span, BF),
             grad_re=(span, F32),
             grad_im=(span, F32),
             signal_grad=(span, BF),
-            kernel_grad=(span, F32),
-            pack_re=((SPAN, 256), BF),
-            pack_im=((SPAN, 256), BF),
+            signal_grad_home=(home, BF),
+            grad_ext=((192, WIDE), F32),
+            taps=((64, WIDE), F32),
+            small=((2, 2, 24, WIDE), F32),
+            small_c=((2, 24, WIDE), F32),
+            small_swap=((4, 24, WIDE), F32),
+            small_sum=((3, 24, WIDE), F32),
+            mode_part=((3, 128, 128), F32),
+            mode_swap=((2, 128, 128), F32),
+            mode_home=((128, WIDE), F32),
         ),
-        14,
-        8,
-    )
-    d = call(
-        kernel_d,
-        4,
-        dict(
-            tokens=tokens,
-            mixer_norm_gain=mixer_norm_gain,
-            shift_taps=shift_taps,
-            skip_gain=skip_gain,
-            signal_grad_home=c["signal_grad_home"],
-            response_grad=c["response_grad"],
-            value_a=a["value_a"],
-            shifted=a["shifted"],
-            key_ext=a["key_ext"],
-            query_grad_a=c["query_grad_a"],
-            grad_b=c["grad_b"],
-        ),
-        dict(mixer_in=mixer_in),
-        dict(),
-        dict(
-            mixed_grad_a=((3, *home), BF),
-            taps_part=((64, WIDE), F32),
-            gain_one=((1, WIDE), F32),
-            token_grad=((1, *home), F32),
-        ),
-        dict(
-            grad_ext=((192, WIDE), F32),
-            rim_out=((64, WIDE), BF),
-            rim_in=((64, WIDE), BF),
-            key_grad_a=(home, F32),
-        ),
-        1,
-        1,
-    )
-    mixed_grad_a = d["mixed_grad_a"].transpose(1, 0, 2).reshape(ROWS, 3 * WIDE)
-    mixed_grad_c = b["mixed_grad_c"].transpose(1, 0, 2).reshape(ROWS, 3 * WIDE)
-    groups = (
-        (b["normed_d"], b["slope_d"], cotangent[0], b["active_d"]),
-        (a["normed_c"], pair_columns(mixed_grad_c, b["grad_d_low"]), a["attended"]),
-        (a["normed_b"], c["slope_b"], c["grad_c_low"], a["active_b"]),
-        (a["normed_a"], pair_columns(mixed_grad_a, c["grad_b_low"]), a["gated"]),
-    )
-    layer_d, pair_c, layer_b, pair_a = weight_sums((LAYER, PAIR, LAYER, PAIR), groups, 0)
-    up_two, down_two = untile_layer(layer_d)
-    in_c, out_c = untile_pair(pair_c)
-    up_one, down_one = untile_layer(layer_b)
-    in_a, out_a = untile_pair(pair_a)
-    owner = is_owner(rank)
-    modes_part = jnp.concatenate([c["coef_part"], c["rate_part"]], axis=0)
-    modes_part = lax.dynamic_update_slice_in_dim(
-        jnp.zeros((128, WIDE), F32), jnp.where(owner, modes_part, 0.0), first, 1
-    )
-    small = jnp.concatenate(
-        [d["taps_part"], modes_part, d["gain_one"], c["skip_part"], c["gain_two"], c["gain_three"], b["gain_four"]], axis=0
-    )
-    small = lax.psum_scatter(small, "seq", scatter_dimension=1, tiled=True)
-    taps = lax.psum_scatter(small[0:64].astype(BF), "batch", scatter_dimension=0, tiled=True).astype(F32)
-    rest = lax.psum(small[64:], "batch")
-    return (
-        b["block_out"],
-        d["token_grad"],
-        rest[128],
-        in_a,
-        taps,
-        rest[0:64],
-        rest[64:128],
-        rest[129],
-        out_a,
-        rest[130],
-        up_one,
-        down_one,
-        rest[131],
-        in_c,
-        out_c,
-        rest[132],
-        up_two,
-        down_two,
+        (160, 64),
+    )
+    vmem = pl.BlockSpec(memory_space=pltpu.VMEM)
+    given = [b[name] for name in ("block_out", "token_grad", "mode_out", "small_out")]
+    for name in kinds:
+        given += [b[name + "_own"], b[name + "_third"]]
+    gain = ((96,), F32)
+    wide, narrow, up, down, mode = ((96, 576), F32), ((96, 192), F32), ((96, 768), F32), ((384, 192), F32), ((64, 96), F32)
+    shapes = (
+        ((1, *home), BF),
+        ((1, *home), F32),
+        gain,
+        wide,
+        ((16, 96), F32),
+        mode,
+        mode,
+        gain,
+        narrow,
+        gain,
+        up,
+        down,
+        gain,
+        wide,
+        narrow,
+        gain,
+        up,
+        down,
+    )
+    return tuple(
+        pl.pallas_call(
+            kernel_z,
+            out_shape=[jax.ShapeDtypeStruct(shape, kind) for shape, kind in shapes],
+            in_specs=[vmem] * len(given),
+            out_specs=[vmem] * len(shapes),
+        )(*given)
     )
 
 

time: 424 us -> 237 us (0.56); the launches traced: 416 us -> 237 us
  Pallas kernels: 340 us -> 232 us
  local copies, waits for them, and re-layouts: 29.5 us -> 3.72 us
  waiting for transfers between devices: 16 us -> 0 us
  between operations: 14.8 us -> 0.68 us
  blocking collectives: 12.5 us -> 0 us
    pallas_call x1, Pallas kernels: 173 us -> 3.48 us  [shards_fast(): pl.pallas_call(kernel_z, out_shape=[jax.ShapeDtypeStruct(shape, kind) for...]
    pallas_call x4 -> x2, Pallas kernels: 166 us -> 229 us  [call(): pl.pallas_call(run, out_shape=[jax.ShapeDtypeStruct(shape, kind) for shap...]
    reduce_scatter x1 -> x0, waiting for transfers between devices: 16 us -> none  [shards_fast(): lax.psum_scatter(small[0:64].astype(BF), 'batch', scatter_dimension=0, ti...]
    psum x1 -> x0, blocking collectives: 12.5 us -> none  [shards_fast(): rest = lax.psum(small[64:], 'batch')]
    unnamed x37 -> x0, local copies, waits for them, and re-layouts: 6.55 us -> none
    broadcast_in_dim x6 -> x0, local copies, waits for them, and re-layouts: 6.36 us -> none  [the longest x5 6.33 us: shards_fast(): gain[None]]
    slice x9 -> x0, local copies, waits for them, and re-layouts: 5.38 us -> none  [the longest x4 2.89 us: untile_pair(): return (both[:, :576], both[:, 576:])]
    reshape x8 -> x0, local copies, waits for them, and re-layouts: 4.99 us -> none  [the longest x2 2.82 us: pair_columns(): parts.reshape(128, 2, 2, 768).transpose(2, 0, 1, 3).reshape(2, 128, 1536)]
  transfers between devices with their start and end apart: 2 -> 0, of which waited for: 1 -> 0; matrix products, arithmetic and copies ran while one was open for 3% -> 0% of each run, Pallas kernels for 42% -> 0%
where the time goes in v3:
time: 237 us
  Pallas kernels  232 us (98%)
  local copies, waits for them, and re-layouts  3.72 us (2%)
    pallas_call x2, Pallas kernels, call(): pl.pallas_call(run, out_shape=[jax.ShapeDtypeStruct(shape, kind) for shap...  229 us

profile of v3, /device:TPU:0, one launch (start us, length us, event | category | flops | bytes accessed | tf_op | source)
XLA Modules:
  0.0 236.7 jit_solution(10417768240008080316)
XLA Ops:
  0.7 61.8 %shard_map.358 = (f32[128,768]{1,0:T(8,128)}, bf16[128,768]{1,0:T(8,128)(2,1)}, f32[128,768]{1,0:T(8,128)}, f32[128,768]{1,0:T(8,128)}, f32[192,768]{1,0:T(8,128...) custom-call(bf16[1,128,768]{2,1,0:T(8,128)(2,1)} %refs_0_.3, ...), custom_call_target="tpu_custom_call" | custom-call | tf_op jit(solution)/shard_map/pallas_call | solution.py:1667
  62.5 167.0 %shard_map.359 = (bf16[1,128,768]{2,1,0:T(8,128)(2,1)}, f32[1,128,768]{2,1,0:T(8,128)}, f32[128,128]{1,0:T(8,128)}, f32[24,128]{1,0:T(8,128)}, bf16[1152,128]{1,...) custom-call(bf16[1,128,768]{2,1,0:T(8,128)(2,1)} %refs_0_.3, ...), custom_call_target="tpu_custom_call" | custom-call | tf_op jit(solution)/shard_map/pallas_call | solution.py:1667
  229.5 3.5 %shard_map.360 = (bf16[1,128,768]{2,1,0:T(8,128)(2,1)}, f32[1,128,768]{2,1,0:T(8,128)}, f32[96]{0:T(128)}, f32[96,576]{1,0:T(8,128)}, f32[16,96]{1,0:T(8,128)}, ...) custom-call(bf16[1,128,768]{2,1,0:T(8,128)(2,1)} %get-tuple-element., ...), custom_call_target="tpu_custom_call" | custom-call | tf_op jit(solution)/shard_map/pallas_call | solution.py:1912
  233.0 1.9 copy.41
  234.8 1.9 copy.42

commit v4 on v3

--- a/solution.py
+++ b/solution.py
@@ -588,6 +588,9 @@
     return pl.ds(pl.multiple_of(BLOCK * block, BLOCK), BLOCK)
 
 
+PARTNERS = ((1, 1, 1), (1, 1, 0), (1, 0, 1), (1, 0, 0), (0, 1, 1), (0, 1, 0), (0, 0, 1))
+
+
 class Spread:
     def __init__(self, net, source, target, outward, only=None):
         self.net, self.source, self.target, self.outward = net, source, target, outward
@@ -607,7 +610,7 @@
     def each_send(self, act, chosen=None):
         me = self.net.s
         for step in range(1, RANKS):
-            rank = lax.rem(me + step, RANKS)
+            rank = self.net.partner(step)
             go = is_owner(rank) if self.outward else is_owner(me)
             if chosen is not None:
                 go = jnp.logical_and(go, chosen(rank))
@@ -635,7 +638,7 @@
     def wait_recv(self):
         me = self.net.s
         for step in range(1, RANKS):
-            rank = lax.rem(me + RANKS - step, RANKS)
+            rank = self.net.partner(step)
 
             @pl.when(is_owner(me) if self.outward else is_owner(rank))
             def _(step=step, rank=rank):
@@ -662,6 +665,12 @@
         self.by_high = (2 * (2 * flip(self.high) + self.low) + self.x, self.b)
         self.used = 0
         self.waiting = []
+
+    def partner(self, step):
+        far, near, side = PARTNERS[step - 1]
+        high = flip(self.high) if far else self.high
+        low = flip(self.low) if near else self.low
+        return 4 * high + 2 * low + (flip(self.x) if side else self.x)
 
     def take(self, count):
         at = self.used
@@ -997,6 +1006,7 @@
 
 
 LAYER, PAIR = (0, 1)
+QUARTERS = 2
 LENGTH = (1152, 576)
 
 
@@ -1007,7 +1017,7 @@
             setattr(self, part, getattr(r, name + "_" + part))
         if kind == LAYER:
             self.across = getattr(r, name + "_across")
-        self.half = LENGTH[kind] // 2
+        self.half = QUARTERS * LENGTH[kind] // 4
         self.shared = []
 
     def give(self, kept, step, columns, other):
@@ -1134,14 +1144,14 @@
 
 def sum_scratch(name, kind):
     length = LENGTH[kind]
-    half = length // 2
+    half = QUARTERS * length // 4
     made = {
         name + "_right": ((512, WIDE), BF),
         name + "_grads": ((2, 2, 2, length, 128), BF),
         name + "_near_a": ((2, 2, half, 128), BF),
-        name + "_near_b": ((2, 2, half, 128), BF),
+        name + "_near_b": ((2, 2, length - half, 128), BF),
         name + "_next_a": ((2, half, 128), BF),
-        name + "_next_b": ((2, half, 128), BF),
+        name + "_next_b": ((2, length - half, 128), BF),
     }
     if kind == LAYER:
         made[name + "_across"] = ((192, 512), BF)
@@ -1186,6 +1196,7 @@
 
 TABLES = ("cos_table", "sin_table")
 KEPT = (
+    "value_next",
     "qkv",
     "lse",
     "attended_full",
@@ -1209,8 +1220,15 @@
     near = Locals(r.local_sem)
     net.hello()
     wait = {}
-    for name in ("mixer_in",) + TABLES + ("mixer_out", "up_first", "down_first", "project_in"):
-        wait[name] = near.start(getattr(r, name + "_hbm"), getattr(r, name))
+
+    def fetch(*names):
+        for name in names:
+            wait[name] = near.start(getattr(r, name + "_hbm"), getattr(r, name))
+
+    thirds = []
+    for index in (2, 0, 1):
+        lanes = slice(WIDE * index, WIDE * index + WIDE)
+        thirds.append(near.start(r.mixer_in_hbm.at[:, lanes], r.mixer_in.at[:, lanes]))
     r.ends[0] = r.doc_lengths[0, 0]
     r.ends[1] = r.ends[0] + r.doc_lengths[0, 1]
     r.ends[2] = r.ends[1] + r.doc_lengths[0, 2]
@@ -1228,26 +1246,40 @@
         gathers.append(Gather(net, mine, lambda y, c: all_of.at[rows_of(2 * y + c), :]))
 
     me = net.s
-    stream = r.tokens[0].astype(F32)
-    normal, _ = pieces(stream)
-    r.normed_a[...] = (normal * r.mixer_norm_gain[...][None]).astype(BF)
-    wait["mixer_in"].wait()
-    r.key_ext[64:192, :] = mm(r.normed_a[...], r.mixer_in[:, WIDE : 2 * WIDE])
-    r.rim_out[...] = r.key_ext[128:192, :].astype(BF)
+    gain_a = r.mixer_norm_gain[...][None]
     net.ready()
-    rim = Beside(net, r.rim_out, r.rim_in, 1)
+    rim = Beside(net, r.tokens.at[0, 64:128, :], r.rim_in, 1)
     rim.start()
-    gather("normed_a")
 
     @pl.when(me == 0)
     def _():
         r.rim_in[...] = jnp.zeros_like(r.rim_in)
 
+    normal, _ = pieces(r.tokens[0].astype(F32))
+    r.normed_a[...] = (normal * gain_a).astype(BF)
+    gather("normed_a")
+    thirds[0].wait()
+    r.value_a[...] = mm(r.normed_a[...], r.mixer_in[:, 2 * WIDE :])
+    r.value_low[...] = r.value_a[0:64, :].astype(BF)
+    later = Beside(net, r.value_low, r.value_next, -1)
+    later.start()
+
+    @pl.when(me == RANKS - 1)
+    def _():
+        r.value_next[...] = jnp.zeros_like(r.value_next)
+
+    thirds[1].wait()
     r.query_a[...] = mm(r.normed_a[...], r.mixer_in[:, 0:WIDE])
-    r.value_a[...] = mm(r.normed_a[...], r.mixer_in[:, 2 * WIDE :])
     keep("query_a", "value_a")
+    thirds[2].wait()
+    fetch("shift_taps", "mode_coef", "mode_rate", *TABLES, "phase_cos", "phase_sin", "mixer_out")
+    fetch("up_first", "down_first", "project_in")
+    r.key_ext[64:192, :] = mm(r.normed_a[...], r.mixer_in[:, WIDE : 2 * WIDE])
     rim.wait_recv()
-    r.key_ext[0:64, :] = r.rim_in[...].astype(F32)
+    normal, _ = pieces(r.rim_in[...].astype(F32))
+    r.key_ext[0:64, :] = mm((normal * gain_a).astype(BF), r.mixer_in[:, WIDE : 2 * WIDE])
+    for name in ("shift_taps", "mode_coef", "mode_rate"):
+        wait[name].wait()
     shift_forward(r.key_ext, r.shift_taps, None, r.shifted)
     r.product_low[...] = (r.shifted[...] * r.value_a[...]).astype(BF)
     go = net.spread(lambda block: r.product_low.at[:, lanes_of(block)], lambda rank: r.signal.at[rows_of(rank), :], True)
@@ -1258,7 +1290,7 @@
     r.coef[...] = r.mode_coef[:, block]
     r.rate[...] = r.mode_rate[:, block]
     modes(r.coef, r.rate, r.mode_rows)
-    for name in TABLES:
+    for name in TABLES + ("phase_cos", "phase_sin"):
         wait[name].wait()
     transform_two(r, r.mode_rows[...], r.kernel_re, r.kernel_im)
     turned = r.kernel_re[...] * r.phase_cos[...] - r.kernel_im[...] * r.phase_sin[...]
@@ -1276,10 +1308,6 @@
     back = net.spread(lambda rank: r.conv.at[rows_of(rank), :], lambda block: r.conv_home.at[:, lanes_of(block)], False)
     back.start()
     back.own()
-    turned = r.signal_re[...] * r.phase_cos[...] - r.signal_im[...] * r.phase_sin[...]
-    r.signal_im[...] = -(r.signal_im[...] * r.phase_cos[...] + r.signal_re[...] * r.phase_sin[...])
-    r.signal_re[...] = turned
-    keep("signal_re", "signal_im")
     for name in ("mixer_out", "up_first", "down_first", "project_in"):
         wait[name].wait()
     back.wait_recv()
@@ -1311,6 +1339,12 @@
     gather("normed_c")
     for made in gathers[:3]:
         made.forward()
+    turned = r.signal_re[...] * r.phase_cos[...] - r.signal_im[...] * r.phase_sin[...]
+    r.signal_im[...] = -(r.signal_im[...] * r.phase_cos[...] + r.signal_re[...] * r.phase_sin[...])
+    r.signal_re[...] = turned
+    keep("signal_re", "signal_im")
+    later.wait_recv()
+    keep("value_next")
     go.wait_recv()
     keep("qkv")
     back = net.spread(lambda rank: r.attended_low.at[rows_of(rank), :], lambda block: r.attended.at[:, lanes_of(block)], False)
@@ -1337,14 +1371,16 @@
     def fetch(name, into=None):
         wait[name] = near.start(getattr(r, name + "_hbm"), getattr(r, into or name))
 
-    for name, into in (("project_out", "out_weight"), ("up_second", "up"), ("down_second", "down")):
-        fetch(name, into)
-    for name in KEPT[:10]:
-        fetch(name)
-    fetch("project_in", "in_weight")
-    fetch("normed_c_all", "pair_one")
-    for name in TABLES:
-        fetch(name)
+    fetch("project_out", "out_weight")
+    chunks = []
+    for step, (index, other) in enumerate(net.order()):
+        lanes = pl.ds(pl.multiple_of(WIDE * index, WIDE), WIDE)
+        chunks.append(
+            (
+                near.start(r.up_second_hbm.at[:, lanes], r.up.at[:, lanes]),
+                near.start(r.down_second_hbm.at[lanes, :], r.down.at[lanes, :]),
+            )
+        )
     r.ends[0] = r.doc_lengths[0, 0]
     r.ends[1] = r.ends[0] + r.doc_lengths[0, 1]
     r.ends[2] = r.ends[1] + r.doc_lengths[0, 2]
@@ -1362,14 +1398,20 @@
     r.turned[...] = r.cotangent[0].T
     r.pair_two[own_rows, :] = r.attended[...]
     net.ready()
-    gather_att = Gather(net, r.pair_two.at[own_rows, :], lambda y, c: r.pair_two.at[rows_of(2 * y + c), :])
     gather_d = Gather(net, r.layer_left.at[own_rows, :], lambda y, c: r.layer_left.at[rows_of(2 * y + c), :])
     sum_d.share_rows(r.turned)
-    wait["up_second"].wait()
-    wait["down_second"].wait()
     gathers = []
     for step, (index, other) in enumerate(net.order()):
         lanes = pl.ds(pl.multiple_of(WIDE * index, WIDE), WIDE)
+        for copy in chunks[step]:
+            copy.wait()
+        if step == 3:
+            for name in KEPT[:11]:
+                fetch(name)
+            fetch("project_in", "in_weight")
+            fetch("normed_c_all", "pair_one")
+            for name in ("shift_taps", "mode_coef", "mode_rate") + TABLES:
+                fetch(name)
         raised = mm(r.layer_left[own_rows, :], r.up[:, lanes])
         active, slope = gelu_parts(raised)
         active = active.astype(BF)
@@ -1396,6 +1438,7 @@
     go = net.spread(lambda block: r.att_grad_home.at[:, lanes_of(block)], lambda rank: r.att_grad.at[rows_of(rank), :], True)
     go.start()
     go.own()
+    gather_att = Gather(net, r.pair_two.at[own_rows, :], lambda y, c: r.pair_two.at[rows_of(2 * y + c), :])
     fetch("up_first", "up")
     fetch("down_first", "down")
     fetch("mixer_out", "out_weight")
@@ -1403,10 +1446,6 @@
 
     r.key_grad[...] = jnp.zeros_like(r.key_grad)
     r.value_grad[...] = jnp.zeros_like(r.value_grad)
-    gather_att.forward()
-    gather_d.forward()
-    gathers[0].forward()
-    gathers[1].forward()
     for name in ("qkv", "lse", "attended_full"):
         wait[name].wait()
     go.wait_recv()
@@ -1424,8 +1463,8 @@
         ("signal_im", "key_grad"),
     ):
         fetch(name, into)
-    gathers[2].forward()
-    gathers[3].forward()
+    for made in [gather_d] + gathers:
+        made.forward()
     gather_d.wait()
     turn(r.layer_left, r.turned_one)
     for made in gathers:
@@ -1443,6 +1482,8 @@
     for index in range(1, 3):
         grad = grad + mm_nt(r.mixed_grad_c[index], r.in_weight[:, WIDE * index : WIDE * index + WIDE])
     fetch("mixer_in", "in_weight")
+    pair_columns(r.mixed_grad_c, r.grad_d_low, r.pairs)
+    sum_c.share_pairs(r.pairs)
     grad, gain_three = pieces_back(grad, normal, inverse_c, r.attention_norm_gain[...][None])
     grad = grad + r.grad_d[...]
     r.total[...] = grad
@@ -1480,9 +1521,16 @@
     )
     go.start()
     go.own()
+    after = Beside(net, r.response_grad_low.at[0:64, :], r.response_next, -1)
+    after.start()
+
+    @pl.when(net.s == RANKS - 1)
+    def _():
+        r.response_next[...] = jnp.zeros_like(r.response_next)
+
     skip_part = jnp.sum(response_grad * (r.shifted[...] * r.value_a[...]), axis=0, keepdims=True)
-    pair_columns(r.mixed_grad_c, r.grad_d_low, r.pairs)
-    sum_c.share_pairs(r.pairs)
+    sum_d.second()
+    gather_att.forward()
     wait["normed_c_all"].wait()
     turn(r.pair_one, r.turned_one)
     gather_att.wait()
@@ -1490,11 +1538,15 @@
     gather_att.free()
     fetch("normed_a_all", "pair_one")
     fetch("gated_all", "pair_two")
+    sum_c.product(r.turned_one, r.turned_two)
+    wait["normed_b_all"].wait()
+    turn(r.layer_left, r.turned_one)
 
     for name in TABLES + ("kernel_re", "kernel_im", "signal_re", "signal_im"):
         wait[name].wait()
     kernel_re, kernel_im, signal_re, signal_im = r.lse, r.attended_full, r.query_grad, r.key_grad
     go.wait_recv()
+    r.signal_grad[SPAN:, :] = jnp.zeros((64, BLOCK), BF)
     transform(r, r.conv_grad[...], r.grad_re, r.grad_im)
     inverse(
         r,
@@ -1503,31 +1555,27 @@
         r.signal_grad,
     )
     back = net.spread(
-        lambda rank: r.signal_grad.at[rows_of(rank), :], lambda block: r.signal_grad_home.at[:, lanes_of(block)], False
+        lambda rank: r.signal_grad.at[pl.ds(pl.multiple_of(ROWS * rank, ROWS), 192), :],
+        lambda block: r.signal_grad_home.at[:, lanes_of(block)],
+        False,
     )
     back.start()
     back.own()
-    sum_d.second()
-    sum_c.product(r.turned_one, r.turned_two)
-    back.wait_recv()
-
-    signal_grad = r.signal_grad_home[...].astype(F32) + r.skip_gain[...][None] * r.response_grad[...]
-    r.grad_ext[0:ROWS, :] = signal_grad * r.value_a[...]
-    r.rim_out[...] = r.grad_ext[0:64, :].astype(BF)
-    rim = Beside(net, r.rim_out, r.rim_in, -1)
-    rim.start()
-    r.mixed_grad_a[2] = (signal_grad * r.shifted[...]).astype(BF)
-
-    @pl.when(net.s == RANKS - 1)
-    def _():
-        r.rim_in[...] = jnp.zeros_like(r.rim_in)
-
-    wait["normed_b_all"].wait()
-    turn(r.layer_left, r.turned_one)
     wait["active_b_all"].wait()
     sum_b.product(r.turned_one, r.layer_second)
-    rim.wait_recv()
-    r.grad_ext[ROWS:192, :] = r.rim_in[...].astype(F32)
+    sum_d.last()
+    sum_c.second()
+    after.wait_recv()
+    for name in ("shift_taps", "mode_coef", "mode_rate", "value_next"):
+        wait[name].wait()
+    back.wait_recv()
+
+    skip = r.skip_gain[...][None]
+    signal_grad = r.signal_grad_home[0:ROWS, :].astype(F32) + skip * r.response_grad[...]
+    r.grad_ext[0:ROWS, :] = signal_grad * r.value_a[...]
+    r.mixed_grad_a[2] = (signal_grad * r.shifted[...]).astype(BF)
+    signal_grad = r.signal_grad_home[ROWS:192, :].astype(F32) + skip * r.response_next[...].astype(F32)
+    r.grad_ext[ROWS:192, :] = signal_grad * r.value_next[...].astype(F32)
     shift_back(r.grad_ext, r.key_ext, r.shift_taps, r.total, r.taps)
     r.mixed_grad_a[1] = r.total[...].astype(BF)
     sum_c.free_columns()
@@ -1546,37 +1594,31 @@
         r.small[block // 2, block % 2, 0:16, :] = r.taps[16 * block : 16 * block + 16, :]
         r.small[block // 2, block % 2, 16:24, :] = gains
     swap = net.send(r.small.at[:, flip(net.c)], r.small_c, net.sibling)
-    wait["normed_a_all"].wait()
-    turn(r.pair_one, r.turned_one)
-    wait["gated_all"].wait()
-    turn(r.pair_two, r.turned_two)
-    sum_a.product(r.turned_one, r.turned_two)
-    swap.wait_recv()
-    r.small[:, net.c] += r.small_c[...]
-    swap = net.send(r.small.at[flip(net.y), net.c], r.small_swap.at[0], net.by_y)
-    sum_d.last()
-    sum_c.second()
-    swap.wait_recv()
-    r.small_sum[0] = r.small[net.y, net.c] + r.small_swap[0]
-    swap = net.send(r.small_sum.at[0], r.small_swap.at[1], net.by_x)
-
     re = r.grad_re[...] * signal_re[...] - r.grad_im[...] * signal_im[...]
     im = r.grad_re[...] * signal_im[...] + r.grad_im[...] * signal_re[...]
     inverse(r, re, im, r.value_grad)
     block = lanes_of(jnp.clip(net.s - 1, 0, OWNERS - 1))
     r.coef[...] = r.mode_coef[:, block]
     r.rate[...] = r.mode_rate[:, block]
+    wait["normed_a_all"].wait()
+    turn(r.pair_one, r.turned_one)
+    wait["gated_all"].wait()
+    turn(r.pair_two, r.turned_two)
+    sum_b.second()
+    swap.wait_recv()
+    r.small[:, net.c] += r.small_c[...]
+    swap = net.send(r.small.at[flip(net.y), net.c], r.small_swap.at[0], net.by_y)
+    sum_c.last()
+    sum_a.product(r.turned_one, r.turned_two)
     modes_back(r.coef, r.rate, r.value_grad, r.mode_part.at[0, 0:64], r.mode_part.at[0, 64:128])
     mode = net.send(r.mode_part.at[0], r.mode_swap.at[0], net.sibling)
-    sum_b.second()
+    swap.wait_recv()
+    r.small_sum[0] = r.small[net.y, net.c] + r.small_swap[0]
+    swap = net.send(r.small_sum.at[0], r.small_swap.at[1], net.by_x)
+    sum_b.last()
     mode.wait_recv()
     r.mode_part[1] = r.mode_part[0] + r.mode_swap[0]
     mode = net.send(r.mode_part.at[1], r.mode_swap.at[1], net.by_y)
-    swap.wait_recv()
-    r.small_sum[1] = r.small_sum[0] + r.small_swap[1]
-    swap = net.send(r.small_sum.at[1], r.small_swap.at[2], net.by_low)
-    sum_d.end(near)
-    sum_c.last()
     sum_a.second()
     mode.wait_recv()
     r.mode_part[2] = r.mode_part[1] + r.mode_swap[1]
@@ -1584,10 +1626,13 @@
     back.start()
     back.own()
     swap.wait_recv()
+    r.small_sum[1] = r.small_sum[0] + r.small_swap[1]
+    swap = net.send(r.small_sum.at[1], r.small_swap.at[2], net.by_low)
+    sum_a.last()
+    swap.wait_recv()
     r.small_sum[2] = r.small_sum[1] + r.small_swap[2]
     swap = net.send(r.small_sum.at[2], r.small_swap.at[3], net.by_high)
-    sum_b.last()
-    sum_a.last()
+    sum_d.end(near)
     sum_c.end(near)
     turn_back = lax.rem(WIDE - 96 * net.s, WIDE)
     back.wait_recv()
@@ -1639,7 +1684,7 @@
         for tile in range(6):
             up[:, 128 * tile : 128 * tile + 128] = block(index, 96 * tile, 96)
         for tile in range(3):
-            down[128 * tile : 128 * tile + 128, :] = block(index, 576 + 192 * tile, 192).T
+            down[:, 128 * tile : 128 * tile + 128] = block(index, 576 + 192 * tile, 192)
     for index, wide, narrow in ((1, project_in, project_out), (3, mixer_in, mixer_out)):
         for tile in range(4):
             wide[:, 128 * tile : 128 * tile + 128] = block(index, 96 * tile, 96)
@@ -1721,6 +1766,7 @@
     home, thrice, tall = (ROWS, WIDE), (3, ROWS, WIDE), (ROWS, 4 * WIDE)
     span = (SPAN, BLOCK)
     kept = dict(
+        value_next=((64, WIDE), BF),
         query_a=(home, F32),
         value_a=(home, F32),
         key_ext=((192, WIDE), F32),
@@ -1737,9 +1783,14 @@
         signal_im=(span, F32),
     )
     lefts = dict(normed_a=(home, BF), gated=(home, BF), normed_b=(home, BF), active_b=(tall, BF), normed_c=(home, BF))
-    modes_scratch = dict(coef=((64, BLOCK), F32), rate=((64, BLOCK), F32))
+    modes_scratch = dict(
+        coef=((64, BLOCK), F32),
+        rate=((64, BLOCK), F32),
+        shift_taps=((64, WIDE), F32),
+        mode_coef=((64, WIDE), F32),
+        mode_rate=((64, WIDE), F32),
+    )
     packs = dict(pack_re=((SPAN, 256), BF), pack_im=((SPAN, 256), BF))
-    rims = dict(rim_out=((64, WIDE), BF), rim_in=((64, WIDE), BF))
     table_scratch = dict(cos_table=((SPAN, SPAN), BF), sin_table=((SPAN, SPAN), BF))
     a = call(
         kernel_a,
@@ -1747,16 +1798,23 @@
         dict(
             tokens=tokens,
             mixer_norm_gain=mixer_norm_gain,
+            skip_gain=skip_gain,
+            gain_second=gain_second,
+            attention_norm_gain=attention_norm_gain,
+        ),
+        dict(
+            mixer_in=mixer_in,
             shift_taps=shift_taps,
             mode_coef=mode_coef,
             mode_rate=mode_rate,
-            skip_gain=skip_gain,
-            gain_second=gain_second,
-            attention_norm_gain=attention_norm_gain,
+            **tables,
             phase_cos=phase_cos,
             phase_sin=phase_sin,
+            mixer_out=mixer_out,
+            up_first=up_first,
+            down_first=down_first,
+            project_in=project_in,
         ),
-        dict(mixer_in=mixer_in, **tables, mixer_out=mixer_out, up_first=up_first, down_first=down_first, project_in=project_in),
         dict(doc_lengths=doc_lengths),
         dict(stream_c=(home, F32), attended=(home, BF)),
         dict(
@@ -1768,8 +1826,11 @@
             **lefts,
             **modes_scratch,
             **packs,
-            **rims,
+            rim_in=((64, WIDE), BF),
             **table_scratch,
+            phase_cos=(span, F32),
+            phase_sin=(span, F32),
+            value_low=((64, WIDE), BF),
             product_low=(home, BF),
             signal=(span, BF),
             mode_rows=(span, F32),
@@ -1783,7 +1844,7 @@
             down_first=((4 * WIDE, WIDE), BF),
             project_in=((WIDE, 3 * WIDE), BF),
         ),
-        (48, 32),
+        (48, 40),
     )
     kinds = dict(sum_d=LAYER, sum_c=PAIR, sum_b=LAYER, sum_a=PAIR)
     sum_outs, sums = {}, {}
@@ -1800,9 +1861,6 @@
             stream_c=a["stream_c"],
             attended=a["attended"],
             mixer_norm_gain=mixer_norm_gain,
-            shift_taps=shift_taps,
-            mode_coef=mode_coef,
-            mode_rate=mode_rate,
             skip_gain=skip_gain,
             gain_second=gain_second,
             attention_norm_gain=attention_norm_gain,
@@ -1815,6 +1873,9 @@
             **{name: a[name + "_kept"] for name in kept},
             **{name + "_all": a[name + "_all"] for name in lefts},
             **tables,
+            shift_taps=shift_taps,
+            mode_coef=mode_coef,
+            mode_rate=mode_rate,
             project_in=project_in,
             up_first=up_first,
             down_first=down_first,
@@ -1833,7 +1894,6 @@
             **{name: made for name, made in kept.items() if not name.startswith(("kernel", "signal"))},
             **modes_scratch,
             **packs,
-            **rims,
             **table_scratch,
             **sums,
             up=((WIDE, 4 * WIDE), BF),
@@ -1868,8 +1928,9 @@
             conv_grad=(span, BF),
             grad_re=(span, F32),
             grad_im=(span, F32),
-            signal_grad=(span, BF),
-            signal_grad_home=(home, BF),
+            signal_grad=((SPAN + 64, BLOCK), BF),
+            signal_grad_home=((192, WIDE), BF),
+            response_next=((64, WIDE), BF),
             grad_ext=((192, WIDE), F32),
             taps=((64, WIDE), F32),
             small=((2, 2, 24, WIDE), F32),
@@ -1887,7 +1948,7 @@
     for name in kinds:
         given += [b[name + "_own"], b[name + "_third"]]
     gain = ((96,), F32)
-    wide, narrow, up, down, mode = ((96, 576), F32), ((96, 192), F32), ((96, 768), F32), ((384, 192), F32), ((64, 96), F32)
+    wide, narrow, up, down, mode = ((96, 576), F32), ((96, 192), F32), ((96, 768), F32), ((192, 384), F32), ((64, 96), F32)
     shapes = (
         ((1, *home), BF),
         ((1, *home), F32),
@@ -1908,14 +1969,13 @@
         up,
         down,
     )
-    return tuple(
-        pl.pallas_call(
-            kernel_z,
-            out_shape=[jax.ShapeDtypeStruct(shape, kind) for shape, kind in shapes],
-            in_specs=[vmem] * len(given),
-            out_specs=[vmem] * len(shapes),
-        )(*given)
-    )
+    results = pl.pallas_call(
+        kernel_z,
+        out_shape=[jax.ShapeDtypeStruct(shape, kind) for shape, kind in shapes],
+        in_specs=[vmem] * len(given),
+        out_specs=[vmem] * len(shapes),
+    )(*given)
+    return tuple(result.T if result.shape == (192, 384) else result for result in results)
 
 
 def solution(mesh):

time: 237 us -> 223 us (0.941)
  Pallas kernels: 232 us -> 222 us
  local copies, waits for them, and re-layouts: 3.72 us -> 0 us
    pallas_call x2, Pallas kernels: 229 us -> 218 us  [call(): pl.pallas_call(run, out_shape=[jax.ShapeDtypeStruct(shape, kind) for shap...]
    pallas_call x2 -> x0, local copies, waits for them, and re-layouts: 3.72 us -> none  [shards_fast(): pl.pallas_call(kernel_z, out_shape=[jax.ShapeDtypeStruct(shape, kind) for...]
where the time goes in v4:
time: 223 us; the launch traced here: 222 us
  Pallas kernels  222 us (100%)
    pallas_call x2, Pallas kernels, call(): pl.pallas_call(run, out_shape=[jax.ShapeDtypeStruct(shape, kind) for shap...  218 us

profile of v4, /device:TPU:0, one launch (start us, length us, event | category | flops | bytes accessed | tf_op | source)
XLA Modules:
  0.0 222.5 jit_solution(14676169306825480519)
XLA Ops:
  0.7 63.5 %shard_map.358 = (f32[128,768]{1,0:T(8,128)}, bf16[128,768]{1,0:T(8,128)(2,1)}, bf16[64,768]{1,0:T(8,128)(2,1)}, f32[128,768]{1,0:T(8,128)}, f32[128,768]{1,0:T(...) custom-call(bf16[1,128,768]{2,1,0:T(8,128)(2,1)} %refs_0_.3, ...), custom_call_target="tpu_custom_call" | custom-call | tf_op jit(solution)/shard_map/pallas_call | solution.py:1712
  64.2 154.9 %shard_map.359 = (bf16[1,128,768]{2,1,0:T(8,128)(2,1)}, f32[1,128,768]{2,1,0:T(8,128)}, f32[128,128]{1,0:T(8,128)}, f32[24,128]{1,0:T(8,128)}, bf16[1152,128]{1,...) custom-call(bf16[1,128,768]{2,1,0:T(8,128)(2,1)} %refs_0_.3, ...), custom_call_target="tpu_custom_call" | custom-call | tf_op jit(solution)/shard_map/pallas_call | solution.py:1712
  219.1 3.2 %shard_map.360 = (bf16[1,128,768]{2,1,0:T(8,128)(2,1)}, f32[1,128,768]{2,1,0:T(8,128)}, f32[96]{0:T(128)}, f32[96,576]{1,0:T(8,128)}, f32[16,96]{1,0:T(8,128)}, ...) custom-call(bf16[1,128,768]{2,1,0:T(8,128)(2,1)} %get-tuple-element., ...), custom_call_target="tpu_custom_call" | custom-call | tf_op jit(solution)/shard_map/pallas_call | solution.py:1972
